TPU v7x, 32 devices: a whole 2x2x4 slice. The times are simulated.
32 devices in a mesh: dp: 32 (over z, y, x, core).
Axes of the slice: x: 2, y: 2, z: 4, core: 2. Of those that a mesh axis runs over, the one named last changes fastest.
Arguments:
- tokens: bfloat16 [24576, 256], P('dp'), may hold values from -6 to 6
- lengths: int32 [192], P('dp'), may hold values from 1 to 128, as said below
- w_qkv: bfloat16 [256, 768], P('dp'), may hold values from -0.375 to 0.375
- w_attn: bfloat16 [256, 256], P('dp'), may hold values from -0.75 to 0.75
- w_in: bfloat16 [256, 768], P('dp'), may hold values from -0.375 to 0.375
- w_mlp: bfloat16 [384, 256], P(None, 'dp'), may hold values from -0.3125 to 0.3125
- gain_attn: bfloat16 [256], P('dp'), may hold values from 0.5 to 1.5
- gain_mlp: bfloat16 [256], P('dp'), may hold values from 0.5 to 1.5
- cotangent: bfloat16 [24576, 256], P('dp'), may hold values from -6 to 6
Outputs:
- block_out: bfloat16 [24576, 256], P('dp')
- grad_tokens: float32 [24576, 256], P('dp')
- grad_qkv: float32 [256, 768], P('dp')
- grad_attn: float32 [256, 256], P('dp')
- grad_in: float32 [256, 768], P('dp')
- grad_mlp: float32 [384, 256], P(None, 'dp')
- grad_gain_attn: float32 [256], P('dp')
- grad_gain_mlp: float32 [256], P('dp')
Inputs may be any that keep to these rules, and one draw needn't show every extreme that they name: `lengths`: entry i is the block of rows i * 128 to (i + 1) * 128 - 1; device d holds entries d * 3 * 2 onward, micro-batch m of it the 2 entries from m * 2.
All inputs are finite; a program needn't handle non-finite values.
Results may differ from a plain program's by a relative error of at most 0.011.
Values may be sent and summed in bfloat16 or wider, within the bound.
No kernel may reach another device: no remote copies, remote signals or barrier semaphores. Data moves between devices by JAX's collectives and lax.ppermute only.
A program may use at most 64 MiB of HBM per device.

v0:
```python
import jax
import jax.numpy as jnp
from jax import lax
from jax.sharding import PartitionSpec as P

D = 256
FF = 384
HEADS = 4
HEAD_DIM = 64
BLOCK = 128
MICRO = 3
BLOCKS = 2


rope_base = 160000.0
eps_norm = 1e-05


def tables():
    half_dim = HEAD_DIM // 2
    frequency = rope_base ** (-(jnp.arange(half_dim, dtype=jnp.float32) * 2.0) / HEAD_DIM)
    angles = jnp.arange(BLOCK, dtype=jnp.float32)[:, None] * frequency[None, :]
    angles = jnp.concatenate([angles, angles], axis=1)
    return (jnp.cos(angles), jnp.sin(angles))


def rotate(values, cos_table, sine_table):
    half_dim = HEAD_DIM // 2
    turned = jnp.concatenate([-values[..., half_dim:], values[..., :half_dim]], axis=-1)
    return values * cos_table[None, :, None, :] + turned * sine_table[None, :, None, :]


def unrotate(values, cos_table, sine_table):
    half_dim = HEAD_DIM // 2
    scaled = values * sine_table[None, :, None, :]
    turned = jnp.concatenate([scaled[..., half_dim:], -scaled[..., :half_dim]], axis=-1)
    return values * cos_table[None, :, None, :] + turned


def standardize(values):
    centre = values - jnp.mean(values, axis=-1, keepdims=True)
    inverse = lax.rsqrt(jnp.mean(centre * centre, axis=-1, keepdims=True) + eps_norm)
    return (centre * inverse, inverse)


def norm_back(d_hat, hat_rows, inverse):
    mean_one = jnp.mean(d_hat, axis=-1, keepdims=True)
    mean_two = jnp.mean(d_hat * hat_rows, axis=-1, keepdims=True)
    return inverse * (d_hat - mean_one - hat_rows * mean_two)


def times_t(left, right):
    return lax.dot_general(
        left, right, (((1,), (1,)), ((), ())), preferred_element_type=jnp.float32
    )


def outer_sum(left, right):
    return lax.dot_general(
        left, right, (((0,), (0,)), ((), ())), preferred_element_type=jnp.float32
    )


def gelu_slope(values):
    normal_cdf = 0.5 * (1.0 + lax.erf(values * 0.7071067811865476))
    return normal_cdf + values * jnp.exp(-0.5 * values * values) * 0.3989422804014327


def attention_scores(queries, key_rows, live_key):
    scores = jnp.einsum("bqhd,bkhd->bhqk", queries, key_rows, preferred_element_type=jnp.float32)
    scores = scores * HEAD_DIM ** (-0.5)
    return jnp.where(live_key[:, None, None, :], scores, -1e30)


def forward(token_rows, seq_lengths, weights_all):
    w_qkv, w_attn, w_in, w_mlp, gain_attn, gain_mlp = weights_all
    block_count = seq_lengths.shape[0]
    cos_table, sine_table = tables()
    hat_one, inv_one = standardize(token_rows)
    normed = (hat_one * gain_attn.astype(jnp.float32)).astype(jnp.bfloat16)
    merged = jnp.dot(normed, w_qkv, preferred_element_type=jnp.float32)
    merged = merged.reshape(block_count, BLOCK, 3, HEADS, HEAD_DIM)
    queries = rotate(merged[:, :, 0], cos_table, sine_table).astype(jnp.bfloat16)
    key_rows = rotate(merged[:, :, 1], cos_table, sine_table).astype(jnp.bfloat16)
    value_rows = merged[:, :, 2].astype(jnp.bfloat16)
    live_key = jnp.arange(BLOCK)[None, :] < seq_lengths[:, None]
    scores = attention_scores(queries, key_rows, live_key)
    row_max = jnp.max(scores, axis=-1, keepdims=True)
    exp_part = jnp.exp(scores - row_max)
    row_total = jnp.sum(exp_part, axis=-1, keepdims=True)
    log_total = row_max + jnp.log(row_total)
    shares = (exp_part / row_total).astype(jnp.bfloat16)
    mixture = jnp.einsum("bhqk,bkhd->bqhd", shares, value_rows, preferred_element_type=jnp.float32)
    mixture = mixture.reshape(block_count * BLOCK, D).astype(jnp.bfloat16)
    middle = token_rows + jnp.dot(mixture, w_attn, preferred_element_type=jnp.float32)
    hat_two, inv_two = standardize(middle)
    normed_two = (hat_two * gain_mlp.astype(jnp.float32)).astype(jnp.bfloat16)
    merged_two = jnp.dot(normed_two, w_in, preferred_element_type=jnp.float32)
    inner_part = merged_two[:, :FF]
    gate_part = merged_two[:, FF:]
    hidden = (jax.nn.gelu(inner_part, approximate=False) * gate_part).astype(jnp.bfloat16)
    result = middle + jnp.dot(hidden, w_mlp, preferred_element_type=jnp.float32)
    live_row = live_key.reshape(-1, 1)
    block_out = jnp.where(live_row, result, 0.0).astype(jnp.bfloat16)
    memory = (
        normed,
        hat_one,
        inv_one,
        queries,
        key_rows,
        value_rows,
        log_total,
        mixture,
        hat_two,
        inv_two,
        normed_two,
        inner_part,
        gate_part,
        hidden,
        live_key,
    )
    return (block_out, memory)


def backward(memory, cot_rows, weights_all):
    w_qkv, w_attn, w_in, w_mlp, gain_attn, gain_mlp = weights_all
    (
        normed,
        hat_one,
        inv_one,
        queries,
        key_rows,
        value_rows,
        log_total,
        mixture,
        hat_two,
        inv_two,
        normed_two,
        inner_part,
        gate_part,
        hidden,
        live_key,
    ) = memory
    block_count = live_key.shape[0]
    cos_table, sine_table = tables()
    out_grad = jnp.where(live_key.reshape(-1, 1), cot_rows, 0.0)
    out_low = out_grad.astype(jnp.bfloat16)
    d_hidden = times_t(out_low, w_mlp)
    d_inner = d_hidden * gate_part * gelu_slope(inner_part)
    d_gate = d_hidden * jax.nn.gelu(inner_part, approximate=False)
    d_merged_two = jnp.concatenate([d_inner, d_gate], axis=1).astype(jnp.bfloat16)
    d_normed_two = times_t(d_merged_two, w_in)
    gain_two_grad = jnp.sum(d_normed_two * hat_two, axis=0)
    d_middle = out_grad + norm_back(d_normed_two * gain_mlp.astype(jnp.float32), hat_two, inv_two)
    d_att = d_middle.astype(jnp.bfloat16)
    d_mixture = times_t(d_att, w_attn).astype(jnp.bfloat16)
    d_mixture = d_mixture.reshape(block_count, BLOCK, HEADS, HEAD_DIM)
    scores = attention_scores(queries, key_rows, live_key)
    shares = jnp.exp(scores - log_total)
    shares_low = shares.astype(jnp.bfloat16)
    d_shares = jnp.einsum(
        "bqhd,bkhd->bhqk", d_mixture, value_rows, preferred_element_type=jnp.float32
    )
    d_values = jnp.einsum(
        "bhqk,bqhd->bkhd", shares_low, d_mixture, preferred_element_type=jnp.float32
    )
    d_scores = shares * (d_shares - jnp.sum(shares * d_shares, axis=-1, keepdims=True))
    d_scores = d_scores.astype(jnp.bfloat16)
    d_queries = jnp.einsum(
        "bhqk,bkhd->bqhd", d_scores, key_rows, preferred_element_type=jnp.float32
    )
    d_keys = jnp.einsum("bhqk,bqhd->bkhd", d_scores, queries, preferred_element_type=jnp.float32)
    d_queries = unrotate(d_queries * HEAD_DIM ** (-0.5), cos_table, sine_table)
    d_keys = unrotate(d_keys * HEAD_DIM ** (-0.5), cos_table, sine_table)
    d_merged = jnp.stack([d_queries, d_keys, d_values], axis=2)
    d_merged = d_merged.reshape(block_count * BLOCK, 3 * D).astype(jnp.bfloat16)
    d_normed = times_t(d_merged, w_qkv)
    gain_one_grad = jnp.sum(d_normed * hat_one, axis=0)
    grad_rows = d_middle + norm_back(d_normed * gain_attn.astype(jnp.float32), hat_one, inv_one)
    pieces = (normed, d_merged, mixture, d_att, normed_two, d_merged_two, hidden, out_low)
    return (grad_rows, pieces, (gain_one_grad, gain_two_grad))


def weight_grads(pieces):
    normed, d_merged, mixture, d_att, normed_two, d_merged_two, hidden, out_low = pieces
    return (
        outer_sum(normed, d_merged),
        outer_sum(mixture, d_att),
        outer_sum(normed_two, d_merged_two),
        outer_sum(hidden, out_low),
    )


def on_device(tokens, lengths, w_qkv, w_attn, w_in, w_mlp, gain_attn, gain_mlp, cotangent):
    rows_per = BLOCKS * BLOCK
    out_blocks = []
    grad_blocks = []
    saved = []
    gain_saved = []
    for batch_index in range(MICRO):
        start_row = batch_index * rows_per
        token_rows = tokens[start_row : start_row + rows_per].astype(jnp.float32)
        cot_rows = cotangent[start_row : start_row + rows_per].astype(jnp.float32)
        seq_lengths = lengths[batch_index * BLOCKS : (batch_index + 1) * BLOCKS]
        weights_all = (
            lax.all_gather(w_qkv, "dp", axis=0, tiled=True),
            lax.all_gather(w_attn, "dp", axis=0, tiled=True),
            lax.all_gather(w_in, "dp", axis=0, tiled=True),
            lax.all_gather(w_mlp, "dp", axis=1, tiled=True),
            lax.all_gather(gain_attn, "dp", axis=0, tiled=True),
            lax.all_gather(gain_mlp, "dp", axis=0, tiled=True),
        )
        block_out, memory = forward(token_rows, seq_lengths, weights_all)
        weights_all = (
            lax.all_gather(w_qkv, "dp", axis=0, tiled=True),
            lax.all_gather(w_attn, "dp", axis=0, tiled=True),
            lax.all_gather(w_in, "dp", axis=0, tiled=True),
            lax.all_gather(w_mlp, "dp", axis=1, tiled=True),
            lax.all_gather(gain_attn, "dp", axis=0, tiled=True),
            lax.all_gather(gain_mlp, "dp", axis=0, tiled=True),
        )
        grad_rows, pieces, gain_grads = backward(memory, cot_rows, weights_all)
        out_blocks.append(block_out)
        grad_blocks.append(grad_rows)
        saved.append(pieces)
        gain_saved.append(gain_grads)
    joined = tuple(
        (jnp.concatenate([record[position] for record in saved], axis=0) for position in range(8))
    )
    g_qkv, g_attn, g_in, g_mlp = weight_grads(joined)
    gain_first = gain_saved[0][0]
    gain_second = gain_saved[0][1]
    for record in gain_saved[1:]:
        gain_first = gain_first + record[0]
        gain_second = gain_second + record[1]
    shard_sums = (
        lax.psum_scatter(g_qkv, "dp", scatter_dimension=0, tiled=True),
        lax.psum_scatter(g_attn, "dp", scatter_dimension=0, tiled=True),
        lax.psum_scatter(g_in, "dp", scatter_dimension=0, tiled=True),
        lax.psum_scatter(g_mlp, "dp", scatter_dimension=1, tiled=True),
        lax.psum_scatter(gain_first, "dp", scatter_dimension=0, tiled=True),
        lax.psum_scatter(gain_second, "dp", scatter_dimension=0, tiled=True),
    )
    return (
        jnp.concatenate(out_blocks, axis=0),
        jnp.concatenate(grad_blocks, axis=0),
        shard_sums[0],
        shard_sums[1],
        shard_sums[2],
        shard_sums[3],
        shard_sums[4],
        shard_sums[5],
    )


def solution(mesh):
    return jax.shard_map(
        on_device,
        mesh=mesh,
        in_specs=(
            P("dp", None),
            P("dp"),
            P("dp", None),
            P("dp", None),
            P("dp", None),
            P(None, "dp"),
            P("dp"),
            P("dp"),
            P("dp", None),
        ),
        out_specs=(
            P("dp", None),
            P("dp", None),
            P("dp", None),
            P("dp", None),
            P("dp", None),
            P(None, "dp"),
            P("dp"),
            P("dp"),
        ),
        check_vma=False,
    )
```

profile of v0, /device:TPU:0, one launch (start us, length us, event | category | flops | bytes accessed | tf_op | source)
XLA Modules:
  0.0 702.1 jit_solution(17646584342923000085)
XLA Ops:
  9.5 42.0 %all-reduce.6 = (bf16[256]{0:T(256)(128)(2,1)S(1)}, bf16[256]{0:T(256)(128)(2,1)}) all-reduce(bf16[256]{0:T(256)(128)(2,1)S(1)} %dynamic-update-slice, bf16[256]{0:T(256)(128)(2,1)S(1)} %dynamic-update-slice.1), channel_id=1, replica_groups=mesh['dp'=32] {'dp'}, use_global_device_ids=true, to_apply=%add | all-reduce | flops 512 | bytes 2048
  51.5 1.2 convert_reduce_fusion.2
  52.8 1.3 fusion.166
  54.2 41.5 %all_gather.13 = bf16[256,768]{1,0:T(8,128)(2,1)S(1)} all-gather(bf16[8,768]{1,0:T(8,128)(2,1)S(1)} %copy-done.75), channel_id=1, replica_groups=mesh['dp'=32] {'dp'}, dimensions={0}, use_global_device_ids=true | all-gather | bytes 405504 | tf_op jit(solution)/shard_map/all_gather | solution.py:206
  103.7 37.0 %all_gather.14 = bf16[256,256]{1,0:T(8,128)(2,1)S(1)} all-gather(bf16[8,256]{1,0:T(8,128)(2,1)S(1)} %copy-done.100), channel_id=1, replica_groups=mesh['dp'=32] {'dp'}, dimensions={0}, use_global_device_ids=true | all-gather | bytes 135168 | tf_op jit(solution)/shard_map/all_gather | solution.py:207
  140.7 38.6 %all_gather.17 = bf16[384,256]{0,1:T(8,128)(2,1)S(1)} all-gather(bf16[384,8]{0,1:T(8,128)(2,1)S(1)} %copy-done.94), channel_id=1, replica_groups=mesh['dp'=32] {'dp'}, dimensions={1}, use_global_device_ids=true | all-gather | bytes 202752 | tf_op jit(solution)/shard_map/all_gather | solution.py:209
  179.4 37.9 %all_gather.16 = bf16[256,768]{1,0:T(8,128)(2,1)S(1)} all-gather(bf16[8,768]{1,0:T(8,128)(2,1)S(1)} %copy-done.76), channel_id=1, replica_groups=mesh['dp'=32] {'dp'}, dimensions={0}, use_global_device_ids=true | all-gather | bytes 405504 | tf_op jit(solution)/shard_map/all_gather | solution.py:208
  227.5 1.2 multiply_convert_fusion.5
  230.4 1.2 multiply_convert_fusion.3
  232.7 1.3 fusion.239
  234.0 1.8 multiply_convert_fusion.4
  236.6 1.2 fusion.33
  237.9 2.1 multiply_reduce_fusion.4
  240.0 1.9 fusion.241
  243.7 2.7 fusion.9
  249.5 1.2 multiply_reduce_fusion
  258.8 1.2 multiply_reduce_fusion.1
  268.3 1.4 fusion.3
  273.9 37.0 %all-reduce.5 = (f32[256]{0:T(256)S(1)}, f32[256]{0:T(256)S(1)}) all-reduce(f32[256]{0:T(256)S(1)} %add_add_fusion.1, f32[256]{0:T(256)S(1)} %add_add_fusion), channel_id=6, replica_groups=mesh['dp'=32] {'dp'}, use_global_device_ids=true, to_apply=%region_40.41.clone | all-reduce | flops 512 | bytes 4096
  314.6 48.4 %all-reduce.9.cloned.1.call-done = f32[384,256]{0,1:T(8,128)} async-done(((f32[384,256]{0,1:T(8,128)}), f32[384,256]{0,1:T(8,128)}) %all-reduce.9.cloned.1.call-update) | async-done | bytes 393232
  363.0 1.3 constant_dynamic-slice_fusion
  364.3 134.0 %reduce-scatter.6.cloned.1.call-done = f32[8,256]{1,0:T(8,128)} async-done(((f32[256,256]{1,0:T(8,128)}), f32[8,256]{1,0:T(8,128)}) %reduce-scatter.6.cloned.1.call-update) | async-done | bytes 8208 | tf_op jit(solution)/shard_map/reduce_scatter | solution.py:238
  498.3 97.1 %reduce-scatter.8.cloned.1.call-done = f32[8,768]{1,0:T(8,128)} async-done(((f32[256,768]{1,0:T(8,128)}), f32[8,768]{1,0:T(8,128)}) %reduce-scatter.8.cloned.1.call-update) | async-done | bytes 24592 | tf_op jit(solution)/shard_map/reduce_scatter | solution.py:239
  595.4 100.1 %reduce-scatter.4.cloned.1.call-done = f32[8,768]{1,0:T(8,128)} async-done(((f32[256,768]{1,0:T(8,128)}), f32[8,768]{1,0:T(8,128)}) %reduce-scatter.4.cloned.1.call-update) | async-done | bytes 24592 | tf_op jit(solution)/shard_map/reduce_scatter | solution.py:237
  (371 shorter events, 51.8 us)
Async XLA Ops:
  7.2 88.5 %copy-start = (bf16[768,256]{1,0:T(8,128)(2,1)S(1)}, bf16[768,256]{1,0:T(8,128)(2,1)}, u32[]{:S(2)}) copy-start(bf16[768,256]{1,0:T(8,128)(2,1)} %param.9) | copy-start | bytes 1179652
  7.2 47.0 %copy-start.75 = (bf16[8,768]{1,0:T(8,128)(2,1)S(1)}, bf16[8,768]{1,0:T(8,128)(2,1)}, u32[]{:S(2)}) copy-start(bf16[8,768]{1,0:T(8,128)(2,1)} %param.11) | copy-start | bytes 36868
  7.2 355.8 %all-reduce.9.cloned.1.call-start = ((), (), s32[]{:S(2)}) async-start(), calls=%async_computation.6 | async-start | bytes 786432
  51.5 44.4 %copy-start.85 = (f32[256]{0:T(256)}, f32[256]{0:T(256)S(1)}, u32[]{:S(2)}) copy-start(f32[256]{0:T(256)S(1)} %convert_element_type.197) | copy-start | bytes 3076
  52.7 43.2 %copy-start.67 = (f32[256]{0:T(256)}, f32[256]{0:T(256)S(1)}, u32[]{:S(2)}) copy-start(f32[256]{0:T(256)S(1)} %get-tuple-element.153) | copy-start | bytes 3076
  52.7 43.2 %copy-start.73 = (f32[256]{0:T(256)}, f32[256]{0:T(256)S(1)}, u32[]{:S(2)}) copy-start(f32[256]{0:T(256)S(1)} %get-tuple-element.154) | copy-start | bytes 3076
  54.1 42.8 %copy-start.79 = (f32[256]{0:T(256)}, f32[256]{0:T(256)S(1)}, u32[]{:S(2)}) copy-start(f32[256]{0:T(256)S(1)} %add_rsqrt_fusion.5) | copy-start | bytes 3076
  54.1 42.8 %copy-start.87 = (f32[256]{0:T(256)}, f32[256]{0:T(256)S(1)}, u32[]{:S(2)}) copy-start(f32[256]{0:T(256)S(1)} %add_rsqrt_fusion.3) | copy-start | bytes 3076
  54.2 42.8 %copy-start.81 = (f32[256]{0:T(256)}, f32[256]{0:T(256)S(1)}, u32[]{:S(2)}) copy-start(f32[256]{0:T(256)S(1)} %add_rsqrt_fusion.1) | copy-start | bytes 3076
  102.0 38.7 %copy-start.1 = (f32[2,128,3,4,64]{1,0,4,3,2:T(2,128)}, f32[2,128,3,4,64]{1,0,4,3,2:T(2,128)S(1)}, u32[]{:S(2)}) copy-start(f32[2,128,3,4,64]{1,0,4,3,2:T(2,128)S(1)} %reshape.348) | copy-start | bytes 2359300
  102.1 38.6 %copy-start.94 = (bf16[384,8]{0,1:T(8,128)(2,1)S(1)}, bf16[384,8]{0,1:T(8,128)(2,1)}, u32[]{:S(2)}) copy-start(bf16[384,8]{0,1:T(8,128)(2,1)} %param.14) | copy-start | bytes 18436
  102.2 122.7 %copy-start.49 = (bf16[2,128,1,4,64]{1,0,4,3,2:T(2,128)(2,1)}, bf16[2,128,1,4,64]{1,0,4,3,2:T(2,128)(2,1)S(1)}, u32[]{:S(2)}) copy-start(bf16[2,128,1,4,64]{1,0,4,3,2:T(2,128)(2,1)S(1)} %slice.213) | copy-start | bytes 393220
  102.2 77.1 %copy-start.76 = (bf16[8,768]{1,0:T(8,128)(2,1)S(1)}, bf16[8,768]{1,0:T(8,128)(2,1)}, u32[]{:S(2)}) copy-start(bf16[8,768]{1,0:T(8,128)(2,1)} %param.13) | copy-start | bytes 36868
  102.2 115.0 %copy-start.24 = (f32[2,128,4,64]{1,0,3,2:T(2,128)S(1)}, f32[2,128,4,64]{1,0,3,2:T(2,128)}, u32[]{:S(2)}) copy-start(f32[2,128,4,64]{1,0,3,2:T(2,128)} %get-tuple-element.61) | copy-start | bytes 786436
  102.3 115.0 %copy-start.22 = (f32[2,128,4,64]{1,0,3,2:T(2,128)S(1)}, f32[2,128,4,64]{1,0,3,2:T(2,128)}, u32[]{:S(2)}) copy-start(f32[2,128,4,64]{1,0,3,2:T(2,128)} %get-tuple-element.62) | copy-start | bytes 786436
  102.8 129.8 %copy-start.77 = (f32[256]{0:T(256)}, f32[256]{0:T(256)S(1)}, u32[]{:S(2)}) copy-start(f32[256]{0:T(256)S(1)} %convert_element_type.206) | copy-start | bytes 3076
  103.0 129.7 %copy-start.96 = (pred[256]{0:T(512)(128)(4,1)}, pred[256]{0:T(512)(128)(4,1)S(1)}, u32[]{:S(2)}) copy-start(pred[256]{0:T(512)(128)(4,1)S(1)} %get-tuple-element.121) | copy-start | bytes 772
  140.7 76.7 %copy-start.23 = (f32[2,128,4,64]{1,0,3,2:T(2,128)S(1)}, f32[2,128,4,64]{1,0,3,2:T(2,128)}, u32[]{:S(2)}) copy-start(f32[2,128,4,64]{1,0,3,2:T(2,128)} %get-tuple-element.63) | copy-start | bytes 786436
  179.3 54.7 %copy-start.7 = (bf16[384,256]{0,1:T(8,128)(2,1)}, bf16[384,256]{0,1:T(8,128)(2,1)S(1)}, u32[]{:S(2)}) copy-start(bf16[384,256]{0,1:T(8,128)(2,1)S(1)} %all_gather.17) | copy-start | bytes 589828
  221.3 11.4 %copy-start.92 = (pred[256]{0:T(512)(128)(4,1)}, pred[256]{0:T(512)(128)(4,1)S(1)}, u32[]{:S(2)}) copy-start(pred[256]{0:T(512)(128)(4,1)S(1)} %get-tuple-element.156) | copy-start | bytes 772
  237.8 260.5 %reduce-scatter.6.cloned.1.call-start = ((), (), s32[]{:S(2)}) async-start(), calls=%async_computation.4 | async-start | bytes 270336 | tf_op jit(solution)/shard_map/reduce_scatter | solution.py:238
  243.6 351.8 %reduce-scatter.8.cloned.1.call-start = ((), (), s32[]{:S(2)}) async-start(), calls=%async_computation.5 | async-start | bytes 811008 | tf_op jit(solution)/shard_map/reduce_scatter | solution.py:239
  246.5 449.1 %reduce-scatter.4.cloned.1.call-start = ((), (), s32[]{:S(2)}) async-start(), calls=%async_computation.3 | async-start | bytes 811008 | tf_op jit(solution)/shard_map/reduce_scatter | solution.py:237
  273.8 39.1 %copy-start.21 = (f32[256,256]{1,0:T(8,128)S(1)}, f32[256,256]{1,0:T(8,128)}, u32[]{:S(2)}) copy-start(f32[256,256]{1,0:T(8,128)} %get-tuple-element.45) | copy-start | bytes 786436
  (90 other events, 141.3 us)
Sparse Core Ops, SparseCore 0:
  237.9 125.0 all-reduce.8
  365.9 132.3 reduce-scatter.5
  504.0 91.3 reduce-scatter.7
  601.0 94.5 reduce-scatter.3
where the time goes:
time: 703 us; the launch traced here: 702 us
  waiting for transfers between devices  380 us (54%)
  blocking collectives  234 us (33%)
  matrix products  30.1 us (4%)
  local copies, waits for them, and re-layouts  26.7 us (4%)
  other arithmetic  15.7 us (2%)
  between operations  15.5 us (2%)
    reduce_scatter x1, waiting for transfers between devices, on_device(): lax.psum_scatter(g_attn, 'dp', scatter_dimension=0, tiled=True)  134 us
    reduce_scatter x1, waiting for transfers between devices, on_device(): lax.psum_scatter(g_qkv, 'dp', scatter_dimension=0, tiled=True)  100 us
    reduce_scatter x1, waiting for transfers between devices, on_device(): lax.psum_scatter(g_in, 'dp', scatter_dimension=0, tiled=True)  97.1 us
    unnamed x2, blocking collectives  79.1 us
    unnamed x5, waiting for transfers between devices  48.5 us
    all_gather x1, blocking collectives, on_device(): lax.all_gather(w_qkv, 'dp', axis=0, tiled=True)  41.5 us
    all_gather x1, blocking collectives, on_device(): lax.all_gather(w_mlp, 'dp', axis=1, tiled=True)  38.6 us
    all_gather x1, blocking collectives, on_device(): lax.all_gather(w_in, 'dp', axis=0, tiled=True)  37.9 us
  transfers between devices with their start and end apart: 4, of which 4 were waited for; matrix products, arithmetic and copies ran while one was open for 5% of the time, Pallas kernels for 0%

commit v1 on v0

v1 whole, which is shorter than its diff:
```python
import functools

import jax
import jax.numpy as jnp
import numpy as np
from jax import lax
from jax.experimental import pallas as pl
from jax.experimental.pallas import tpu as pltpu
from jax.sharding import PartitionSpec as P

D = 256
FF = 384
HEADS = 4
HEAD_DIM = 64
BLOCK = 128
BLOCKS = 2
HALF = D // 2
WIDE = HEADS * BLOCK
QKV = 3 * D
LANES = 128
FIRST = QKV + D + LANES
SECOND = 2 * FF + FF
SUMS = QKV + D

rope_base = 160000.0
eps_norm = 1e-05
bf16 = jnp.bfloat16
f32 = jnp.float32


def tables():
    half_dim = HEAD_DIM // 2
    frequency = rope_base ** (-(np.arange(half_dim) * 2.0) / HEAD_DIM)
    angles = np.arange(BLOCK)[:, None] * frequency[None, :]
    angles = np.tile(angles, (BLOCKS, HEADS))
    return np.cos(angles).astype(np.float32), np.sin(angles).astype(np.float32)


def mm(left, right):
    return lax.dot_general(left, right, (((1,), (0,)), ((), ())), preferred_element_type=f32)


def mm_nt(left, right):
    return lax.dot_general(left, right, (((1,), (1,)), ((), ())), preferred_element_type=f32)


def mm_tn(left, right):
    return lax.dot_general(left, right, (((0,), (0,)), ((), ())), preferred_element_type=f32)


def spread_columns(forward):
    old = lax.broadcasted_iota(jnp.int32, (D, D), 0 if forward else 1)
    new = lax.broadcasted_iota(jnp.int32, (D, D), 1 if forward else 0)
    target = ((old // 32) % 2) * HALF + (old // HEAD_DIM) * 32 + old % 32
    return jnp.where(target == new, 1.0, 0.0).astype(bf16)


def to_column(row):
    size = row.shape[1]
    here = lax.broadcasted_iota(jnp.int32, (size, size), 0)
    there = lax.broadcasted_iota(jnp.int32, (size, size), 1)
    return jnp.sum(jnp.where(here == there, row, 0.0), axis=1, keepdims=True)


def to_row(column):
    size = column.shape[0]
    here = lax.broadcasted_iota(jnp.int32, (size, size), 0)
    there = lax.broadcasted_iota(jnp.int32, (size, size), 1)
    return jnp.sum(jnp.where(here == there, column, 0.0), axis=0, keepdims=True)


def pack_kernel(w_qkv, w_attn, w_in, w_mlp, gain_attn, gain_mlp, out):
    spread = spread_columns(True)
    out[:, :D] = mm(w_qkv[:, :D], spread).astype(bf16)
    out[:, D : 2 * D] = mm(w_qkv[:, D : 2 * D], spread).astype(bf16)
    out[:, 2 * D : QKV] = w_qkv[:, 2 * D :]
    out[:, QKV : QKV + D] = w_attn[...]
    lane = lax.broadcasted_iota(jnp.int32, (out.shape[0], LANES), 1)
    gains = jnp.where(lane == 0, to_column(gain_attn[...].astype(f32)), 0.0)
    gains = jnp.where(lane == 1, to_column(gain_mlp[...].astype(f32)), gains)
    out[:, QKV + D : FIRST] = gains.astype(bf16)
    out[:, FIRST : FIRST + 2 * FF] = w_in[...]
    out[:, FIRST + 2 * FF :] = w_mlp[...]


def end_kernel(kept, got, w_qkv, w_in, gain_attn, gain_mlp, g_qkv, g_attn, g_in, g_mlp, g_first, g_second):
    total = kept[...].astype(f32) + got[...].astype(f32)
    part = total[:, :QKV]
    g_qkv[...] = part
    g_first[...] = to_row(jnp.sum(part * w_qkv[...].astype(f32), axis=1, keepdims=True)) / gain_attn[...].astype(f32)
    g_attn[...] = total[:, QKV : QKV + D]
    part = total[:, QKV + D : QKV + D + 2 * FF]
    g_in[...] = part
    g_second[...] = to_row(jnp.sum(part * w_in[...].astype(f32), axis=1, keepdims=True)) / gain_mlp[...].astype(f32)
    g_mlp[...] = total[:, QKV + D + 2 * FF :]


def standardize(values):
    centre = values - jnp.mean(values, axis=-1, keepdims=True)
    inverse = lax.rsqrt(jnp.mean(centre * centre, axis=-1, keepdims=True) + eps_norm)
    return centre * inverse, inverse


def norm_back(d_hat, hat_rows, inverse):
    mean_one = jnp.mean(d_hat, axis=-1, keepdims=True)
    mean_two = jnp.mean(d_hat * hat_rows, axis=-1, keepdims=True)
    return inverse * (d_hat - mean_one - hat_rows * mean_two)


def stack_heads(rows, masks):
    return jnp.concatenate([rows * mask for mask in masks], axis=0)


def turn_heads(values):
    return jnp.concatenate(
        [values[:, h * BLOCK : (h + 1) * BLOCK].T for h in range(HEADS)], axis=1
    )


def slot_order(hops, rows, me, slot_axis):
    slots = lax.broadcasted_iota(jnp.int32, (D, D), slot_axis)
    place = slots // rows
    owner = jnp.full((D, D), me, jnp.int32)
    for bit, mask in enumerate(hops):
        owner = owner ^ (((place >> bit) & 1) * mask)
    found = owner * rows + slots % rows == lax.broadcasted_iota(jnp.int32, (D, D), 1 - slot_axis)
    return jnp.where(found, 1.0, 0.0).astype(bf16)


def head_masks():
    lane = lax.broadcasted_iota(jnp.int32, (1, D), 1)
    spread = [jnp.where((lane % HALF) // 32 == h, 1.0, 0.0).astype(bf16) for h in range(HEADS)]
    plain = [jnp.where(lane // HEAD_DIM == h, 1.0, 0.0).astype(bf16) for h in range(HEADS)]
    return spread, plain


def chunks(total):
    cap = BLOCKS * BLOCK
    return [(i, slice(i * cap, (i + 1) * cap)) for i in range(total // cap)]


def block_slices(start):
    return [slice(start + b * BLOCK, start + (b + 1) * BLOCK) for b in range(BLOCKS)]


def live_rows(lengths, index):
    row = lax.broadcasted_iota(jnp.int32, (BLOCK, 1), 0)
    live = [jnp.where(row < lengths[index * BLOCKS + b], 1.0, 0.0) for b in range(BLOCKS)]
    return jnp.concatenate(live, axis=0) > 0.5


def attend_kernel(
    hops, rows, me, lengths, tokens, packed, other, cos, sin, weights, w_attn, gains, normed, heads, shares, mixture
):
    order = slot_order(hops, rows, me[0], 1)
    ordered = mm(order[:, : D // 2], packed[...]) + mm(order[:, D // 2 :], other[...])
    weights[...] = ordered[:, :QKV].astype(bf16)
    w_attn[...] = ordered[:, QKV : QKV + D].astype(bf16)
    here = lax.broadcasted_iota(jnp.int32, (D, D), 0) == lax.broadcasted_iota(jnp.int32, (D, D), 1)
    for k in range(2):
        column = ordered[:, QKV + D + k : QKV + D + k + 1]
        gains[k : k + 1, :] = jnp.sum(jnp.where(here, column, 0.0), axis=0, keepdims=True)
    gain = gains[0:1, :]
    w_qkv = weights[...]
    c = cos[...]
    s = sin[...]
    spread_masks, plain_masks = head_masks()
    key_lane = lax.broadcasted_iota(jnp.int32, (1, BLOCK), 1)
    for index, part in chunks(tokens.shape[0]):
        low = (standardize(tokens[part].astype(f32))[0] * gain).astype(bf16)
        normed[part] = low
        qkv = mm(low, w_qkv)

        def rope(base):
            low, high = qkv[:, base : base + HALF], qkv[:, base + HALF : base + D]
            return jnp.concatenate([low * c - high * s, high * c + low * s], axis=1)

        heads[part, :D] = (rope(0) * HEAD_DIM ** (-0.5)).astype(bf16)
        heads[part, D : 2 * D] = rope(D).astype(bf16)
        heads[part, 2 * D :] = qkv[:, 2 * D :].astype(bf16)
        for b, block in enumerate(block_slices(part.start)):
            live = key_lane < lengths[index * BLOCKS + b]
            scores = mm_nt(heads[block, :D], stack_heads(heads[block, D : 2 * D], spread_masks))
            for h in range(HEADS):
                cut = slice(h * BLOCK, (h + 1) * BLOCK)
                one = jnp.where(live, scores[:, cut], -1e30)
                grown = jnp.exp(one - jnp.max(one, axis=1, keepdims=True))
                shares[block, cut] = grown * (1.0 / jnp.sum(grown, axis=1, keepdims=True))
            mixed = mm(shares[block].astype(bf16), stack_heads(heads[block, 2 * D :], plain_masks))
            mixture[block] = mixed.astype(bf16)


def feed_kernel(
    hops, rows, me, lengths, tokens, cot, packed, other, attn, gains, mixture,
    w_mlp, middle, hidden, d_middle, d_mixture, g_attn, sums, hat_two_low, out_low, d_att, d_merged,
):
    order = slot_order(hops, rows, me[0], 1)
    ordered = mm(order[:, : D // 2], packed[...]) + mm(order[:, D // 2 :], other[...])
    ordered = ordered.astype(bf16)
    w_attn = attn[...]
    w_in = ordered[:, : 2 * FF]
    w_mlp[...] = ordered[:, 2 * FF :]
    gain = gains[1:2, :]
    for index, part in chunks(tokens.shape[0]):
        mid = tokens[part].astype(f32) + mm(mixture[part], w_attn)
        middle[part] = mid
        hat_two, inv_two = standardize(mid)
        low = (hat_two * gain).astype(bf16)
        hat_two_low[part] = low
        merged = mm(low, w_in)
        inner = merged[:, :FF]
        gate = merged[:, FF:]
        cdf = 0.5 * (1.0 + lax.erf(inner * 0.7071067811865476))
        curved = inner * cdf
        slope = cdf + inner * jnp.exp(-0.5 * inner * inner) * 0.3989422804014327
        hidden[part] = (curved * gate).astype(bf16)
        out_grad = jnp.where(live_rows(lengths, index), cot[part].astype(f32), 0.0)
        out_low[part] = out_grad.astype(bf16)
        d_hidden = mm(out_low[part], w_mlp[...])
        d_merged[part, :FF] = (d_hidden * gate * slope).astype(bf16)
        d_merged[part, FF:] = (d_hidden * curved).astype(bf16)
        d_normed = mm_nt(d_merged[part], w_in)
        d_mid = out_grad + norm_back(d_normed * gain, hat_two, inv_two)
        d_middle[part] = d_mid
        d_att[part] = d_mid.astype(bf16)
        d_mixture[part] = mm_nt(d_att[part], w_attn).astype(bf16)
    order = slot_order(hops, rows, me[0], 0)
    total = mm_tn(hat_two_low[...], d_merged[...]).astype(bf16)
    sums[:, : 2 * FF] = mm(order, total).astype(bf16)
    total = mm_tn(out_low[...], hidden[...]).astype(bf16)
    sums[:, 2 * FF :] = mm(order, total).astype(bf16)
    g_attn[...] = mm_tn(mixture[...], d_att[...]).astype(bf16)


def attend_back_kernel(
    hops, rows, me, heads, shares, d_mixture, normed, g_attn, cos, sin, sums, d_qkv
):
    c = cos[...]
    s = sin[...]
    spread_masks, plain_masks = head_masks()

    def rope_back(grads):
        low, high = grads[:, :HALF], grads[:, HALF:]
        return jnp.concatenate([low * c + high * s, high * c - low * s], axis=1).astype(bf16)

    for index, part in chunks(heads.shape[0]):
        d_queries = []
        d_keys = []
        for block in block_slices(part.start):
            queries, key_rows, value_rows = heads[block, :D], heads[block, D : 2 * D], heads[block, 2 * D :]
            d_mixed = d_mixture[block]
            d_shares = mm_nt(d_mixed, stack_heads(value_rows, plain_masks))
            d_scores = []
            for h in range(HEADS):
                cut = slice(h * BLOCK, (h + 1) * BLOCK)
                one, d_one = shares[block, cut], d_shares[:, cut]
                d_one = one * (d_one - jnp.sum(one * d_one, axis=1, keepdims=True))
                d_scores.append(d_one.astype(bf16))
            d_scores = jnp.concatenate(d_scores, axis=1)
            d_queries.append(mm(d_scores, stack_heads(key_rows, spread_masks)))
            d_keys.append(mm(turn_heads(d_scores), stack_heads(queries, spread_masks)))
            d_values = mm(turn_heads(shares[block].astype(bf16)), stack_heads(d_mixed, plain_masks))
            d_qkv[block, 2 * D :] = d_values.astype(bf16)
        d_qkv[part, :D] = rope_back(jnp.concatenate(d_queries, axis=0) * HEAD_DIM ** (-0.5))
        d_qkv[part, D : 2 * D] = rope_back(jnp.concatenate(d_keys, axis=0))
    order = slot_order(hops, rows, me[0], 0)
    total = mm_tn(normed[...], d_qkv[...]).astype(bf16)
    placed = mm(order, total).astype(bf16)
    spread = spread_columns(False)
    sums[:, :D] = mm(placed[:, :D], spread).astype(bf16)
    sums[:, D : 2 * D] = mm(placed[:, D : 2 * D], spread).astype(bf16)
    sums[:, 2 * D : QKV] = placed[:, 2 * D :]
    sums[:, QKV:] = mm(order, g_attn[...]).astype(bf16)


def outputs_kernel(lengths, tokens, weights, gains, d_qkv, d_middle, middle, hidden, w_mlp, out, grad):
    gain = gains[0:1, :]
    for index, part in chunks(tokens.shape[0]):
        result = middle[part] + mm_nt(hidden[part], w_mlp[...])
        out[part] = jnp.where(live_rows(lengths, index), result, 0.0).astype(bf16)
        hat_one, inv_one = standardize(tokens[part].astype(f32))
        d_normed = mm_nt(d_qkv[part], weights[...])
        grad[part] = d_middle[part] + norm_back(d_normed * gain, hat_one, inv_one)


SMALL = pl.BlockSpec(memory_space=pltpu.SMEM)
NEAR = pl.BlockSpec(memory_space=pltpu.VMEM)


def call(kernel, in_specs, shapes, scratch=()):
    return pl.pallas_call(
        kernel,
        in_specs=in_specs,
        out_specs=[NEAR] * len(shapes),
        out_shape=[jax.ShapeDtypeStruct(shape, kind) for shape, kind in shapes],
        scratch_shapes=[pltpu.VMEM(shape, kind) for shape, kind in scratch],
        compiler_params=pltpu.CompilerParams(vmem_limit_bytes=32 * 1024 * 1024),
    )


def put(room, piece, slot, column=0):
    return lax.dynamic_update_slice(room, piece, (slot, 0, column))


def on_device(n, tokens, lengths, w_qkv, w_attn, w_in, w_mlp, gain_attn, gain_mlp, cotangent):
    rows = D // n
    count = tokens.shape[0]
    hops = []
    while 2 ** len(hops) < n:
        hops.append(n >> (len(hops) + 1))
    last = len(hops) - 1
    swapped = list(hops)
    joined = last
    if last > 1:
        swapped[last - 2], swapped[last - 1] = hops[last - 1], hops[last - 2]
        joined = last - 2
    hops, swapped = tuple(hops), tuple(swapped)
    gain_attn = gain_attn.reshape(1, rows)
    gain_mlp = gain_mlp.reshape(1, rows)

    def trade(values, mask):
        return lax.ppermute(values, "dp", [(i, i ^ mask) for i in range(n)])

    held = pl.pallas_call(
        pack_kernel, out_specs=NEAR, out_shape=jax.ShapeDtypeStruct((rows, FIRST + SECOND), bf16)
    )(w_qkv, w_attn, w_in, w_mlp.T, gain_attn, gain_mlp)
    room = put(jnp.zeros((2**joined, rows, FIRST + SECOND), bf16), held[None], 0)
    for k in range(joined):
        room = put(room, trade(room[: 2**k], hops[k]), 2**k)
    first = put(jnp.zeros((n // 2, rows, FIRST), bf16), room[:, :, :FIRST], 0)
    second = put(jnp.zeros((n // 2, rows, SECOND), bf16), room[:, :, FIRST:], 0)
    for k in range(joined, last):
        one, two = trade(first[: 2**k], hops[k]), trade(second[: 2**k], swapped[k])
        first, second = put(first, one, 2**k), put(second, two, 2**k)
    first_got, second_got = trade(first, 1), trade(second, 1)
    first = first.reshape(D // 2, FIRST), first_got.reshape(D // 2, FIRST)
    second = second.reshape(D // 2, SECOND), second_got.reshape(D // 2, SECOND)

    cos, sin = tables()
    cos, sin = jnp.asarray(cos), jnp.asarray(sin)
    me = lax.axis_index("dp").astype(jnp.int32).reshape(1)
    weights, attn, gains, normed, heads, shares, mixture = call(
        functools.partial(attend_kernel, hops, rows),
        [SMALL] * 2 + [NEAR] * 5,
        [((D, QKV), bf16), ((D, D), bf16), ((2, D), f32), ((count, D), bf16), ((count, QKV), bf16), ((count, WIDE), f32), ((count, D), bf16)],
    )(me, lengths, tokens, *first, cos, sin)
    w_mlp_all, middle, hidden, d_middle, d_mixture, g_attn, second_sums = call(
        functools.partial(feed_kernel, swapped, rows),
        [SMALL] * 2 + [NEAR] * 7,
        [((D, FF), bf16), ((count, D), f32), ((count, FF), bf16), ((count, D), f32), ((count, D), bf16), ((D, D), bf16), ((D, 3 * FF), bf16)],
        [((count, D), bf16), ((count, D), bf16), ((count, D), bf16), ((count, 2 * FF), bf16)],
    )(me, lengths, tokens, cotangent, *second, attn, gains, mixture)
    first_sums, d_qkv = call(
        functools.partial(attend_back_kernel, hops, rows),
        [SMALL] + [NEAR] * 7,
        [((D, SUMS), bf16), ((count, QKV), bf16)],
    )(me, heads, shares, d_mixture, normed, g_attn, cos, sin)
    out, grad = call(
        outputs_kernel, [SMALL] + [NEAR] * 8, [((count, D), bf16), ((count, D), f32)]
    )(lengths, tokens, weights, gains, d_qkv, d_middle, middle, hidden, w_mlp_all)

    def halve(kept, mask):
        half = kept.shape[0] // 2
        got = trade(kept[half:], mask)
        return (kept[:half].astype(f32) + got.astype(f32)).astype(bf16)

    first, second = first_sums.reshape(n, rows, SUMS), second_sums.reshape(n, rows, 3 * FF)
    for k in range(last, joined - 1, -1):
        first, second = halve(first, hops[k]), halve(second, swapped[k])
    kept = jnp.zeros((2**joined, rows, SUMS + 3 * FF), bf16)
    kept = put(put(kept, first, 0), second, 0, SUMS)
    for k in range(joined - 1, 0, -1):
        kept = halve(kept, hops[k])
    got = trade(kept[1], hops[0])
    g_qkv, g_attn, g_in, g_mlp, g_first, g_second = call(
        end_kernel,
        [NEAR] * 6,
        [((rows, QKV), f32), ((rows, D), f32), ((rows, 2 * FF), f32), ((rows, FF), f32), ((1, rows), f32), ((1, rows), f32)],
    )(kept[0], got, w_qkv, w_in, gain_attn, gain_mlp)
    return out, grad, g_qkv, g_attn, g_in, g_mlp.T, g_first.reshape(rows), g_second.reshape(rows)


def solution(mesh):
    rows = P("dp", None)
    return jax.shard_map(
        functools.partial(on_device, mesh.shape["dp"]),
        mesh=mesh,
        in_specs=(rows, P("dp"), rows, rows, rows, P(None, "dp"), P("dp"), P("dp"), rows),
        out_specs=(rows, rows, rows, rows, rows, P(None, "dp"), P("dp"), P("dp")),
        check_vma=False,
    )
```

time: 703 us -> 62.6 us (0.09)
  waiting for transfers between devices: 380 us -> 18.7 us
  blocking collectives: 234 us -> 0 us
  matrix products: 30.1 us -> 0 us
  local copies, waits for them, and re-layouts: 26.7 us -> 1.11 us
  starting transfers between devices: 0.38 us -> 23.9 us
  Pallas kernels: 0 us -> 17.5 us
  other arithmetic: 15.7 us -> 0.28 us
  between operations: 15.5 us -> 0.93 us
    reduce_scatter x3 -> x0, waiting for transfers between devices: 331 us -> none  [the longest x1 134 us: on_device(): lax.psum_scatter(g_attn, 'dp', scatter_dimension=0, tiled=True)]
    all_gather x4 -> x0, blocking collectives: 155 us -> none  [the longest x1 41.5 us: on_device(): lax.all_gather(w_qkv, 'dp', axis=0, tiled=True)]
    unnamed x2 -> x0, blocking collectives: 79.1 us -> none
    unnamed x5 -> x0, waiting for transfers between devices: 48.5 us -> none
    dot_general x46 -> x0, matrix products: 30.1 us -> none  [the longest x12 10.9 us: times_t(): lax.dot_general(left, right, (((1,), (1,)), ((), ())), preferred_element_...]
    ppermute x0 -> x16, starting transfers between devices: none -> 23.9 us  [trade(): return lax.ppermute(values, 'dp', [(i, i ^ mask) for i in range(n)])]
    ppermute x0 -> x16, waiting for transfers between devices: none -> 18.7 us  [trade(): return lax.ppermute(values, 'dp', [(i, i ^ mask) for i in range(n)])]
    unnamed x233 -> x18, local copies, waits for them, and re-layouts: 18.5 us -> 0.05 us
  transfers between devices with their start and end apart: 4 -> 16, of which waited for: 4 -> 11; matrix products, arithmetic and copies ran while one was open for 5% -> 2% of each run, Pallas kernels for 0% -> 11%
where the time goes in v1:
time: 62.6 us; the launch traced here: 62.4 us
  starting transfers between devices  23.9 us (38%)
  waiting for transfers between devices  18.7 us (30%)
  Pallas kernels  17.5 us (28%)
  local copies, waits for them, and re-layouts  1.11 us (2%)
  between operations  0.93 us (1%)
    ppermute x16, starting transfers between devices, trade(): return lax.ppermute(values, 'dp', [(i, i ^ mask) for i in range(n)])  23.9 us
    ppermute x16, waiting for transfers between devices, trade(): return lax.ppermute(values, 'dp', [(i, i ^ mask) for i in range(n)])  18.7 us
    pallas_call x1, Pallas kernels, on_device(): call(functools.partial(feed_kernel, swapped, rows), [SMALL] * 2 + [NEAR]...  5.07 us
    pallas_call x1, Pallas kernels, on_device(): call(functools.partial(attend_kernel, hops, rows), [SMALL] * 2 + [NEAR] *...  4.36 us
    pallas_call x1, Pallas kernels, on_device(): call(functools.partial(attend_back_kernel, hops, rows), [SMALL] + [NEAR]...  3.46 us
    pallas_call x1, Pallas kernels, on_device(): call(outputs_kernel, [SMALL] + [NEAR] * 8, [((count, D), bf16), ((count,...  2.42 us
    pallas_call x1, Pallas kernels, on_device(): pl.pallas_call(pack_kernel, out_specs=NEAR, out_shape=jax.ShapeDtypeStruc...  1.55 us
  transfers between devices with their start and end apart: 16, of which 11 were waited for; matrix products, arithmetic and copies ran while one was open for 2% of the time, Pallas kernels for 11%

profile of v1, /device:TPU:0, one launch (start us, length us, event | category | flops | bytes accessed | tf_op | source)
XLA Modules:
  0.0 62.4 jit_solution(230109620463877090)
XLA Ops:
  0.6 1.6 %shard_map.170 = bf16[8,2304]{1,0:T(8,128)(2,1)} custom-call(bf16[8,768]{1,0:T(8,128)(2,1)} %w_qkv.3, bf16[8,256]{1,0:T(8,128)(2,1)} %w_attn.1, bf16[8,768]{1,0:T(8,128)(2,1)} %w_in.3, bf16[8,384]{1,0:T(8,128)(2,1)} %bitcast.36, bf16[1,8]{1,0:T(2,128)(2,1)} %bitcast.30, bf16[1,8]{1,0:T(2,128)(2,1)} %bitcast.32), custom_call_target="tpu_custom_call" | custom-call | tf_op jit(solution)/shard_map/pallas_call | solution.py:324
  2.2 4.0 %collective-permute-start = (bf16[1,8,2304]{2,1,0:T(8,128)(2,1)}, bf16[1,8,2304]{2,1,0:T(8,128)(2,1)S(1)}, u32[]{:S(2)}, u32[]{:S(2)}) collective-permute-start(bf16[1,8,2304]{2,1,0:T(8,128)(2,1)} %bitcast.34), channel_id=1, source_target_pairs={{0,16},{1,17},{2,18},{3,19},{4,20},{5,21},{6,22},{7,23},{8,24},{9,... | collective-permute-start | bytes 110600 | tf_op jit(solution)/shard_map/ppermute | solution.py:322
  7.0 1.7 %collective-permute-done = bf16[1,8,2304]{2,1,0:T(8,128)(2,1)S(1)} collective-permute-done((bf16[1,8,2304]{2,1,0:T(8,128)(2,1)}, bf16[1,8,2304]{2,1,0:T(8,128)(2,1)S(1)}, u32[]{:S(2)}, u32[]{:S(2)}) %collective-permute-start) | collective-permute-done | bytes 36896 | tf_op jit(solution)/shard_map/ppermute | solution.py:322
  8.8 1.6 %collective-permute-start.1 = (bf16[2,8,2304]{2,1,0:T(8,128)(2,1)S(1)}, bf16[2,8,2304]{2,1,0:T(8,128)(2,1)S(1)}, u32[]{:S(2)}, u32[]{:S(2)}) collective-permute-start(bf16[2,8,2304]{2,1,0:T(8,128)(2,1)S(1)} %slice.97), channel_id=1, source_target_pairs={{0,8},{1,9},{2,10},{3,11},{4,12},{5,13},{6,14},{7,15},{8,0},{9,1},... | collective-permute-start | bytes 221192 | tf_op jit(solution)/shard_map/ppermute | solution.py:322
  10.4 2.8 %collective-permute-done.1 = bf16[2,8,2304]{2,1,0:T(8,128)(2,1)S(1)} collective-permute-done((bf16[2,8,2304]{2,1,0:T(8,128)(2,1)S(1)}, bf16[2,8,2304]{2,1,0:T(8,128)(2,1)S(1)}, u32[]{:S(2)}, u32[]{:S(2)}) %collective-permute-start.1) | collective-permute-done | bytes 73760 | tf_op jit(solution)/shard_map/ppermute | solution.py:322
  13.3 1.8 %collective-permute-start.2 = (bf16[4,8,1152]{2,1,0:T(8,128)(2,1)S(1)}, bf16[4,8,1152]{2,1,0:T(8,128)(2,1)S(1)}, u32[]{:S(2)}, u32[]{:S(2)}) collective-permute-start(bf16[4,8,1152]{2,1,0:T(8,128)(2,1)S(1)} %get-tuple-element.57), channel_id=1, source_target_pairs={{0,4},{1,5},{2,6},{3,7},{4,0},{5,1},{6,2},{7,3},{8,12},{9,13},{10,... | collective-permute-start | bytes 221192 | tf_op jit(solution)/shard_map/ppermute | solution.py:322
  15.1 1.5 %collective-permute-start.5 = (bf16[4,8,1152]{2,1,0:T(8,128)(2,1)S(1)}, bf16[4,8,1152]{2,1,0:T(8,128)(2,1)S(1)}, u32[]{:S(2)}, u32[]{:S(2)}) collective-permute-start(bf16[4,8,1152]{2,1,0:T(8,128)(2,1)S(1)} %get-tuple-element.56), channel_id=1, source_target_pairs={{0,2},{1,3},{2,0},{3,1},{4,6},{5,7},{6,4},{7,5},{8,10},{9,11},{10,... | collective-permute-start | bytes 221192 | tf_op jit(solution)/shard_map/ppermute | solution.py:322
  16.6 1.1 %collective-permute-done.2 = bf16[4,8,1152]{2,1,0:T(8,128)(2,1)S(1)} collective-permute-done((bf16[4,8,1152]{2,1,0:T(8,128)(2,1)S(1)}, bf16[4,8,1152]{2,1,0:T(8,128)(2,1)S(1)}, u32[]{:S(2)}, u32[]{:S(2)}) %collective-permute-start.2) | collective-permute-done | bytes 73760 | tf_op jit(solution)/shard_map/ppermute | solution.py:322
  17.7 1.8 %collective-permute-start.3 = (bf16[8,8,1152]{2,1,0:T(8,128)(2,1)S(1)}, bf16[8,8,1152]{2,1,0:T(8,128)(2,1)S(1)}, u32[]{:S(2)}, u32[]{:S(2)}) collective-permute-start(bf16[8,8,1152]{2,1,0:T(8,128)(2,1)S(1)} %slice.99), channel_id=1, source_target_pairs={{0,2},{1,3},{2,0},{3,1},{4,6},{5,7},{6,4},{7,5},{8,10},{9,11},{10,... | collective-permute-start | bytes 442376 | tf_op jit(solution)/shard_map/ppermute | solution.py:322
  19.5 2.4 %collective-permute-start.6 = (bf16[8,8,1152]{2,1,0:T(8,128)(2,1)S(1)}, bf16[8,8,1152]{2,1,0:T(8,128)(2,1)S(1)}, u32[]{:S(2)}, u32[]{:S(2)}) collective-permute-start(bf16[8,8,1152]{2,1,0:T(8,128)(2,1)S(1)} %slice.101), channel_id=1, source_target_pairs={{0,4},{1,5},{2,6},{3,7},{4,0},{5,1},{6,2},{7,3},{8,12},{9,13},{10,... | collective-permute-start | bytes 442376 | tf_op jit(solution)/shard_map/ppermute | solution.py:322
  23.0 2.0 %collective-permute-done.6 = bf16[8,8,1152]{2,1,0:T(8,128)(2,1)S(1)} collective-permute-done((bf16[8,8,1152]{2,1,0:T(8,128)(2,1)S(1)}, bf16[8,8,1152]{2,1,0:T(8,128)(2,1)S(1)}, u32[]{:S(2)}, u32[]{:S(2)}) %collective-permute-start.6) | collective-permute-done | bytes 147488 | tf_op jit(solution)/shard_map/ppermute | solution.py:322
  25.2 4.4 %shard_map.171 = (bf16[256,768]{1,0:T(8,128)(2,1)S(1)}, bf16[256,256]{1,0:T(8,128)(2,1)S(1)}, f32[2,256]{1,0:T(2,128)S(1)}, bf16[768,256]{1,0:T(8,128)(2,1)S(1)}...) custom-call(s32[1]{0:T(128)} %bitcast.me, s32[6]{0:T(128)S(1)} %copy-done.6, ...), custom_call_target="tpu_custom_call" | custom-call | tf_op jit(solution)/shard_map/pallas_call | solution.py:342
  29.6 5.1 %shard_map.172 = (bf16[256,384]{1,0:T(8,128)(2,1)S(1)}, f32[768,256]{1,0:T(8,128)S(1)}, bf16[768,384]{1,0:T(8,128)(2,1)S(1)}, f32[768,256]{1,0:T(8,128)S(1)}, bf...) custom-call(s32[1]{0:T(128)} %bitcast.me, s32[6]{0:T(128)S(1)} %copy-done.6, ...), custom_call_target="tpu_custom_call" | custom-call | tf_op jit(solution)/shard_map/pallas_call | solution.py:347
  34.6 3.5 %shard_map.173 = (bf16[256,1024]{1,0:T(8,128)(2,1)S(1)}, bf16[768,768]{1,0:T(8,128)(2,1)S(1)}) custom-call(s32[1]{0:T(128)} %bitcast.me, bf16[768,768]{1,0:T(8,128)(2,1)S(1)} %get-tuple-element.34.heads, f32[768,512]{1,0:T(8,128)S(1)} %get-tuple-element.35.shares, bf16[768,256]{1,0:T(8,128)(2,1)S(1)} %get-tuple-element.38.d_mixture, ...), custom_call_target="tpu_custom_call" | custom-call | tf_op jit(solution)/shard_map/pallas_call | solution.py:353
  39.9 1.2 %collective-permute-start.9 = (bf16[8,8,1024]{2,1,0:T(8,128)(2,1)S(1)}, bf16[8,8,1024]{2,1,0:T(8,128)(2,1)S(1)}, u32[]{:S(2)}, u32[]{:S(2)}) collective-permute-start(bf16[8,8,1024]{2,1,0:T(8,128)(2,1)S(1)} %slice.103), channel_id=1, source_target_pairs={{0,2},{1,3},{2,0},{3,1},{4,6},{5,7},{6,4},{7,5},{8,10},{9,11},{10,... | collective-permute-start | bytes 393224 | tf_op jit(solution)/shard_map/ppermute | solution.py:322
  41.2 2.3 %collective-permute-start.12 = (bf16[8,8,1152]{2,1,0:T(8,128)(2,1)S(1)}, bf16[8,8,1152]{2,1,0:T(8,128)(2,1)S(1)}, u32[]{:S(2)}, u32[]{:S(2)}) collective-permute-start(bf16[8,8,1152]{2,1,0:T(8,128)(2,1)S(1)} %slice.107), channel_id=1, source_target_pairs={{0,4},{1,5},{2,6},{3,7},{4,0},{5,1},{6,2},{7,3},{8,12},{9,13},{10,... | collective-permute-start | bytes 442376 | tf_op jit(solution)/shard_map/ppermute | solution.py:322
  43.5 2.3 %collective-permute-done.9 = bf16[8,8,1024]{2,1,0:T(8,128)(2,1)S(1)} collective-permute-done((bf16[8,8,1024]{2,1,0:T(8,128)(2,1)S(1)}, bf16[8,8,1024]{2,1,0:T(8,128)(2,1)S(1)}, u32[]{:S(2)}, u32[]{:S(2)}) %collective-permute-start.9) | collective-permute-done | bytes 131104 | tf_op jit(solution)/shard_map/ppermute | solution.py:322
  45.8 2.1 %collective-permute-start.10 = (bf16[4,8,1024]{2,1,0:T(8,128)(2,1)S(1)}, bf16[4,8,1024]{2,1,0:T(8,128)(2,1)S(1)}, u32[]{:S(2)}, u32[]{:S(2)}) collective-permute-start(bf16[4,8,1024]{2,1,0:T(8,128)(2,1)S(1)} %slice.105), channel_id=1, source_target_pairs={{0,4},{1,5},{2,6},{3,7},{4,0},{5,1},{6,2},{7,3},{8,12},{9,13},{10,... | collective-permute-start | bytes 196616 | tf_op jit(solution)/shard_map/ppermute | solution.py:322
  48.0 1.2 %collective-permute-start.13 = (bf16[4,8,1152]{2,1,0:T(8,128)(2,1)S(1)}, bf16[4,8,1152]{2,1,0:T(8,128)(2,1)S(1)}, u32[]{:S(2)}, u32[]{:S(2)}) collective-permute-start(bf16[4,8,1152]{2,1,0:T(8,128)(2,1)S(1)} %slice.109), channel_id=1, source_target_pairs={{0,2},{1,3},{2,0},{3,1},{4,6},{5,7},{6,4},{7,5},{8,10},{9,11},{10,... | collective-permute-start | bytes 221192 | tf_op jit(solution)/shard_map/ppermute | solution.py:322
  50.2 2.2 %collective-permute-done.13 = bf16[4,8,1152]{2,1,0:T(8,128)(2,1)S(1)} collective-permute-done((bf16[4,8,1152]{2,1,0:T(8,128)(2,1)S(1)}, bf16[4,8,1152]{2,1,0:T(8,128)(2,1)S(1)}, u32[]{:S(2)}, u32[]{:S(2)}) %collective-permute-start.13) | collective-permute-done | bytes 73760 | tf_op jit(solution)/shard_map/ppermute | solution.py:322
  52.4 1.1 %collective-permute-start.14 = (bf16[2,8,2176]{2,1,0:T(8,128)(2,1)S(1)}, bf16[2,8,2176]{2,1,0:T(8,128)(2,1)S(1)}, u32[]{:S(2)}, u32[]{:S(2)}) collective-permute-start(bf16[2,8,2176]{2,1,0:T(8,128)(2,1)S(1)} %pad_maximum_fusion), channel_id=1, source_target_pairs={{0,8},{1,9},{2,10},{3,11},{4,12},{5,13},{6,14},{7,15},{8,0},{9,1},... | collective-permute-start | bytes 208904 | tf_op jit(solution)/shard_map/ppermute | solution.py:322
  53.5 3.3 %collective-permute-done.14 = bf16[2,8,2176]{2,1,0:T(8,128)(2,1)S(1)} collective-permute-done((bf16[2,8,2176]{2,1,0:T(8,128)(2,1)S(1)}, bf16[2,8,2176]{2,1,0:T(8,128)(2,1)S(1)}, u32[]{:S(2)}, u32[]{:S(2)}) %collective-permute-start.14) | collective-permute-done | bytes 69664 | tf_op jit(solution)/shard_map/ppermute | solution.py:322
  56.8 2.2 %collective-permute-start.15 = (bf16[8,2176]{1,0:T(8,128)(2,1)S(1)}, bf16[8,2176]{1,0:T(8,128)(2,1)S(1)}, u32[]{:S(2)}, u32[]{:S(2)}) collective-permute-start(bf16[8,2176]{1,0:T(8,128)(2,1)S(1)} %get-tuple-element.58), channel_id=1, source_target_pairs={{0,16},{1,17},{2,18},{3,19},{4,20},{5,21},{6,22},{7,23},{8,24},{9,... | collective-permute-start | bytes 104456 | tf_op jit(solution)/shard_map/ppermute | solution.py:322
  59.1 2.4 %shard_map.174 = (bf16[768,256]{1,0:T(8,128)(2,1)}, f32[768,256]{1,0:T(8,128)}) custom-call(s32[6]{0:T(128)S(1)} %copy-done.6, bf16[768,256]{1,0:T(8,128)(2,1)S(1)} %copy-done, bf16[256,768]{1,0:T(8,128)(2,1)S(1)} %get-tuple-element.32.weights, f32[2,256]{1,0:T(2,128)S(1)} %get-tuple-element.33.gains, bf16[768,768]{1,0:T(8,128)(2,1)S(1)} %get-tuple-element.41.d_qkv, ...), custom_call_target="tpu_custom_call" | custom-call | tf_op jit(solution)/shard_map/pallas_call | solution.py:358
  (60 shorter events, 6.1 us)
Async XLA Ops:
  2.2 6.6 %collective-permute-start = (bf16[1,8,2304]{2,1,0:T(8,128)(2,1)}, bf16[1,8,2304]{2,1,0:T(8,128)(2,1)S(1)}, u32[]{:S(2)}, u32[]{:S(2)}) collective-permute-start(bf16[1,8,2304]{2,1,0:T(8,128)(2,1)} %bitcast.34), channel_id=1, source_target_pairs={{0,16},{1,17},{2,18},{3,19},{4,20},{5,21},{6,22},{7,23},{8,24},{9,... | collective-permute-start | bytes 110600 | tf_op jit(solution)/shard_map/ppermute | solution.py:322
  8.8 4.4 %collective-permute-start.1 = (bf16[2,8,2304]{2,1,0:T(8,128)(2,1)S(1)}, bf16[2,8,2304]{2,1,0:T(8,128)(2,1)S(1)}, u32[]{:S(2)}, u32[]{:S(2)}) collective-permute-start(bf16[2,8,2304]{2,1,0:T(8,128)(2,1)S(1)} %slice.97), channel_id=1, source_target_pairs={{0,8},{1,9},{2,10},{3,11},{4,12},{5,13},{6,14},{7,15},{8,0},{9,1},... | collective-permute-start | bytes 221192 | tf_op jit(solution)/shard_map/ppermute | solution.py:322
  13.2 11.9 %copy-start = (bf16[768,256]{1,0:T(8,128)(2,1)S(1)}, bf16[768,256]{1,0:T(8,128)(2,1)}, u32[]{:S(2)}) copy-start(bf16[768,256]{1,0:T(8,128)(2,1)} %tokens.5) | copy-start | bytes 1179652
  13.2 11.9 %copy-start.1 = (f32[256,128]{1,0:T(8,128)S(1)}, f32[256,128]{1,0:T(8,128)}, u32[]{:S(2)}) copy-start(f32[256,128]{1,0:T(8,128)} %constant.7.clone.sin) | copy-start | bytes 393220
  13.2 11.9 %copy-start.2 = (f32[256,128]{1,0:T(8,128)S(1)}, f32[256,128]{1,0:T(8,128)}, u32[]{:S(2)}) copy-start(f32[256,128]{1,0:T(8,128)} %constant.6.clone.cos) | copy-start | bytes 393220
  13.3 11.9 %copy-start.6 = (s32[6]{0:T(128)S(1)}, s32[6]{0:T(128)}, u32[]{:S(2)}) copy-start(s32[6]{0:T(128)} %lengths.5) | copy-start | bytes 76
  13.3 4.4 %collective-permute-start.2 = (bf16[4,8,1152]{2,1,0:T(8,128)(2,1)S(1)}, bf16[4,8,1152]{2,1,0:T(8,128)(2,1)S(1)}, u32[]{:S(2)}, u32[]{:S(2)}) collective-permute-start(bf16[4,8,1152]{2,1,0:T(8,128)(2,1)S(1)} %get-tuple-element.57), channel_id=1, source_target_pairs={{0,4},{1,5},{2,6},{3,7},{4,0},{5,1},{6,2},{7,3},{8,12},{9,13},{10,... | collective-permute-start | bytes 221192 | tf_op jit(solution)/shard_map/ppermute | solution.py:322
  15.1 4.4 %collective-permute-start.5 = (bf16[4,8,1152]{2,1,0:T(8,128)(2,1)S(1)}, bf16[4,8,1152]{2,1,0:T(8,128)(2,1)S(1)}, u32[]{:S(2)}, u32[]{:S(2)}) collective-permute-start(bf16[4,8,1152]{2,1,0:T(8,128)(2,1)S(1)} %get-tuple-element.56), channel_id=1, source_target_pairs={{0,2},{1,3},{2,0},{3,1},{4,6},{5,7},{6,4},{7,5},{8,10},{9,11},{10,... | collective-permute-start | bytes 221192 | tf_op jit(solution)/shard_map/ppermute | solution.py:322
  17.7 11.8 %copy-start.3 = (bf16[768,256]{1,0:T(8,128)(2,1)S(1)}, bf16[768,256]{1,0:T(8,128)(2,1)}, u32[]{:S(2)}) copy-start(bf16[768,256]{1,0:T(8,128)(2,1)} %cot.1) | copy-start | bytes 1179652
  17.7 5.2 %collective-permute-start.3 = (bf16[8,8,1152]{2,1,0:T(8,128)(2,1)S(1)}, bf16[8,8,1152]{2,1,0:T(8,128)(2,1)S(1)}, u32[]{:S(2)}, u32[]{:S(2)}) collective-permute-start(bf16[8,8,1152]{2,1,0:T(8,128)(2,1)S(1)} %slice.99), channel_id=1, source_target_pairs={{0,2},{1,3},{2,0},{3,1},{4,6},{5,7},{6,4},{7,5},{8,10},{9,11},{10,... | collective-permute-start | bytes 442376 | tf_op jit(solution)/shard_map/ppermute | solution.py:322
  19.5 5.5 %collective-permute-start.6 = (bf16[8,8,1152]{2,1,0:T(8,128)(2,1)S(1)}, bf16[8,8,1152]{2,1,0:T(8,128)(2,1)S(1)}, u32[]{:S(2)}, u32[]{:S(2)}) collective-permute-start(bf16[8,8,1152]{2,1,0:T(8,128)(2,1)S(1)} %slice.101), channel_id=1, source_target_pairs={{0,4},{1,5},{2,6},{3,7},{4,0},{5,1},{6,2},{7,3},{8,12},{9,13},{10,... | collective-permute-start | bytes 442376 | tf_op jit(solution)/shard_map/ppermute | solution.py:322
  23.0 2.2 %collective-permute-start.4 = (bf16[16,8,1152]{2,1,0:T(8,128)(2,1)S(1)}, bf16[16,8,1152]{2,1,0:T(8,128)(2,1)S(1)}, u32[]{:S(2)}, u32[]{:S(2)}) collective-permute-start(bf16[16,8,1152]{2,1,0:T(8,128)(2,1)S(1)} %constant_dynamic-update-slice_fusion.2), channel_id=1, source_target_pairs={{0,1},{1,0},{2,3},{3,2},{4,5},{5,4},{6,7},{7,6},{8,9},{9,8},{10,11... | collective-permute-start | bytes 884744 | tf_op jit(solution)/shard_map/ppermute | solution.py:322
  25.1 4.5 %collective-permute-start.7 = (bf16[16,8,1152]{2,1,0:T(8,128)(2,1)S(1)}, bf16[16,8,1152]{2,1,0:T(8,128)(2,1)S(1)}, u32[]{:S(2)}, u32[]{:S(2)}) collective-permute-start(bf16[16,8,1152]{2,1,0:T(8,128)(2,1)S(1)} %constant_dynamic-update-slice_fusion), channel_id=1, source_target_pairs={{0,1},{1,0},{2,3},{3,2},{4,5},{5,4},{6,7},{7,6},{8,9},{9,8},{10,11... | collective-permute-start | bytes 884744 | tf_op jit(solution)/shard_map/ppermute | solution.py:322
  38.1 1.7 %collective-permute-start.8 = (bf16[16,8,1024]{2,1,0:T(8,128)(2,1)S(1)}, bf16[16,8,1024]{2,1,0:T(8,128)(2,1)S(1)}, u32[]{:S(2)}, u32[]{:S(2)}) collective-permute-start(bf16[16,8,1024]{2,1,0:T(8,128)(2,1)S(1)} %slice_bitcast_fusion.1), channel_id=1, source_target_pairs={{0,1},{1,0},{2,3},{3,2},{4,5},{5,4},{6,7},{7,6},{8,9},{9,8},{10,11... | collective-permute-start | bytes 786440 | tf_op jit(solution)/shard_map/ppermute | solution.py:322
  38.7 2.4 %collective-permute-start.11 = (bf16[16,8,1152]{2,1,0:T(8,128)(2,1)S(1)}, bf16[16,8,1152]{2,1,0:T(8,128)(2,1)S(1)}, u32[]{:S(2)}, u32[]{:S(2)}) collective-permute-start(bf16[16,8,1152]{2,1,0:T(8,128)(2,1)S(1)} %slice_bitcast_fusion), channel_id=1, source_target_pairs={{0,1},{1,0},{2,3},{3,2},{4,5},{5,4},{6,7},{7,6},{8,9},{9,8},{10,11... | collective-permute-start | bytes 884744 | tf_op jit(solution)/shard_map/ppermute | solution.py:322
  39.9 5.8 %collective-permute-start.9 = (bf16[8,8,1024]{2,1,0:T(8,128)(2,1)S(1)}, bf16[8,8,1024]{2,1,0:T(8,128)(2,1)S(1)}, u32[]{:S(2)}, u32[]{:S(2)}) collective-permute-start(bf16[8,8,1024]{2,1,0:T(8,128)(2,1)S(1)} %slice.103), channel_id=1, source_target_pairs={{0,2},{1,3},{2,0},{3,1},{4,6},{5,7},{6,4},{7,5},{8,10},{9,11},{10,... | collective-permute-start | bytes 393224 | tf_op jit(solution)/shard_map/ppermute | solution.py:322
  41.2 6.7 %collective-permute-start.12 = (bf16[8,8,1152]{2,1,0:T(8,128)(2,1)S(1)}, bf16[8,8,1152]{2,1,0:T(8,128)(2,1)S(1)}, u32[]{:S(2)}, u32[]{:S(2)}) collective-permute-start(bf16[8,8,1152]{2,1,0:T(8,128)(2,1)S(1)} %slice.107), channel_id=1, source_target_pairs={{0,4},{1,5},{2,6},{3,7},{4,0},{5,1},{6,2},{7,3},{8,12},{9,13},{10,... | collective-permute-start | bytes 442376 | tf_op jit(solution)/shard_map/ppermute | solution.py:322
  45.8 4.3 %collective-permute-start.10 = (bf16[4,8,1024]{2,1,0:T(8,128)(2,1)S(1)}, bf16[4,8,1024]{2,1,0:T(8,128)(2,1)S(1)}, u32[]{:S(2)}, u32[]{:S(2)}) collective-permute-start(bf16[4,8,1024]{2,1,0:T(8,128)(2,1)S(1)} %slice.105), channel_id=1, source_target_pairs={{0,4},{1,5},{2,6},{3,7},{4,0},{5,1},{6,2},{7,3},{8,12},{9,13},{10,... | collective-permute-start | bytes 196616 | tf_op jit(solution)/shard_map/ppermute | solution.py:322
  48.0 4.4 %collective-permute-start.13 = (bf16[4,8,1152]{2,1,0:T(8,128)(2,1)S(1)}, bf16[4,8,1152]{2,1,0:T(8,128)(2,1)S(1)}, u32[]{:S(2)}, u32[]{:S(2)}) collective-permute-start(bf16[4,8,1152]{2,1,0:T(8,128)(2,1)S(1)} %slice.109), channel_id=1, source_target_pairs={{0,2},{1,3},{2,0},{3,1},{4,6},{5,7},{6,4},{7,5},{8,10},{9,11},{10,... | collective-permute-start | bytes 221192 | tf_op jit(solution)/shard_map/ppermute | solution.py:322
  52.4 4.4 %collective-permute-start.14 = (bf16[2,8,2176]{2,1,0:T(8,128)(2,1)S(1)}, bf16[2,8,2176]{2,1,0:T(8,128)(2,1)S(1)}, u32[]{:S(2)}, u32[]{:S(2)}) collective-permute-start(bf16[2,8,2176]{2,1,0:T(8,128)(2,1)S(1)} %pad_maximum_fusion), channel_id=1, source_target_pairs={{0,8},{1,9},{2,10},{3,11},{4,12},{5,13},{6,14},{7,15},{8,0},{9,1},... | collective-permute-start | bytes 208904 | tf_op jit(solution)/shard_map/ppermute | solution.py:322
  56.8 4.9 %collective-permute-start.15 = (bf16[8,2176]{1,0:T(8,128)(2,1)S(1)}, bf16[8,2176]{1,0:T(8,128)(2,1)S(1)}, u32[]{:S(2)}, u32[]{:S(2)}) collective-permute-start(bf16[8,2176]{1,0:T(8,128)(2,1)S(1)} %get-tuple-element.58), channel_id=1, source_target_pairs={{0,16},{1,17},{2,18},{3,19},{4,20},{5,21},{6,22},{7,23},{8,24},{9,... | collective-permute-start | bytes 104456 | tf_op jit(solution)/shard_map/ppermute | solution.py:322
  59.1 2.7 %copy-start.5 = (bf16[8,768]{1,0:T(8,128)(2,1)S(1)}, bf16[8,768]{1,0:T(8,128)(2,1)}, u32[]{:S(2)}) copy-start(bf16[8,768]{1,0:T(8,128)(2,1)} %w_in.3) | copy-start | bytes 36868
  59.1 2.7 %copy-start.7 = (bf16[8]{0:T(256)(128)(2,1)S(1)}, bf16[8]{0:T(256)(128)(2,1)}, u32[]{:S(2)}) copy-start(bf16[8]{0:T(256)(128)(2,1)} %param.17) | copy-start | bytes 52
  59.1 2.7 %copy-start.8 = (bf16[8]{0:T(256)(128)(2,1)S(1)}, bf16[8]{0:T(256)(128)(2,1)}, u32[]{:S(2)}) copy-start(bf16[8]{0:T(256)(128)(2,1)} %param.18) | copy-start | bytes 52
  (1 other events, 2.7 us)

commit v2 on v1

--- a/solution.py
+++ b/solution.py
@@ -13,7 +13,6 @@
 HEADS = 4
 HEAD_DIM = 64
 BLOCK = 128
-BLOCKS = 2
 HALF = D // 2
 WIDE = HEADS * BLOCK
 QKV = 3 * D
@@ -32,7 +31,7 @@
     half_dim = HEAD_DIM // 2
     frequency = rope_base ** (-(np.arange(half_dim) * 2.0) / HEAD_DIM)
     angles = np.arange(BLOCK)[:, None] * frequency[None, :]
-    angles = np.tile(angles, (BLOCKS, HEADS))
+    angles = np.tile(angles, (1, HEADS))
     return np.cos(angles).astype(np.float32), np.sin(angles).astype(np.float32)
 
 
@@ -134,18 +133,9 @@
     return spread, plain
 
 
-def chunks(total):
-    cap = BLOCKS * BLOCK
-    return [(i, slice(i * cap, (i + 1) * cap)) for i in range(total // cap)]
-
-
-def block_slices(start):
-    return [slice(start + b * BLOCK, start + (b + 1) * BLOCK) for b in range(BLOCKS)]
-
-
-def live_rows(lengths, index):
+def live_rows(lengths, count):
     row = lax.broadcasted_iota(jnp.int32, (BLOCK, 1), 0)
-    live = [jnp.where(row < lengths[index * BLOCKS + b], 1.0, 0.0) for b in range(BLOCKS)]
+    live = [jnp.where(row < lengths[b], 1.0, 0.0) for b in range(count // BLOCK)]
     return jnp.concatenate(live, axis=0) > 0.5
 
 
@@ -162,32 +152,35 @@
         gains[k : k + 1, :] = jnp.sum(jnp.where(here, column, 0.0), axis=0, keepdims=True)
     gain = gains[0:1, :]
     w_qkv = weights[...]
-    c = cos[...]
-    s = sin[...]
+    c, s = cos[...], sin[...]
     spread_masks, plain_masks = head_masks()
     key_lane = lax.broadcasted_iota(jnp.int32, (1, BLOCK), 1)
-    for index, part in chunks(tokens.shape[0]):
-        low = (standardize(tokens[part].astype(f32))[0] * gain).astype(bf16)
-        normed[part] = low
-        qkv = mm(low, w_qkv)
-
-        def rope(base):
-            low, high = qkv[:, base : base + HALF], qkv[:, base + HALF : base + D]
-            return jnp.concatenate([low * c - high * s, high * c + low * s], axis=1)
-
-        heads[part, :D] = (rope(0) * HEAD_DIM ** (-0.5)).astype(bf16)
-        heads[part, D : 2 * D] = rope(D).astype(bf16)
-        heads[part, 2 * D :] = qkv[:, 2 * D :].astype(bf16)
-        for b, block in enumerate(block_slices(part.start)):
-            live = key_lane < lengths[index * BLOCKS + b]
-            scores = mm_nt(heads[block, :D], stack_heads(heads[block, D : 2 * D], spread_masks))
-            for h in range(HEADS):
-                cut = slice(h * BLOCK, (h + 1) * BLOCK)
-                one = jnp.where(live, scores[:, cut], -1e30)
-                grown = jnp.exp(one - jnp.max(one, axis=1, keepdims=True))
-                shares[block, cut] = grown * (1.0 / jnp.sum(grown, axis=1, keepdims=True))
-            mixed = mm(shares[block].astype(bf16), stack_heads(heads[block, 2 * D :], plain_masks))
-            mixture[block] = mixed.astype(bf16)
+    count = tokens.shape[0] // BLOCK
+    for part in [slice(b * BLOCK, (b + 1) * BLOCK) for b in range(count)]:
+        normed[part] = (standardize(tokens[part].astype(f32))[0] * gain).astype(bf16)
+
+    def rope(base):
+        both = mm(normed[...], w_qkv[:, base : base + D])
+        low, high = both[:, :HALF].reshape(count, BLOCK, HALF), both[:, HALF:].reshape(count, BLOCK, HALF)
+        both = jnp.concatenate([low * c - high * s, high * c + low * s], axis=2)
+        return both.reshape(count * BLOCK, D)
+
+    heads[:, :D] = (rope(0) * HEAD_DIM ** (-0.5)).astype(bf16)
+    heads[:, D : 2 * D] = rope(D).astype(bf16)
+    heads[:, 2 * D :] = mm(normed[...], w_qkv[:, 2 * D :]).astype(bf16)
+    parts = [slice(b * BLOCK, (b + 1) * BLOCK) for b in range(count)]
+    for block in parts:
+        shares[block] = mm_nt(heads[block, :D], stack_heads(heads[block, D : 2 * D], spread_masks))
+    for b, block in enumerate(parts):
+        live = key_lane < lengths[b]
+        for h in range(HEADS):
+            cut = slice(h * BLOCK, (h + 1) * BLOCK)
+            one = jnp.where(live, shares[block, cut], -1e30)
+            grown = jnp.exp(one - jnp.max(one, axis=1, keepdims=True))
+            shares[block, cut] = grown * (1.0 / jnp.sum(grown, axis=1, keepdims=True))
+    for block in parts:
+        mixed = mm(shares[block].astype(bf16), stack_heads(heads[block, 2 * D :], plain_masks))
+        mixture[block] = mixed.astype(bf16)
 
 
 def feed_kernel(
@@ -201,29 +194,27 @@
     w_in = ordered[:, : 2 * FF]
     w_mlp[...] = ordered[:, 2 * FF :]
     gain = gains[1:2, :]
-    for index, part in chunks(tokens.shape[0]):
-        mid = tokens[part].astype(f32) + mm(mixture[part], w_attn)
-        middle[part] = mid
-        hat_two, inv_two = standardize(mid)
-        low = (hat_two * gain).astype(bf16)
-        hat_two_low[part] = low
-        merged = mm(low, w_in)
-        inner = merged[:, :FF]
-        gate = merged[:, FF:]
-        cdf = 0.5 * (1.0 + lax.erf(inner * 0.7071067811865476))
-        curved = inner * cdf
-        slope = cdf + inner * jnp.exp(-0.5 * inner * inner) * 0.3989422804014327
-        hidden[part] = (curved * gate).astype(bf16)
-        out_grad = jnp.where(live_rows(lengths, index), cot[part].astype(f32), 0.0)
-        out_low[part] = out_grad.astype(bf16)
-        d_hidden = mm(out_low[part], w_mlp[...])
-        d_merged[part, :FF] = (d_hidden * gate * slope).astype(bf16)
-        d_merged[part, FF:] = (d_hidden * curved).astype(bf16)
-        d_normed = mm_nt(d_merged[part], w_in)
-        d_mid = out_grad + norm_back(d_normed * gain, hat_two, inv_two)
-        d_middle[part] = d_mid
-        d_att[part] = d_mid.astype(bf16)
-        d_mixture[part] = mm_nt(d_att[part], w_attn).astype(bf16)
+    mid = tokens[...].astype(f32) + mm(mixture[...], w_attn)
+    middle[...] = mid
+    hat_two, inv_two = standardize(mid)
+    hat_two_low[...] = (hat_two * gain).astype(bf16)
+    merged = mm(hat_two_low[...], w_in)
+    inner = merged[:, :FF]
+    gate = merged[:, FF:]
+    cdf = 0.5 * (1.0 + lax.erf(inner * 0.7071067811865476))
+    curved = inner * cdf
+    slope = cdf + inner * jnp.exp(-0.5 * inner * inner) * 0.3989422804014327
+    hidden[...] = (curved * gate).astype(bf16)
+    out_grad = jnp.where(live_rows(lengths, tokens.shape[0]), cot[...].astype(f32), 0.0)
+    out_low[...] = out_grad.astype(bf16)
+    d_hidden = mm(out_low[...], w_mlp[...])
+    d_merged[:, :FF] = (d_hidden * gate * slope).astype(bf16)
+    d_merged[:, FF:] = (d_hidden * curved).astype(bf16)
+    d_normed = mm_nt(d_merged[...], w_in)
+    d_mid = out_grad + norm_back(d_normed * gain, hat_two, inv_two)
+    d_middle[...] = d_mid
+    d_att[...] = d_mid.astype(bf16)
+    d_mixture[...] = mm_nt(d_att[...], w_attn).astype(bf16)
     order = slot_order(hops, rows, me[0], 0)
     total = mm_tn(hat_two_low[...], d_merged[...]).astype(bf16)
     sums[:, : 2 * FF] = mm(order, total).astype(bf16)
@@ -235,34 +226,31 @@
 def attend_back_kernel(
     hops, rows, me, heads, shares, d_mixture, normed, g_attn, cos, sin, sums, d_qkv
 ):
-    c = cos[...]
-    s = sin[...]
+    c, s = cos[...], sin[...]
     spread_masks, plain_masks = head_masks()
 
     def rope_back(grads):
         low, high = grads[:, :HALF], grads[:, HALF:]
         return jnp.concatenate([low * c + high * s, high * c - low * s], axis=1).astype(bf16)
 
-    for index, part in chunks(heads.shape[0]):
-        d_queries = []
-        d_keys = []
-        for block in block_slices(part.start):
-            queries, key_rows, value_rows = heads[block, :D], heads[block, D : 2 * D], heads[block, 2 * D :]
-            d_mixed = d_mixture[block]
-            d_shares = mm_nt(d_mixed, stack_heads(value_rows, plain_masks))
-            d_scores = []
-            for h in range(HEADS):
-                cut = slice(h * BLOCK, (h + 1) * BLOCK)
-                one, d_one = shares[block, cut], d_shares[:, cut]
-                d_one = one * (d_one - jnp.sum(one * d_one, axis=1, keepdims=True))
-                d_scores.append(d_one.astype(bf16))
-            d_scores = jnp.concatenate(d_scores, axis=1)
-            d_queries.append(mm(d_scores, stack_heads(key_rows, spread_masks)))
-            d_keys.append(mm(turn_heads(d_scores), stack_heads(queries, spread_masks)))
-            d_values = mm(turn_heads(shares[block].astype(bf16)), stack_heads(d_mixed, plain_masks))
-            d_qkv[block, 2 * D :] = d_values.astype(bf16)
-        d_qkv[part, :D] = rope_back(jnp.concatenate(d_queries, axis=0) * HEAD_DIM ** (-0.5))
-        d_qkv[part, D : 2 * D] = rope_back(jnp.concatenate(d_keys, axis=0))
+    parts = [slice(b * BLOCK, (b + 1) * BLOCK) for b in range(heads.shape[0] // BLOCK)]
+    d_shares = [mm_nt(d_mixture[block], stack_heads(heads[block, 2 * D :], plain_masks)) for block in parts]
+    d_values = [mm(turn_heads(shares[block].astype(bf16)), stack_heads(d_mixture[block], plain_masks)) for block in parts]
+    for block, d_value in zip(parts, d_values):
+        d_qkv[block, 2 * D :] = d_value.astype(bf16)
+    d_scores = []
+    for block, d_share in zip(parts, d_shares):
+        pieces = []
+        for h in range(HEADS):
+            cut = slice(h * BLOCK, (h + 1) * BLOCK)
+            one, d_one = shares[block, cut], d_share[:, cut]
+            d_one = one * (d_one - jnp.sum(one * d_one, axis=1, keepdims=True))
+            pieces.append(d_one.astype(bf16))
+        d_scores.append(jnp.concatenate(pieces, axis=1))
+    for block, d_score in zip(parts, d_scores):
+        d_qkv[block, :D] = rope_back(mm(d_score, stack_heads(heads[block, D : 2 * D], spread_masks)) * HEAD_DIM ** (-0.5))
+    for block, d_score in zip(parts, d_scores):
+        d_qkv[block, D : 2 * D] = rope_back(mm(turn_heads(d_score), stack_heads(heads[block, :D], spread_masks)))
     order = slot_order(hops, rows, me[0], 0)
     total = mm_tn(normed[...], d_qkv[...]).astype(bf16)
     placed = mm(order, total).astype(bf16)
@@ -275,12 +263,11 @@
 
 def outputs_kernel(lengths, tokens, weights, gains, d_qkv, d_middle, middle, hidden, w_mlp, out, grad):
     gain = gains[0:1, :]
-    for index, part in chunks(tokens.shape[0]):
-        result = middle[part] + mm_nt(hidden[part], w_mlp[...])
-        out[part] = jnp.where(live_rows(lengths, index), result, 0.0).astype(bf16)
-        hat_one, inv_one = standardize(tokens[part].astype(f32))
-        d_normed = mm_nt(d_qkv[part], weights[...])
-        grad[part] = d_middle[part] + norm_back(d_normed * gain, hat_one, inv_one)
+    result = middle[...] + mm_nt(hidden[...], w_mlp[...])
+    out[...] = jnp.where(live_rows(lengths, tokens.shape[0]), result, 0.0).astype(bf16)
+    hat_one, inv_one = standardize(tokens[...].astype(f32))
+    d_normed = mm_nt(d_qkv[...], weights[...])
+    grad[...] = d_middle[...] + norm_back(d_normed * gain, hat_one, inv_one)
 
 
 SMALL = pl.BlockSpec(memory_space=pltpu.SMEM)

time: 62.6 us -> 59.1 us (0.944)
  Pallas kernels: 17.5 us -> 14 us
    pallas_call x1, Pallas kernels: 4.36 us -> 2.78 us  [on_device(): call(functools.partial(attend_kernel, hops, rows), [SMALL] * 2 + [NEAR] *...]
    pallas_call x1, Pallas kernels: 3.46 us -> 2.43 us  [on_device(): call(functools.partial(attend_back_kernel, hops, rows), [SMALL] + [NEAR]...]
    pallas_call x1, Pallas kernels: 5.07 us -> 4.15 us  [on_device(): call(functools.partial(feed_kernel, swapped, rows), [SMALL] * 2 + [NEAR]...]
  transfers between devices with their start and end apart: 16 -> 16, of which waited for: 11 -> 11; matrix products, arithmetic and copies ran while one was open for 2% -> 2% of each run, Pallas kernels for 11% -> 9%
where the time goes in v2:
time: 59.1 us; the launch traced here: 58.9 us
  starting transfers between devices  23.9 us (40%)
  waiting for transfers between devices  18.6 us (31%)
  Pallas kernels  14 us (24%)
  local copies, waits for them, and re-layouts  1.11 us (2%)
  between operations  0.92 us (2%)
    ppermute x16, starting transfers between devices, trade(): return lax.ppermute(values, 'dp', [(i, i ^ mask) for i in range(n)])  23.9 us
    ppermute x16, waiting for transfers between devices, trade(): return lax.ppermute(values, 'dp', [(i, i ^ mask) for i in range(n)])  18.6 us
    pallas_call x1, Pallas kernels, on_device(): call(functools.partial(feed_kernel, swapped, rows), [SMALL] * 2 + [NEAR]...  4.15 us
    pallas_call x1, Pallas kernels, on_device(): call(functools.partial(attend_kernel, hops, rows), [SMALL] * 2 + [NEAR] *...  2.78 us
    pallas_call x1, Pallas kernels, on_device(): call(outputs_kernel, [SMALL] + [NEAR] * 8, [((count, D), bf16), ((count,...  2.43 us
    pallas_call x1, Pallas kernels, on_device(): call(functools.partial(attend_back_kernel, hops, rows), [SMALL] + [NEAR]...  2.43 us
    pallas_call x1, Pallas kernels, on_device(): pl.pallas_call(pack_kernel, out_specs=NEAR, out_shape=jax.ShapeDtypeStruc...  1.55 us
  transfers between devices with their start and end apart: 16, of which 11 were waited for; matrix products, arithmetic and copies ran while one was open for 2% of the time, Pallas kernels for 9%

profile of v2, /device:TPU:0, one launch (start us, length us, event | category | flops | bytes accessed | tf_op | source)
XLA Modules:
  0.0 58.9 jit_solution(13560402244436895890)
XLA Ops:
  0.6 1.6 %shard_map.170 = bf16[8,2304]{1,0:T(8,128)(2,1)} custom-call(bf16[8,768]{1,0:T(8,128)(2,1)} %w_qkv.3, bf16[8,256]{1,0:T(8,128)(2,1)} %w_attn.1, bf16[8,768]{1,0:T(8,128)(2,1)} %w_in.3, bf16[8,384]{1,0:T(8,128)(2,1)} %bitcast.36, bf16[1,8]{1,0:T(2,128)(2,1)} %bitcast.30, bf16[1,8]{1,0:T(2,128)(2,1)} %bitcast.32), custom_call_target="tpu_custom_call" | custom-call | tf_op jit(solution)/shard_map/pallas_call | solution.py:311
  2.2 4.0 %collective-permute-start = (bf16[1,8,2304]{2,1,0:T(8,128)(2,1)}, bf16[1,8,2304]{2,1,0:T(8,128)(2,1)S(1)}, u32[]{:S(2)}, u32[]{:S(2)}) collective-permute-start(bf16[1,8,2304]{2,1,0:T(8,128)(2,1)} %bitcast.34), channel_id=1, source_target_pairs={{0,16},{1,17},{2,18},{3,19},{4,20},{5,21},{6,22},{7,23},{8,24},{9,... | collective-permute-start | bytes 110600 | tf_op jit(solution)/shard_map/ppermute | solution.py:309
  7.0 1.7 %collective-permute-done = bf16[1,8,2304]{2,1,0:T(8,128)(2,1)S(1)} collective-permute-done((bf16[1,8,2304]{2,1,0:T(8,128)(2,1)}, bf16[1,8,2304]{2,1,0:T(8,128)(2,1)S(1)}, u32[]{:S(2)}, u32[]{:S(2)}) %collective-permute-start) | collective-permute-done | bytes 36896 | tf_op jit(solution)/shard_map/ppermute | solution.py:309
  8.8 1.6 %collective-permute-start.1 = (bf16[2,8,2304]{2,1,0:T(8,128)(2,1)S(1)}, bf16[2,8,2304]{2,1,0:T(8,128)(2,1)S(1)}, u32[]{:S(2)}, u32[]{:S(2)}) collective-permute-start(bf16[2,8,2304]{2,1,0:T(8,128)(2,1)S(1)} %slice.97), channel_id=1, source_target_pairs={{0,8},{1,9},{2,10},{3,11},{4,12},{5,13},{6,14},{7,15},{8,0},{9,1},... | collective-permute-start | bytes 221192 | tf_op jit(solution)/shard_map/ppermute | solution.py:309
  10.4 2.8 %collective-permute-done.1 = bf16[2,8,2304]{2,1,0:T(8,128)(2,1)S(1)} collective-permute-done((bf16[2,8,2304]{2,1,0:T(8,128)(2,1)S(1)}, bf16[2,8,2304]{2,1,0:T(8,128)(2,1)S(1)}, u32[]{:S(2)}, u32[]{:S(2)}) %collective-permute-start.1) | collective-permute-done | bytes 73760 | tf_op jit(solution)/shard_map/ppermute | solution.py:309
  13.3 1.8 %collective-permute-start.2 = (bf16[4,8,1152]{2,1,0:T(8,128)(2,1)S(1)}, bf16[4,8,1152]{2,1,0:T(8,128)(2,1)S(1)}, u32[]{:S(2)}, u32[]{:S(2)}) collective-permute-start(bf16[4,8,1152]{2,1,0:T(8,128)(2,1)S(1)} %get-tuple-element.57), channel_id=1, source_target_pairs={{0,4},{1,5},{2,6},{3,7},{4,0},{5,1},{6,2},{7,3},{8,12},{9,13},{10,... | collective-permute-start | bytes 221192 | tf_op jit(solution)/shard_map/ppermute | solution.py:309
  15.1 1.5 %collective-permute-start.5 = (bf16[4,8,1152]{2,1,0:T(8,128)(2,1)S(1)}, bf16[4,8,1152]{2,1,0:T(8,128)(2,1)S(1)}, u32[]{:S(2)}, u32[]{:S(2)}) collective-permute-start(bf16[4,8,1152]{2,1,0:T(8,128)(2,1)S(1)} %get-tuple-element.56), channel_id=1, source_target_pairs={{0,2},{1,3},{2,0},{3,1},{4,6},{5,7},{6,4},{7,5},{8,10},{9,11},{10,... | collective-permute-start | bytes 221192 | tf_op jit(solution)/shard_map/ppermute | solution.py:309
  16.6 1.1 %collective-permute-done.2 = bf16[4,8,1152]{2,1,0:T(8,128)(2,1)S(1)} collective-permute-done((bf16[4,8,1152]{2,1,0:T(8,128)(2,1)S(1)}, bf16[4,8,1152]{2,1,0:T(8,128)(2,1)S(1)}, u32[]{:S(2)}, u32[]{:S(2)}) %collective-permute-start.2) | collective-permute-done | bytes 73760 | tf_op jit(solution)/shard_map/ppermute | solution.py:309
  17.7 1.8 %collective-permute-start.3 = (bf16[8,8,1152]{2,1,0:T(8,128)(2,1)S(1)}, bf16[8,8,1152]{2,1,0:T(8,128)(2,1)S(1)}, u32[]{:S(2)}, u32[]{:S(2)}) collective-permute-start(bf16[8,8,1152]{2,1,0:T(8,128)(2,1)S(1)} %slice.99), channel_id=1, source_target_pairs={{0,2},{1,3},{2,0},{3,1},{4,6},{5,7},{6,4},{7,5},{8,10},{9,11},{10,... | collective-permute-start | bytes 442376 | tf_op jit(solution)/shard_map/ppermute | solution.py:309
  19.5 2.4 %collective-permute-start.6 = (bf16[8,8,1152]{2,1,0:T(8,128)(2,1)S(1)}, bf16[8,8,1152]{2,1,0:T(8,128)(2,1)S(1)}, u32[]{:S(2)}, u32[]{:S(2)}) collective-permute-start(bf16[8,8,1152]{2,1,0:T(8,128)(2,1)S(1)} %slice.101), channel_id=1, source_target_pairs={{0,4},{1,5},{2,6},{3,7},{4,0},{5,1},{6,2},{7,3},{8,12},{9,13},{10,... | collective-permute-start | bytes 442376 | tf_op jit(solution)/shard_map/ppermute | solution.py:309
  23.0 2.0 %collective-permute-done.6 = bf16[8,8,1152]{2,1,0:T(8,128)(2,1)S(1)} collective-permute-done((bf16[8,8,1152]{2,1,0:T(8,128)(2,1)S(1)}, bf16[8,8,1152]{2,1,0:T(8,128)(2,1)S(1)}, u32[]{:S(2)}, u32[]{:S(2)}) %collective-permute-start.6) | collective-permute-done | bytes 147488 | tf_op jit(solution)/shard_map/ppermute | solution.py:309
  25.2 2.8 %shard_map.171 = (bf16[256,768]{1,0:T(8,128)(2,1)S(1)}, bf16[256,256]{1,0:T(8,128)(2,1)S(1)}, f32[2,256]{1,0:T(2,128)S(1)}, bf16[768,256]{1,0:T(8,128)(2,1)S(1)}...) custom-call(s32[1]{0:T(128)} %bitcast.me, s32[6]{0:T(128)S(1)} %copy-done.6, ...), custom_call_target="tpu_custom_call" | custom-call | tf_op jit(solution)/shard_map/pallas_call | solution.py:329
  28.0 4.2 %shard_map.172 = (bf16[256,384]{1,0:T(8,128)(2,1)S(1)}, f32[768,256]{1,0:T(8,128)S(1)}, bf16[768,384]{1,0:T(8,128)(2,1)S(1)}, f32[768,256]{1,0:T(8,128)S(1)}, bf...) custom-call(s32[1]{0:T(128)} %bitcast.me, s32[6]{0:T(128)S(1)} %copy-done.6, ...), custom_call_target="tpu_custom_call" | custom-call | tf_op jit(solution)/shard_map/pallas_call | solution.py:334
  32.1 2.4 %shard_map.173 = (bf16[256,1024]{1,0:T(8,128)(2,1)S(1)}, bf16[768,768]{1,0:T(8,128)(2,1)S(1)}) custom-call(s32[1]{0:T(128)} %bitcast.me, bf16[768,768]{1,0:T(8,128)(2,1)S(1)} %get-tuple-element.34.heads, f32[768,512]{1,0:T(8,128)S(1)} %get-tuple-element.35.shares, bf16[768,256]{1,0:T(8,128)(2,1)S(1)} %get-tuple-element.38.d_mixture, ...), custom_call_target="tpu_custom_call" | custom-call | tf_op jit(solution)/shard_map/pallas_call | solution.py:340
  36.4 1.2 %collective-permute-start.9 = (bf16[8,8,1024]{2,1,0:T(8,128)(2,1)S(1)}, bf16[8,8,1024]{2,1,0:T(8,128)(2,1)S(1)}, u32[]{:S(2)}, u32[]{:S(2)}) collective-permute-start(bf16[8,8,1024]{2,1,0:T(8,128)(2,1)S(1)} %slice.103), channel_id=1, source_target_pairs={{0,2},{1,3},{2,0},{3,1},{4,6},{5,7},{6,4},{7,5},{8,10},{9,11},{10,... | collective-permute-start | bytes 393224 | tf_op jit(solution)/shard_map/ppermute | solution.py:309
  37.7 2.3 %collective-permute-start.12 = (bf16[8,8,1152]{2,1,0:T(8,128)(2,1)S(1)}, bf16[8,8,1152]{2,1,0:T(8,128)(2,1)S(1)}, u32[]{:S(2)}, u32[]{:S(2)}) collective-permute-start(bf16[8,8,1152]{2,1,0:T(8,128)(2,1)S(1)} %slice.107), channel_id=1, source_target_pairs={{0,4},{1,5},{2,6},{3,7},{4,0},{5,1},{6,2},{7,3},{8,12},{9,13},{10,... | collective-permute-start | bytes 442376 | tf_op jit(solution)/shard_map/ppermute | solution.py:309
  40.0 2.3 %collective-permute-done.9 = bf16[8,8,1024]{2,1,0:T(8,128)(2,1)S(1)} collective-permute-done((bf16[8,8,1024]{2,1,0:T(8,128)(2,1)S(1)}, bf16[8,8,1024]{2,1,0:T(8,128)(2,1)S(1)}, u32[]{:S(2)}, u32[]{:S(2)}) %collective-permute-start.9) | collective-permute-done | bytes 131104 | tf_op jit(solution)/shard_map/ppermute | solution.py:309
  42.3 2.1 %collective-permute-start.10 = (bf16[4,8,1024]{2,1,0:T(8,128)(2,1)S(1)}, bf16[4,8,1024]{2,1,0:T(8,128)(2,1)S(1)}, u32[]{:S(2)}, u32[]{:S(2)}) collective-permute-start(bf16[4,8,1024]{2,1,0:T(8,128)(2,1)S(1)} %slice.105), channel_id=1, source_target_pairs={{0,4},{1,5},{2,6},{3,7},{4,0},{5,1},{6,2},{7,3},{8,12},{9,13},{10,... | collective-permute-start | bytes 196616 | tf_op jit(solution)/shard_map/ppermute | solution.py:309
  44.4 1.2 %collective-permute-start.13 = (bf16[4,8,1152]{2,1,0:T(8,128)(2,1)S(1)}, bf16[4,8,1152]{2,1,0:T(8,128)(2,1)S(1)}, u32[]{:S(2)}, u32[]{:S(2)}) collective-permute-start(bf16[4,8,1152]{2,1,0:T(8,128)(2,1)S(1)} %slice.109), channel_id=1, source_target_pairs={{0,2},{1,3},{2,0},{3,1},{4,6},{5,7},{6,4},{7,5},{8,10},{9,11},{10,... | collective-permute-start | bytes 221192 | tf_op jit(solution)/shard_map/ppermute | solution.py:309
  46.6 2.2 %collective-permute-done.13 = bf16[4,8,1152]{2,1,0:T(8,128)(2,1)S(1)} collective-permute-done((bf16[4,8,1152]{2,1,0:T(8,128)(2,1)S(1)}, bf16[4,8,1152]{2,1,0:T(8,128)(2,1)S(1)}, u32[]{:S(2)}, u32[]{:S(2)}) %collective-permute-start.13) | collective-permute-done | bytes 73760 | tf_op jit(solution)/shard_map/ppermute | solution.py:309
  48.9 1.1 %collective-permute-start.14 = (bf16[2,8,2176]{2,1,0:T(8,128)(2,1)S(1)}, bf16[2,8,2176]{2,1,0:T(8,128)(2,1)S(1)}, u32[]{:S(2)}, u32[]{:S(2)}) collective-permute-start(bf16[2,8,2176]{2,1,0:T(8,128)(2,1)S(1)} %pad_maximum_fusion), channel_id=1, source_target_pairs={{0,8},{1,9},{2,10},{3,11},{4,12},{5,13},{6,14},{7,15},{8,0},{9,1},... | collective-permute-start | bytes 208904 | tf_op jit(solution)/shard_map/ppermute | solution.py:309
  50.0 3.3 %collective-permute-done.14 = bf16[2,8,2176]{2,1,0:T(8,128)(2,1)S(1)} collective-permute-done((bf16[2,8,2176]{2,1,0:T(8,128)(2,1)S(1)}, bf16[2,8,2176]{2,1,0:T(8,128)(2,1)S(1)}, u32[]{:S(2)}, u32[]{:S(2)}) %collective-permute-start.14) | collective-permute-done | bytes 69664 | tf_op jit(solution)/shard_map/ppermute | solution.py:309
  53.3 2.3 %collective-permute-start.15 = (bf16[8,2176]{1,0:T(8,128)(2,1)S(1)}, bf16[8,2176]{1,0:T(8,128)(2,1)S(1)}, u32[]{:S(2)}, u32[]{:S(2)}) collective-permute-start(bf16[8,2176]{1,0:T(8,128)(2,1)S(1)} %get-tuple-element.58), channel_id=1, source_target_pairs={{0,16},{1,17},{2,18},{3,19},{4,20},{5,21},{6,22},{7,23},{8,24},{9,... | collective-permute-start | bytes 104456 | tf_op jit(solution)/shard_map/ppermute | solution.py:309
  55.6 2.4 %shard_map.174 = (bf16[768,256]{1,0:T(8,128)(2,1)}, f32[768,256]{1,0:T(8,128)}) custom-call(s32[6]{0:T(128)S(1)} %copy-done.6, bf16[768,256]{1,0:T(8,128)(2,1)S(1)} %copy-done, bf16[256,768]{1,0:T(8,128)(2,1)S(1)} %get-tuple-element.32.weights, f32[2,256]{1,0:T(2,128)S(1)} %get-tuple-element.33.gains, bf16[768,768]{1,0:T(8,128)(2,1)S(1)} %get-tuple-element.41.d_qkv, ...), custom_call_target="tpu_custom_call" | custom-call | tf_op jit(solution)/shard_map/pallas_call | solution.py:345
  (60 shorter events, 6.1 us)
Async XLA Ops:
  2.2 6.6 %collective-permute-start = (bf16[1,8,2304]{2,1,0:T(8,128)(2,1)}, bf16[1,8,2304]{2,1,0:T(8,128)(2,1)S(1)}, u32[]{:S(2)}, u32[]{:S(2)}) collective-permute-start(bf16[1,8,2304]{2,1,0:T(8,128)(2,1)} %bitcast.34), channel_id=1, source_target_pairs={{0,16},{1,17},{2,18},{3,19},{4,20},{5,21},{6,22},{7,23},{8,24},{9,... | collective-permute-start | bytes 110600 | tf_op jit(solution)/shard_map/ppermute | solution.py:309
  8.8 4.4 %collective-permute-start.1 = (bf16[2,8,2304]{2,1,0:T(8,128)(2,1)S(1)}, bf16[2,8,2304]{2,1,0:T(8,128)(2,1)S(1)}, u32[]{:S(2)}, u32[]{:S(2)}) collective-permute-start(bf16[2,8,2304]{2,1,0:T(8,128)(2,1)S(1)} %slice.97), channel_id=1, source_target_pairs={{0,8},{1,9},{2,10},{3,11},{4,12},{5,13},{6,14},{7,15},{8,0},{9,1},... | collective-permute-start | bytes 221192 | tf_op jit(solution)/shard_map/ppermute | solution.py:309
  13.2 11.9 %copy-start = (bf16[768,256]{1,0:T(8,128)(2,1)S(1)}, bf16[768,256]{1,0:T(8,128)(2,1)}, u32[]{:S(2)}) copy-start(bf16[768,256]{1,0:T(8,128)(2,1)} %tokens.5) | copy-start | bytes 1179652
  13.2 11.9 %copy-start.2 = (f32[128,128]{1,0:T(8,128)S(1)}, f32[128,128]{1,0:T(8,128)}, u32[]{:S(2)}) copy-start(f32[128,128]{1,0:T(8,128)} %constant.7.clone.sin) | copy-start | bytes 196612
  13.2 11.9 %copy-start.3 = (f32[128,128]{1,0:T(8,128)S(1)}, f32[128,128]{1,0:T(8,128)}, u32[]{:S(2)}) copy-start(f32[128,128]{1,0:T(8,128)} %constant.6.clone.cos) | copy-start | bytes 196612
  13.3 11.9 %copy-start.6 = (s32[6]{0:T(128)S(1)}, s32[6]{0:T(128)}, u32[]{:S(2)}) copy-start(s32[6]{0:T(128)} %lengths.5) | copy-start | bytes 76
  13.3 4.4 %collective-permute-start.2 = (bf16[4,8,1152]{2,1,0:T(8,128)(2,1)S(1)}, bf16[4,8,1152]{2,1,0:T(8,128)(2,1)S(1)}, u32[]{:S(2)}, u32[]{:S(2)}) collective-permute-start(bf16[4,8,1152]{2,1,0:T(8,128)(2,1)S(1)} %get-tuple-element.57), channel_id=1, source_target_pairs={{0,4},{1,5},{2,6},{3,7},{4,0},{5,1},{6,2},{7,3},{8,12},{9,13},{10,... | collective-permute-start | bytes 221192 | tf_op jit(solution)/shard_map/ppermute | solution.py:309
  15.1 4.4 %collective-permute-start.5 = (bf16[4,8,1152]{2,1,0:T(8,128)(2,1)S(1)}, bf16[4,8,1152]{2,1,0:T(8,128)(2,1)S(1)}, u32[]{:S(2)}, u32[]{:S(2)}) collective-permute-start(bf16[4,8,1152]{2,1,0:T(8,128)(2,1)S(1)} %get-tuple-element.56), channel_id=1, source_target_pairs={{0,2},{1,3},{2,0},{3,1},{4,6},{5,7},{6,4},{7,5},{8,10},{9,11},{10,... | collective-permute-start | bytes 221192 | tf_op jit(solution)/shard_map/ppermute | solution.py:309
  17.7 10.3 %copy-start.1 = (bf16[768,256]{1,0:T(8,128)(2,1)S(1)}, bf16[768,256]{1,0:T(8,128)(2,1)}, u32[]{:S(2)}) copy-start(bf16[768,256]{1,0:T(8,128)(2,1)} %cot.1) | copy-start | bytes 1179652
  17.7 5.2 %collective-permute-start.3 = (bf16[8,8,1152]{2,1,0:T(8,128)(2,1)S(1)}, bf16[8,8,1152]{2,1,0:T(8,128)(2,1)S(1)}, u32[]{:S(2)}, u32[]{:S(2)}) collective-permute-start(bf16[8,8,1152]{2,1,0:T(8,128)(2,1)S(1)} %slice.99), channel_id=1, source_target_pairs={{0,2},{1,3},{2,0},{3,1},{4,6},{5,7},{6,4},{7,5},{8,10},{9,11},{10,... | collective-permute-start | bytes 442376 | tf_op jit(solution)/shard_map/ppermute | solution.py:309
  19.5 5.5 %collective-permute-start.6 = (bf16[8,8,1152]{2,1,0:T(8,128)(2,1)S(1)}, bf16[8,8,1152]{2,1,0:T(8,128)(2,1)S(1)}, u32[]{:S(2)}, u32[]{:S(2)}) collective-permute-start(bf16[8,8,1152]{2,1,0:T(8,128)(2,1)S(1)} %slice.101), channel_id=1, source_target_pairs={{0,4},{1,5},{2,6},{3,7},{4,0},{5,1},{6,2},{7,3},{8,12},{9,13},{10,... | collective-permute-start | bytes 442376 | tf_op jit(solution)/shard_map/ppermute | solution.py:309
  23.0 2.2 %collective-permute-start.4 = (bf16[16,8,1152]{2,1,0:T(8,128)(2,1)S(1)}, bf16[16,8,1152]{2,1,0:T(8,128)(2,1)S(1)}, u32[]{:S(2)}, u32[]{:S(2)}) collective-permute-start(bf16[16,8,1152]{2,1,0:T(8,128)(2,1)S(1)} %constant_dynamic-update-slice_fusion.2), channel_id=1, source_target_pairs={{0,1},{1,0},{2,3},{3,2},{4,5},{5,4},{6,7},{7,6},{8,9},{9,8},{10,11... | collective-permute-start | bytes 884744 | tf_op jit(solution)/shard_map/ppermute | solution.py:309
  25.1 2.9 %collective-permute-start.7 = (bf16[16,8,1152]{2,1,0:T(8,128)(2,1)S(1)}, bf16[16,8,1152]{2,1,0:T(8,128)(2,1)S(1)}, u32[]{:S(2)}, u32[]{:S(2)}) collective-permute-start(bf16[16,8,1152]{2,1,0:T(8,128)(2,1)S(1)} %constant_dynamic-update-slice_fusion), channel_id=1, source_target_pairs={{0,1},{1,0},{2,3},{3,2},{4,5},{5,4},{6,7},{7,6},{8,9},{9,8},{10,11... | collective-permute-start | bytes 884744 | tf_op jit(solution)/shard_map/ppermute | solution.py:309
  34.6 1.7 %collective-permute-start.8 = (bf16[16,8,1024]{2,1,0:T(8,128)(2,1)S(1)}, bf16[16,8,1024]{2,1,0:T(8,128)(2,1)S(1)}, u32[]{:S(2)}, u32[]{:S(2)}) collective-permute-start(bf16[16,8,1024]{2,1,0:T(8,128)(2,1)S(1)} %slice_bitcast_fusion.1), channel_id=1, source_target_pairs={{0,1},{1,0},{2,3},{3,2},{4,5},{5,4},{6,7},{7,6},{8,9},{9,8},{10,11... | collective-permute-start | bytes 786440 | tf_op jit(solution)/shard_map/ppermute | solution.py:309
  35.2 2.4 %collective-permute-start.11 = (bf16[16,8,1152]{2,1,0:T(8,128)(2,1)S(1)}, bf16[16,8,1152]{2,1,0:T(8,128)(2,1)S(1)}, u32[]{:S(2)}, u32[]{:S(2)}) collective-permute-start(bf16[16,8,1152]{2,1,0:T(8,128)(2,1)S(1)} %slice_bitcast_fusion), channel_id=1, source_target_pairs={{0,1},{1,0},{2,3},{3,2},{4,5},{5,4},{6,7},{7,6},{8,9},{9,8},{10,11... | collective-permute-start | bytes 884744 | tf_op jit(solution)/shard_map/ppermute | solution.py:309
  36.4 5.8 %collective-permute-start.9 = (bf16[8,8,1024]{2,1,0:T(8,128)(2,1)S(1)}, bf16[8,8,1024]{2,1,0:T(8,128)(2,1)S(1)}, u32[]{:S(2)}, u32[]{:S(2)}) collective-permute-start(bf16[8,8,1024]{2,1,0:T(8,128)(2,1)S(1)} %slice.103), channel_id=1, source_target_pairs={{0,2},{1,3},{2,0},{3,1},{4,6},{5,7},{6,4},{7,5},{8,10},{9,11},{10,... | collective-permute-start | bytes 393224 | tf_op jit(solution)/shard_map/ppermute | solution.py:309
  37.7 6.7 %collective-permute-start.12 = (bf16[8,8,1152]{2,1,0:T(8,128)(2,1)S(1)}, bf16[8,8,1152]{2,1,0:T(8,128)(2,1)S(1)}, u32[]{:S(2)}, u32[]{:S(2)}) collective-permute-start(bf16[8,8,1152]{2,1,0:T(8,128)(2,1)S(1)} %slice.107), channel_id=1, source_target_pairs={{0,4},{1,5},{2,6},{3,7},{4,0},{5,1},{6,2},{7,3},{8,12},{9,13},{10,... | collective-permute-start | bytes 442376 | tf_op jit(solution)/shard_map/ppermute | solution.py:309
  42.3 4.3 %collective-permute-start.10 = (bf16[4,8,1024]{2,1,0:T(8,128)(2,1)S(1)}, bf16[4,8,1024]{2,1,0:T(8,128)(2,1)S(1)}, u32[]{:S(2)}, u32[]{:S(2)}) collective-permute-start(bf16[4,8,1024]{2,1,0:T(8,128)(2,1)S(1)} %slice.105), channel_id=1, source_target_pairs={{0,4},{1,5},{2,6},{3,7},{4,0},{5,1},{6,2},{7,3},{8,12},{9,13},{10,... | collective-permute-start | bytes 196616 | tf_op jit(solution)/shard_map/ppermute | solution.py:309
  44.4 4.4 %collective-permute-start.13 = (bf16[4,8,1152]{2,1,0:T(8,128)(2,1)S(1)}, bf16[4,8,1152]{2,1,0:T(8,128)(2,1)S(1)}, u32[]{:S(2)}, u32[]{:S(2)}) collective-permute-start(bf16[4,8,1152]{2,1,0:T(8,128)(2,1)S(1)} %slice.109), channel_id=1, source_target_pairs={{0,2},{1,3},{2,0},{3,1},{4,6},{5,7},{6,4},{7,5},{8,10},{9,11},{10,... | collective-permute-start | bytes 221192 | tf_op jit(solution)/shard_map/ppermute | solution.py:309
  48.9 4.4 %collective-permute-start.14 = (bf16[2,8,2176]{2,1,0:T(8,128)(2,1)S(1)}, bf16[2,8,2176]{2,1,0:T(8,128)(2,1)S(1)}, u32[]{:S(2)}, u32[]{:S(2)}) collective-permute-start(bf16[2,8,2176]{2,1,0:T(8,128)(2,1)S(1)} %pad_maximum_fusion), channel_id=1, source_target_pairs={{0,8},{1,9},{2,10},{3,11},{4,12},{5,13},{6,14},{7,15},{8,0},{9,1},... | collective-permute-start | bytes 208904 | tf_op jit(solution)/shard_map/ppermute | solution.py:309
  53.3 4.9 %collective-permute-start.15 = (bf16[8,2176]{1,0:T(8,128)(2,1)S(1)}, bf16[8,2176]{1,0:T(8,128)(2,1)S(1)}, u32[]{:S(2)}, u32[]{:S(2)}) collective-permute-start(bf16[8,2176]{1,0:T(8,128)(2,1)S(1)} %get-tuple-element.58), channel_id=1, source_target_pairs={{0,16},{1,17},{2,18},{3,19},{4,20},{5,21},{6,22},{7,23},{8,24},{9,... | collective-permute-start | bytes 104456 | tf_op jit(solution)/shard_map/ppermute | solution.py:309
  55.6 2.6 %copy-start.5 = (bf16[8,768]{1,0:T(8,128)(2,1)S(1)}, bf16[8,768]{1,0:T(8,128)(2,1)}, u32[]{:S(2)}) copy-start(bf16[8,768]{1,0:T(8,128)(2,1)} %w_in.3) | copy-start | bytes 36868
  55.6 2.6 %copy-start.7 = (bf16[8]{0:T(256)(128)(2,1)S(1)}, bf16[8]{0:T(256)(128)(2,1)}, u32[]{:S(2)}) copy-start(bf16[8]{0:T(256)(128)(2,1)} %param.17) | copy-start | bytes 52
  55.6 2.6 %copy-start.8 = (bf16[8]{0:T(256)(128)(2,1)S(1)}, bf16[8]{0:T(256)(128)(2,1)}, u32[]{:S(2)}) copy-start(bf16[8]{0:T(256)(128)(2,1)} %param.18) | copy-start | bytes 52
  (1 other events, 2.6 us)

commit v3 on v2

--- a/solution.py
+++ b/solution.py
@@ -295,13 +295,14 @@
     hops = []
     while 2 ** len(hops) < n:
         hops.append(n >> (len(hops) + 1))
+    hops = tuple(hops)
     last = len(hops) - 1
-    swapped = list(hops)
-    joined = last
-    if last > 1:
-        swapped[last - 2], swapped[last - 1] = hops[last - 1], hops[last - 2]
-        joined = last - 2
-    hops, swapped = tuple(hops), tuple(swapped)
+    single = max(last - 2, 0)
+    plane = [0]
+    for mask in hops[single:last]:
+        plane += [mask ^ other for other in plane]
+    plane = plane[1:]
+    size = 2**single
     gain_attn = gain_attn.reshape(1, rows)
     gain_mlp = gain_mlp.reshape(1, rows)
 
@@ -311,14 +312,14 @@
     held = pl.pallas_call(
         pack_kernel, out_specs=NEAR, out_shape=jax.ShapeDtypeStruct((rows, FIRST + SECOND), bf16)
     )(w_qkv, w_attn, w_in, w_mlp.T, gain_attn, gain_mlp)
-    room = put(jnp.zeros((2**joined, rows, FIRST + SECOND), bf16), held[None], 0)
-    for k in range(joined):
+    room = put(jnp.zeros((size, rows, FIRST + SECOND), bf16), held[None], 0)
+    for k in range(single):
         room = put(room, trade(room[: 2**k], hops[k]), 2**k)
-    first = put(jnp.zeros((n // 2, rows, FIRST), bf16), room[:, :, :FIRST], 0)
-    second = put(jnp.zeros((n // 2, rows, SECOND), bf16), room[:, :, FIRST:], 0)
-    for k in range(joined, last):
-        one, two = trade(first[: 2**k], hops[k]), trade(second[: 2**k], swapped[k])
-        first, second = put(first, one, 2**k), put(second, two, 2**k)
+    got = [trade(room, mask) for mask in plane]
+    room = put(jnp.zeros((n // 2, rows, FIRST + SECOND), bf16), room, 0)
+    for k, piece in enumerate(got):
+        room = put(room, piece, size * (k + 1))
+    first, second = room[:, :, :FIRST], room[:, :, FIRST:]
     first_got, second_got = trade(first, 1), trade(second, 1)
     first = first.reshape(D // 2, FIRST), first_got.reshape(D // 2, FIRST)
     second = second.reshape(D // 2, SECOND), second_got.reshape(D // 2, SECOND)
@@ -332,7 +333,7 @@
         [((D, QKV), bf16), ((D, D), bf16), ((2, D), f32), ((count, D), bf16), ((count, QKV), bf16), ((count, WIDE), f32), ((count, D), bf16)],
     )(me, lengths, tokens, *first, cos, sin)
     w_mlp_all, middle, hidden, d_middle, d_mixture, g_attn, second_sums = call(
-        functools.partial(feed_kernel, swapped, rows),
+        functools.partial(feed_kernel, hops, rows),
         [SMALL] * 2 + [NEAR] * 7,
         [((D, FF), bf16), ((count, D), f32), ((count, FF), bf16), ((count, D), f32), ((count, D), bf16), ((D, D), bf16), ((D, 3 * FF), bf16)],
         [((count, D), bf16), ((count, D), bf16), ((count, D), bf16), ((count, 2 * FF), bf16)],
@@ -352,11 +353,14 @@
         return (kept[:half].astype(f32) + got.astype(f32)).astype(bf16)
 
     first, second = first_sums.reshape(n, rows, SUMS), second_sums.reshape(n, rows, 3 * FF)
-    for k in range(last, joined - 1, -1):
-        first, second = halve(first, hops[k]), halve(second, swapped[k])
-    kept = jnp.zeros((2**joined, rows, SUMS + 3 * FF), bf16)
-    kept = put(put(kept, first, 0), second, 0, SUMS)
-    for k in range(joined - 1, 0, -1):
+    first, second = halve(first, 1), halve(second, 1)
+    kept = put(put(jnp.zeros((n // 2, rows, SUMS + 3 * FF), bf16), first, 0), second, 0, SUMS)
+    got = [trade(kept[size * (k + 1) : size * (k + 2)], mask) for k, mask in enumerate(plane)]
+    total = kept[:size].astype(f32)
+    for piece in got:
+        total = total + piece.astype(f32)
+    kept = total.astype(bf16)
+    for k in range(single - 1, 0, -1):
         kept = halve(kept, hops[k])
     got = trade(kept[1], hops[0])
     g_qkv, g_attn, g_in, g_mlp, g_first, g_second = call(

time: 59.1 us -> 55.4 us (0.937)
  starting transfers between devices: 23.9 us -> 17.9 us
  waiting for transfers between devices: 18.6 us -> 21 us
    ppermute x16 -> x14, starting transfers between devices: 23.9 us -> 17.9 us  [trade(): return lax.ppermute(values, 'dp', [(i, i ^ mask) for i in range(n)])]
    ppermute x16 -> x14, waiting for transfers between devices: 18.6 us -> 21 us  [trade(): return lax.ppermute(values, 'dp', [(i, i ^ mask) for i in range(n)])]
  transfers between devices with their start and end apart: 16 -> 14, of which waited for: 11 -> 11; matrix products, arithmetic and copies ran while one was open for 2% -> 2% of each run, Pallas kernels for 9% -> 9%
where the time goes in v3:
time: 55.4 us; the launch traced here: 55.1 us
  waiting for transfers between devices  21 us (38%)
  starting transfers between devices  17.9 us (32%)
  Pallas kernels  14 us (25%)
  local copies, waits for them, and re-layouts  1.09 us (2%)
  between operations  0.85 us (2%)
    ppermute x14, waiting for transfers between devices, trade(): return lax.ppermute(values, 'dp', [(i, i ^ mask) for i in range(n)])  21 us
    ppermute x14, starting transfers between devices, trade(): return lax.ppermute(values, 'dp', [(i, i ^ mask) for i in range(n)])  17.9 us
    pallas_call x1, Pallas kernels, on_device(): call(functools.partial(feed_kernel, hops, rows), [SMALL] * 2 + [NEAR] * 7...  4.15 us
    pallas_call x1, Pallas kernels, on_device(): call(functools.partial(attend_kernel, hops, rows), [SMALL] * 2 + [NEAR] *...  2.78 us
    pallas_call x1, Pallas kernels, on_device(): call(outputs_kernel, [SMALL] + [NEAR] * 8, [((count, D), bf16), ((count,...  2.43 us
    pallas_call x1, Pallas kernels, on_device(): call(functools.partial(attend_back_kernel, hops, rows), [SMALL] + [NEAR]...  2.43 us
    pallas_call x1, Pallas kernels, on_device(): pl.pallas_call(pack_kernel, out_specs=NEAR, out_shape=jax.ShapeDtypeStruc...  1.55 us
  transfers between devices with their start and end apart: 14, of which 11 were waited for; matrix products, arithmetic and copies ran while one was open for 2% of the time, Pallas kernels for 9%

profile of v3, /device:TPU:0, one launch (start us, length us, event | category | flops | bytes accessed | tf_op | source)
XLA Modules:
  0.0 55.1 jit_solution(11234473674648673252)
XLA Ops:
  0.6 1.6 %shard_map.170 = bf16[8,2304]{1,0:T(8,128)(2,1)} custom-call(bf16[8,768]{1,0:T(8,128)(2,1)} %w_qkv.3, bf16[8,256]{1,0:T(8,128)(2,1)} %w_attn.1, bf16[8,768]{1,0:T(8,128)(2,1)} %w_in.3, bf16[8,384]{1,0:T(8,128)(2,1)} %bitcast.36, bf16[1,8]{1,0:T(2,128)(2,1)} %bitcast.30, bf16[1,8]{1,0:T(2,128)(2,1)} %bitcast.32), custom_call_target="tpu_custom_call" | custom-call | tf_op jit(solution)/shard_map/pallas_call | solution.py:312
  2.2 4.0 %collective-permute-start = (bf16[1,8,2304]{2,1,0:T(8,128)(2,1)}, bf16[1,8,2304]{2,1,0:T(8,128)(2,1)S(1)}, u32[]{:S(2)}, u32[]{:S(2)}) collective-permute-start(bf16[1,8,2304]{2,1,0:T(8,128)(2,1)} %bitcast.34), channel_id=1, source_target_pairs={{0,16},{1,17},{2,18},{3,19},{4,20},{5,21},{6,22},{7,23},{8,24},{9,... | collective-permute-start | bytes 110600 | tf_op jit(solution)/shard_map/ppermute | solution.py:310
  6.2 0.8 %dynamic_update_slice.25 = bf16[4,8,2304]{2,1,0:T(8,128)(2,1)S(1)} pad(bf16[1,8,2304]{2,1,0:T(8,128)(2,1)} %bitcast.35, bf16[]{:T(256)} %constant.11.clone.1), padding=0_3x0_0x0_0 | pad | bytes 184322 | tf_op jit(solution)/shard_map/dynamic_update_slice | solution.py:289
  7.0 1.7 %collective-permute-done = bf16[1,8,2304]{2,1,0:T(8,128)(2,1)S(1)} collective-permute-done((bf16[1,8,2304]{2,1,0:T(8,128)(2,1)}, bf16[1,8,2304]{2,1,0:T(8,128)(2,1)S(1)}, u32[]{:S(2)}, u32[]{:S(2)}) %collective-permute-start) | collective-permute-done | bytes 36896 | tf_op jit(solution)/shard_map/ppermute | solution.py:310
  8.8 1.6 %collective-permute-start.1 = (bf16[2,8,2304]{2,1,0:T(8,128)(2,1)S(1)}, bf16[2,8,2304]{2,1,0:T(8,128)(2,1)S(1)}, u32[]{:S(2)}, u32[]{:S(2)}) collective-permute-start(bf16[2,8,2304]{2,1,0:T(8,128)(2,1)S(1)} %slice.71), channel_id=1, source_target_pairs={{0,8},{1,9},{2,10},{3,11},{4,12},{5,13},{6,14},{7,15},{8,0},{9,1},... | collective-permute-start | bytes 221192 | tf_op jit(solution)/shard_map/ppermute | solution.py:310
  10.4 2.8 %collective-permute-done.1 = bf16[2,8,2304]{2,1,0:T(8,128)(2,1)S(1)} collective-permute-done((bf16[2,8,2304]{2,1,0:T(8,128)(2,1)S(1)}, bf16[2,8,2304]{2,1,0:T(8,128)(2,1)S(1)}, u32[]{:S(2)}, u32[]{:S(2)}) %collective-permute-start.1) | collective-permute-done | bytes 73760 | tf_op jit(solution)/shard_map/ppermute | solution.py:310
  13.2 1.7 %collective-permute-start.2 = (bf16[4,8,2304]{2,1,0:T(8,128)(2,1)S(1)}, bf16[4,8,2304]{2,1,0:T(8,128)(2,1)S(1)}, u32[]{:S(2)}, u32[]{:S(2)}) collective-permute-start(bf16[4,8,2304]{2,1,0:T(8,128)(2,1)S(1)} %constant_dynamic-update-slice_fusion.3), channel_id=1, source_target_pairs={{0,4},{1,5},{2,6},{3,7},{4,0},{5,1},{6,2},{7,3},{8,12},{9,13},{10,... | collective-permute-start | bytes 442376 | tf_op jit(solution)/shard_map/ppermute | solution.py:310
  14.9 1.4 %collective-permute-start.4 = (bf16[4,8,2304]{2,1,0:T(8,128)(2,1)S(1)}, bf16[4,8,2304]{2,1,0:T(8,128)(2,1)S(1)}, u32[]{:S(2)}, u32[]{:S(2)}) collective-permute-start(bf16[4,8,2304]{2,1,0:T(8,128)(2,1)S(1)} %constant_dynamic-update-slice_fusion.3), channel_id=1, source_target_pairs={{0,6},{1,7},{2,4},{3,5},{4,2},{5,3},{6,0},{7,1},{8,14},{9,15},{10,... | collective-permute-start | bytes 442376 | tf_op jit(solution)/shard_map/ppermute | solution.py:310
  16.7 2.5 %collective-permute-done.2 = bf16[4,8,2304]{2,1,0:T(8,128)(2,1)S(1)} collective-permute-done((bf16[4,8,2304]{2,1,0:T(8,128)(2,1)S(1)}, bf16[4,8,2304]{2,1,0:T(8,128)(2,1)S(1)}, u32[]{:S(2)}, u32[]{:S(2)}) %collective-permute-start.2) | collective-permute-done | bytes 147488 | tf_op jit(solution)/shard_map/ppermute | solution.py:310
  19.3 2.2 %collective-permute-done.3 = bf16[4,8,2304]{2,1,0:T(8,128)(2,1)S(1)} collective-permute-done((bf16[4,8,2304]{2,1,0:T(8,128)(2,1)S(1)}, bf16[4,8,2304]{2,1,0:T(8,128)(2,1)S(1)}, u32[]{:S(2)}, u32[]{:S(2)}) %collective-permute-start.3) | collective-permute-done | bytes 147488 | tf_op jit(solution)/shard_map/ppermute | solution.py:310
  22.2 1.1 %collective-permute-done.5 = bf16[16,8,1152]{2,1,0:T(8,128)(2,1)S(1)} collective-permute-done((bf16[16,8,1152]{2,1,0:T(8,128)(2,1)S(1)}, bf16[16,8,1152]{2,1,0:T(8,128)(2,1)S(1)}, u32[]{:S(2)}, u32[]{:S(2)}) %collective-permute-start.5) | collective-permute-done | bytes 294944 | tf_op jit(solution)/shard_map/ppermute | solution.py:310
  23.3 2.8 %shard_map.171 = (bf16[256,768]{1,0:T(8,128)(2,1)S(1)}, bf16[256,256]{1,0:T(8,128)(2,1)S(1)}, f32[2,256]{1,0:T(2,128)S(1)}, bf16[768,256]{1,0:T(8,128)(2,1)S(1)}...) custom-call(s32[1]{0:T(128)} %bitcast.me, s32[6]{0:T(128)S(1)} %copy-done.6, ...), custom_call_target="tpu_custom_call" | custom-call | tf_op jit(solution)/shard_map/pallas_call | solution.py:330
  26.1 4.2 %shard_map.172 = (bf16[256,384]{1,0:T(8,128)(2,1)S(1)}, f32[768,256]{1,0:T(8,128)S(1)}, bf16[768,384]{1,0:T(8,128)(2,1)S(1)}, f32[768,256]{1,0:T(8,128)S(1)}, bf...) custom-call(s32[1]{0:T(128)} %bitcast.me, s32[6]{0:T(128)S(1)} %copy-done.6, ...), custom_call_target="tpu_custom_call" | custom-call | tf_op jit(solution)/shard_map/pallas_call | solution.py:335
  30.3 2.4 %shard_map.173 = (bf16[256,1024]{1,0:T(8,128)(2,1)S(1)}, bf16[768,768]{1,0:T(8,128)(2,1)S(1)}) custom-call(s32[1]{0:T(128)} %bitcast.me, bf16[768,768]{1,0:T(8,128)(2,1)S(1)} %get-tuple-element.34.heads, f32[768,512]{1,0:T(8,128)S(1)} %get-tuple-element.35.shares, bf16[768,256]{1,0:T(8,128)(2,1)S(1)} %get-tuple-element.38.d_mixture, ...), custom_call_target="tpu_custom_call" | custom-call | tf_op jit(solution)/shard_map/pallas_call | solution.py:341
  33.4 0.9 %collective-permute-done.7 = bf16[16,8,1024]{2,1,0:T(8,128)(2,1)S(1)} collective-permute-done((bf16[16,8,1024]{2,1,0:T(8,128)(2,1)S(1)}, bf16[16,8,1024]{2,1,0:T(8,128)(2,1)S(1)}, u32[]{:S(2)}, u32[]{:S(2)}) %collective-permute-start.7) | collective-permute-done | bytes 262176 | tf_op jit(solution)/shard_map/ppermute | solution.py:310
  34.9 1.7 %collective-permute-start.9 = (bf16[4,8,2176]{2,1,0:T(8,128)(2,1)S(1)}, bf16[4,8,2176]{2,1,0:T(8,128)(2,1)S(1)}, u32[]{:S(2)}, u32[]{:S(2)}) collective-permute-start(bf16[4,8,2176]{2,1,0:T(8,128)(2,1)S(1)} %get-tuple-element.60), channel_id=1, source_target_pairs={{0,4},{1,5},{2,6},{3,7},{4,0},{5,1},{6,2},{7,3},{8,12},{9,13},{10,... | collective-permute-start | bytes 417800 | tf_op jit(solution)/shard_map/ppermute | solution.py:310
  36.6 1.5 %collective-permute-start.11 = (bf16[4,8,2176]{2,1,0:T(8,128)(2,1)S(1)}, bf16[4,8,2176]{2,1,0:T(8,128)(2,1)S(1)}, u32[]{:S(2)}, u32[]{:S(2)}) collective-permute-start(bf16[4,8,2176]{2,1,0:T(8,128)(2,1)S(1)} %get-tuple-element.61), channel_id=1, source_target_pairs={{0,6},{1,7},{2,4},{3,5},{4,2},{5,3},{6,0},{7,1},{8,14},{9,15},{10,... | collective-permute-start | bytes 417800 | tf_op jit(solution)/shard_map/ppermute | solution.py:310
  38.4 5.0 %collective-permute-done.9 = bf16[4,8,2176]{2,1,0:T(8,128)(2,1)S(1)} collective-permute-done((bf16[4,8,2176]{2,1,0:T(8,128)(2,1)S(1)}, bf16[4,8,2176]{2,1,0:T(8,128)(2,1)S(1)}, u32[]{:S(2)}, u32[]{:S(2)}) %collective-permute-start.9) | collective-permute-done | bytes 139296 | tf_op jit(solution)/shard_map/ppermute | solution.py:310
  44.0 1.0 %collective-permute-done.10 = bf16[4,8,2176]{2,1,0:T(8,128)(2,1)S(1)} collective-permute-done((bf16[4,8,2176]{2,1,0:T(8,128)(2,1)S(1)}, bf16[4,8,2176]{2,1,0:T(8,128)(2,1)S(1)}, u32[]{:S(2)}, u32[]{:S(2)}) %collective-permute-start.10) | collective-permute-done | bytes 139296 | tf_op jit(solution)/shard_map/ppermute | solution.py:310
  45.1 1.5 %collective-permute-start.12 = (bf16[2,8,2176]{2,1,0:T(8,128)(2,1)S(1)}, bf16[2,8,2176]{2,1,0:T(8,128)(2,1)S(1)}, u32[]{:S(2)}, u32[]{:S(2)}) collective-permute-start(bf16[2,8,2176]{2,1,0:T(8,128)(2,1)S(1)} %slice.81), channel_id=1, source_target_pairs={{0,8},{1,9},{2,10},{3,11},{4,12},{5,13},{6,14},{7,15},{8,0},{9,1},... | collective-permute-start | bytes 208904 | tf_op jit(solution)/shard_map/ppermute | solution.py:310
  46.6 2.9 %collective-permute-done.12 = bf16[2,8,2176]{2,1,0:T(8,128)(2,1)S(1)} collective-permute-done((bf16[2,8,2176]{2,1,0:T(8,128)(2,1)S(1)}, bf16[2,8,2176]{2,1,0:T(8,128)(2,1)S(1)}, u32[]{:S(2)}, u32[]{:S(2)}) %collective-permute-start.12) | collective-permute-done | bytes 69664 | tf_op jit(solution)/shard_map/ppermute | solution.py:310
  49.5 2.5 %collective-permute-start.13 = (bf16[8,2176]{1,0:T(8,128)(2,1)S(1)}, bf16[8,2176]{1,0:T(8,128)(2,1)S(1)}, u32[]{:S(2)}, u32[]{:S(2)}) collective-permute-start(bf16[8,2176]{1,0:T(8,128)(2,1)S(1)} %get-tuple-element.63), channel_id=1, source_target_pairs={{0,16},{1,17},{2,18},{3,19},{4,20},{5,21},{6,22},{7,23},{8,24},{9,... | collective-permute-start | bytes 104456 | tf_op jit(solution)/shard_map/ppermute | solution.py:310
  52.0 2.4 %shard_map.174 = (bf16[768,256]{1,0:T(8,128)(2,1)}, f32[768,256]{1,0:T(8,128)}) custom-call(s32[6]{0:T(128)S(1)} %copy-done.6, bf16[768,256]{1,0:T(8,128)(2,1)S(1)} %copy-done, bf16[256,768]{1,0:T(8,128)(2,1)S(1)} %get-tuple-element.32.weights, f32[2,256]{1,0:T(2,128)S(1)} %get-tuple-element.33.gains, bf16[768,768]{1,0:T(8,128)(2,1)S(1)} %get-tuple-element.41.d_qkv, ...), custom_call_target="tpu_custom_call" | custom-call | tf_op jit(solution)/shard_map/pallas_call | solution.py:346
  54.5 0.6 %shard_map.175 = (f32[8,768]{1,0:T(8,128)}, f32[8,256]{1,0:T(8,128)}, f32[8,768]{1,0:T(8,128)}, f32[8,384]{1,0:T(8,128)}, f32[1,8]{1,0:T(1,128)}, /*index=5*/f32[1,8]{1,0:T(1,128)}) custom-call(bf16[8,2176]{1,0:T(8,128)(2,1)S(1)} %get-tuple-element.64.kept, bf16[8,2176]{1,0:T(8,128)(2,1)S(1)} %collective-permute-done.13.got, bf16[8,768]{1,0:T(8,128)(2,1)S(1)} %copy-done.4, ...), custom_call_target="tpu_custom_call" | custom-call | tf_op jit(solution)/shard_map/pallas_call | solution.py:366
  (46 shorter events, 3.4 us)
Async XLA Ops:
  2.2 6.6 %collective-permute-start = (bf16[1,8,2304]{2,1,0:T(8,128)(2,1)}, bf16[1,8,2304]{2,1,0:T(8,128)(2,1)S(1)}, u32[]{:S(2)}, u32[]{:S(2)}) collective-permute-start(bf16[1,8,2304]{2,1,0:T(8,128)(2,1)} %bitcast.34), channel_id=1, source_target_pairs={{0,16},{1,17},{2,18},{3,19},{4,20},{5,21},{6,22},{7,23},{8,24},{9,... | collective-permute-start | bytes 110600 | tf_op jit(solution)/shard_map/ppermute | solution.py:310
  8.8 4.4 %collective-permute-start.1 = (bf16[2,8,2304]{2,1,0:T(8,128)(2,1)S(1)}, bf16[2,8,2304]{2,1,0:T(8,128)(2,1)S(1)}, u32[]{:S(2)}, u32[]{:S(2)}) collective-permute-start(bf16[2,8,2304]{2,1,0:T(8,128)(2,1)S(1)} %slice.71), channel_id=1, source_target_pairs={{0,8},{1,9},{2,10},{3,11},{4,12},{5,13},{6,14},{7,15},{8,0},{9,1},... | collective-permute-start | bytes 221192 | tf_op jit(solution)/shard_map/ppermute | solution.py:310
  13.2 6.0 %collective-permute-start.2 = (bf16[4,8,2304]{2,1,0:T(8,128)(2,1)S(1)}, bf16[4,8,2304]{2,1,0:T(8,128)(2,1)S(1)}, u32[]{:S(2)}, u32[]{:S(2)}) collective-permute-start(bf16[4,8,2304]{2,1,0:T(8,128)(2,1)S(1)} %constant_dynamic-update-slice_fusion.3), channel_id=1, source_target_pairs={{0,4},{1,5},{2,6},{3,7},{4,0},{5,1},{6,2},{7,3},{8,12},{9,13},{10,... | collective-permute-start | bytes 442376 | tf_op jit(solution)/shard_map/ppermute | solution.py:310
  14.9 6.6 %collective-permute-start.4 = (bf16[4,8,2304]{2,1,0:T(8,128)(2,1)S(1)}, bf16[4,8,2304]{2,1,0:T(8,128)(2,1)S(1)}, u32[]{:S(2)}, u32[]{:S(2)}) collective-permute-start(bf16[4,8,2304]{2,1,0:T(8,128)(2,1)S(1)} %constant_dynamic-update-slice_fusion.3), channel_id=1, source_target_pairs={{0,6},{1,7},{2,4},{3,5},{4,2},{5,3},{6,0},{7,1},{8,14},{9,15},{10,... | collective-permute-start | bytes 442376 | tf_op jit(solution)/shard_map/ppermute | solution.py:310
  16.4 5.1 %collective-permute-start.3 = (bf16[4,8,2304]{2,1,0:T(8,128)(2,1)S(1)}, bf16[4,8,2304]{2,1,0:T(8,128)(2,1)S(1)}, u32[]{:S(2)}, u32[]{:S(2)}) collective-permute-start(bf16[4,8,2304]{2,1,0:T(8,128)(2,1)S(1)} %constant_dynamic-update-slice_fusion.3), channel_id=1, source_target_pairs={{0,2},{1,3},{2,0},{3,1},{4,6},{5,7},{6,4},{7,5},{8,10},{9,11},{10,... | collective-permute-start | bytes 442376 | tf_op jit(solution)/shard_map/ppermute | solution.py:310
  19.2 4.1 %copy-start = (bf16[768,256]{1,0:T(8,128)(2,1)S(1)}, bf16[768,256]{1,0:T(8,128)(2,1)}, u32[]{:S(2)}) copy-start(bf16[768,256]{1,0:T(8,128)(2,1)} %tokens.5) | copy-start | bytes 1179652
  19.2 4.1 %copy-start.2 = (f32[128,128]{1,0:T(8,128)S(1)}, f32[128,128]{1,0:T(8,128)}, u32[]{:S(2)}) copy-start(f32[128,128]{1,0:T(8,128)} %constant.8.clone.sin) | copy-start | bytes 196612
  19.2 4.1 %copy-start.3 = (f32[128,128]{1,0:T(8,128)S(1)}, f32[128,128]{1,0:T(8,128)}, u32[]{:S(2)}) copy-start(f32[128,128]{1,0:T(8,128)} %constant.7.clone.cos) | copy-start | bytes 196612
  19.3 4.1 %copy-start.6 = (s32[6]{0:T(128)S(1)}, s32[6]{0:T(128)}, u32[]{:S(2)}) copy-start(s32[6]{0:T(128)} %lengths.5) | copy-start | bytes 76
  21.6 4.6 %copy-start.1 = (bf16[768,256]{1,0:T(8,128)(2,1)S(1)}, bf16[768,256]{1,0:T(8,128)(2,1)}, u32[]{:S(2)}) copy-start(bf16[768,256]{1,0:T(8,128)(2,1)} %cot.1) | copy-start | bytes 1179652
  21.7 1.6 %collective-permute-start.5 = (bf16[16,8,1152]{2,1,0:T(8,128)(2,1)S(1)}, bf16[16,8,1152]{2,1,0:T(8,128)(2,1)S(1)}, u32[]{:S(2)}, u32[]{:S(2)}) collective-permute-start(bf16[16,8,1152]{2,1,0:T(8,128)(2,1)S(1)} %get-tuple-element.59), channel_id=1, source_target_pairs={{0,1},{1,0},{2,3},{3,2},{4,5},{5,4},{6,7},{7,6},{8,9},{9,8},{10,11... | collective-permute-start | bytes 884744 | tf_op jit(solution)/shard_map/ppermute | solution.py:310
  21.7 4.4 %collective-permute-start.6 = (bf16[16,8,1152]{2,1,0:T(8,128)(2,1)S(1)}, bf16[16,8,1152]{2,1,0:T(8,128)(2,1)S(1)}, u32[]{:S(2)}, u32[]{:S(2)}) collective-permute-start(bf16[16,8,1152]{2,1,0:T(8,128)(2,1)S(1)} %get-tuple-element.56), channel_id=1, source_target_pairs={{0,1},{1,0},{2,3},{3,2},{4,5},{5,4},{6,7},{7,6},{8,9},{9,8},{10,11... | collective-permute-start | bytes 884744 | tf_op jit(solution)/shard_map/ppermute | solution.py:310
  32.7 1.6 %collective-permute-start.7 = (bf16[16,8,1024]{2,1,0:T(8,128)(2,1)S(1)}, bf16[16,8,1024]{2,1,0:T(8,128)(2,1)S(1)}, u32[]{:S(2)}, u32[]{:S(2)}) collective-permute-start(bf16[16,8,1024]{2,1,0:T(8,128)(2,1)S(1)} %slice_bitcast_fusion.1), channel_id=1, source_target_pairs={{0,1},{1,0},{2,3},{3,2},{4,5},{5,4},{6,7},{7,6},{8,9},{9,8},{10,11... | collective-permute-start | bytes 786440 | tf_op jit(solution)/shard_map/ppermute | solution.py:310
  33.0 1.8 %collective-permute-start.8 = (bf16[16,8,1152]{2,1,0:T(8,128)(2,1)S(1)}, bf16[16,8,1152]{2,1,0:T(8,128)(2,1)S(1)}, u32[]{:S(2)}, u32[]{:S(2)}) collective-permute-start(bf16[16,8,1152]{2,1,0:T(8,128)(2,1)S(1)} %slice_bitcast_fusion), channel_id=1, source_target_pairs={{0,1},{1,0},{2,3},{3,2},{4,5},{5,4},{6,7},{7,6},{8,9},{9,8},{10,11... | collective-permute-start | bytes 884744 | tf_op jit(solution)/shard_map/ppermute | solution.py:310
  34.9 8.6 %collective-permute-start.9 = (bf16[4,8,2176]{2,1,0:T(8,128)(2,1)S(1)}, bf16[4,8,2176]{2,1,0:T(8,128)(2,1)S(1)}, u32[]{:S(2)}, u32[]{:S(2)}) collective-permute-start(bf16[4,8,2176]{2,1,0:T(8,128)(2,1)S(1)} %get-tuple-element.60), channel_id=1, source_target_pairs={{0,4},{1,5},{2,6},{3,7},{4,0},{5,1},{6,2},{7,3},{8,12},{9,13},{10,... | collective-permute-start | bytes 417800 | tf_op jit(solution)/shard_map/ppermute | solution.py:310
  36.6 7.4 %collective-permute-start.11 = (bf16[4,8,2176]{2,1,0:T(8,128)(2,1)S(1)}, bf16[4,8,2176]{2,1,0:T(8,128)(2,1)S(1)}, u32[]{:S(2)}, u32[]{:S(2)}) collective-permute-start(bf16[4,8,2176]{2,1,0:T(8,128)(2,1)S(1)} %get-tuple-element.61), channel_id=1, source_target_pairs={{0,6},{1,7},{2,4},{3,5},{4,2},{5,3},{6,0},{7,1},{8,14},{9,15},{10,... | collective-permute-start | bytes 417800 | tf_op jit(solution)/shard_map/ppermute | solution.py:310
  38.0 6.9 %collective-permute-start.10 = (bf16[4,8,2176]{2,1,0:T(8,128)(2,1)S(1)}, bf16[4,8,2176]{2,1,0:T(8,128)(2,1)S(1)}, u32[]{:S(2)}, u32[]{:S(2)}) collective-permute-start(bf16[4,8,2176]{2,1,0:T(8,128)(2,1)S(1)} %get-tuple-element.62), channel_id=1, source_target_pairs={{0,2},{1,3},{2,0},{3,1},{4,6},{5,7},{6,4},{7,5},{8,10},{9,11},{10,... | collective-permute-start | bytes 417800 | tf_op jit(solution)/shard_map/ppermute | solution.py:310
  45.1 4.4 %collective-permute-start.12 = (bf16[2,8,2176]{2,1,0:T(8,128)(2,1)S(1)}, bf16[2,8,2176]{2,1,0:T(8,128)(2,1)S(1)}, u32[]{:S(2)}, u32[]{:S(2)}) collective-permute-start(bf16[2,8,2176]{2,1,0:T(8,128)(2,1)S(1)} %slice.81), channel_id=1, source_target_pairs={{0,8},{1,9},{2,10},{3,11},{4,12},{5,13},{6,14},{7,15},{8,0},{9,1},... | collective-permute-start | bytes 208904 | tf_op jit(solution)/shard_map/ppermute | solution.py:310
  49.5 5.0 %collective-permute-start.13 = (bf16[8,2176]{1,0:T(8,128)(2,1)S(1)}, bf16[8,2176]{1,0:T(8,128)(2,1)S(1)}, u32[]{:S(2)}, u32[]{:S(2)}) collective-permute-start(bf16[8,2176]{1,0:T(8,128)(2,1)S(1)} %get-tuple-element.63), channel_id=1, source_target_pairs={{0,16},{1,17},{2,18},{3,19},{4,20},{5,21},{6,22},{7,23},{8,24},{9,... | collective-permute-start | bytes 104456 | tf_op jit(solution)/shard_map/ppermute | solution.py:310
  52.0 2.4 %copy-start.4 = (bf16[8,768]{1,0:T(8,128)(2,1)S(1)}, bf16[8,768]{1,0:T(8,128)(2,1)}, u32[]{:S(2)}) copy-start(bf16[8,768]{1,0:T(8,128)(2,1)} %w_qkv.3) | copy-start | bytes 36868
  52.0 2.4 %copy-start.5 = (bf16[8,768]{1,0:T(8,128)(2,1)S(1)}, bf16[8,768]{1,0:T(8,128)(2,1)}, u32[]{:S(2)}) copy-start(bf16[8,768]{1,0:T(8,128)(2,1)} %w_in.3) | copy-start | bytes 36868
  52.0 2.5 %copy-start.7 = (bf16[8]{0:T(256)(128)(2,1)S(1)}, bf16[8]{0:T(256)(128)(2,1)}, u32[]{:S(2)}) copy-start(bf16[8]{0:T(256)(128)(2,1)} %param.17) | copy-start | bytes 52
  52.0 2.5 %copy-start.8 = (bf16[8]{0:T(256)(128)(2,1)S(1)}, bf16[8]{0:T(256)(128)(2,1)}, u32[]{:S(2)}) copy-start(bf16[8]{0:T(256)(128)(2,1)} %param.18) | copy-start | bytes 52

commit v4 on v3

--- a/solution.py
+++ b/solution.py
@@ -82,8 +82,11 @@
     out[:, FIRST + 2 * FF :] = w_mlp[...]
 
 
-def end_kernel(kept, got, w_qkv, w_in, gain_attn, gain_mlp, g_qkv, g_attn, g_in, g_mlp, g_first, g_second):
-    total = kept[...].astype(f32) + got[...].astype(f32)
+def end_kernel(*refs):
+    w_qkv, w_in, gain_attn, gain_mlp, g_qkv, g_attn, g_in, g_mlp, g_first, g_second = refs[-10:]
+    total = refs[0][...].astype(f32)
+    for got in refs[1:-10]:
+        total = total + got[...].astype(f32)
     part = total[:, :QKV]
     g_qkv[...] = part
     g_first[...] = to_row(jnp.sum(part * w_qkv[...].astype(f32), axis=1, keepdims=True)) / gain_attn[...].astype(f32)
@@ -296,13 +299,13 @@
     while 2 ** len(hops) < n:
         hops.append(n >> (len(hops) + 1))
     hops = tuple(hops)
-    last = len(hops) - 1
-    single = max(last - 2, 0)
-    plane = [0]
-    for mask in hops[single:last]:
-        plane += [mask ^ other for other in plane]
-    plane = plane[1:]
-    size = 2**single
+    lead = hops[:-1]
+    rounds = []
+    if len(lead) % 2:
+        rounds.append(((lead[0], 1),))
+    for k in range(len(lead) % 2, len(lead), 2):
+        one, two = lead[k], lead[k + 1]
+        rounds.append(((one ^ two, 3), (one, 1), (two, 2)))
     gain_attn = gain_attn.reshape(1, rows)
     gain_mlp = gain_mlp.reshape(1, rows)
 
@@ -312,13 +315,13 @@
     held = pl.pallas_call(
         pack_kernel, out_specs=NEAR, out_shape=jax.ShapeDtypeStruct((rows, FIRST + SECOND), bf16)
     )(w_qkv, w_attn, w_in, w_mlp.T, gain_attn, gain_mlp)
-    room = put(jnp.zeros((size, rows, FIRST + SECOND), bf16), held[None], 0)
-    for k in range(single):
-        room = put(room, trade(room[: 2**k], hops[k]), 2**k)
-    got = [trade(room, mask) for mask in plane]
-    room = put(jnp.zeros((n // 2, rows, FIRST + SECOND), bf16), room, 0)
-    for k, piece in enumerate(got):
-        room = put(room, piece, size * (k + 1))
+    room = held[None]
+    for partners in rounds:
+        size = room.shape[0]
+        got = [(trade(room, mask), place) for mask, place in partners]
+        room = put(jnp.zeros((size * (len(got) + 1), rows, FIRST + SECOND), bf16), room, 0)
+        for piece, place in got:
+            room = put(room, piece, size * place)
     first, second = room[:, :, :FIRST], room[:, :, FIRST:]
     first_got, second_got = trade(first, 1), trade(second, 1)
     first = first.reshape(D // 2, FIRST), first_got.reshape(D // 2, FIRST)
@@ -355,19 +358,22 @@
     first, second = first_sums.reshape(n, rows, SUMS), second_sums.reshape(n, rows, 3 * FF)
     first, second = halve(first, 1), halve(second, 1)
     kept = put(put(jnp.zeros((n // 2, rows, SUMS + 3 * FF), bf16), first, 0), second, 0, SUMS)
-    got = [trade(kept[size * (k + 1) : size * (k + 2)], mask) for k, mask in enumerate(plane)]
-    total = kept[:size].astype(f32)
-    for piece in got:
-        total = total + piece.astype(f32)
-    kept = total.astype(bf16)
-    for k in range(single - 1, 0, -1):
-        kept = halve(kept, hops[k])
-    got = trade(kept[1], hops[0])
+    for k, partners in enumerate(rounds[::-1]):
+        size = kept.shape[0] // (len(partners) + 1)
+        got = [trade(kept[size * place : size * (place + 1)], mask) for mask, place in partners]
+        if k == len(rounds) - 1:
+            break
+        total = kept[:size].astype(f32)
+        for piece in got:
+            total = total + piece.astype(f32)
+        kept = total.astype(bf16)
+        if k == 0:
+            kept, out, grad = lax.optimization_barrier((kept, out, grad))
     g_qkv, g_attn, g_in, g_mlp, g_first, g_second = call(
         end_kernel,
-        [NEAR] * 6,
+        [NEAR] * (5 + len(got)),
         [((rows, QKV), f32), ((rows, D), f32), ((rows, 2 * FF), f32), ((rows, FF), f32), ((1, rows), f32), ((1, rows), f32)],
-    )(kept[0], got, w_qkv, w_in, gain_attn, gain_mlp)
+    )(kept[0], *[piece[0] for piece in got], w_qkv, w_in, gain_attn, gain_mlp)
     return out, grad, g_qkv, g_attn, g_in, g_mlp.T, g_first.reshape(rows), g_second.reshape(rows)
 
 

time: 55.4 us -> 52.2 us (0.942)
  waiting for transfers between devices: 21 us -> 17.4 us
    ppermute x14 -> x16, waiting for transfers between devices: 21 us -> 17.4 us  [trade(): return lax.ppermute(values, 'dp', [(i, i ^ mask) for i in range(n)])]
    ppermute x14 -> x16, starting transfers between devices: 17.9 us -> 18.4 us  [trade(): return lax.ppermute(values, 'dp', [(i, i ^ mask) for i in range(n)])]
  transfers between devices with their start and end apart: 14 -> 16, of which waited for: 11 -> 11; matrix products, arithmetic and copies ran while one was open for 2% -> 2% of each run, Pallas kernels for 9% -> 10%
where the time goes in v4:
time: 52.2 us; the launch traced here: 52 us
  starting transfers between devices  18.4 us (35%)
  waiting for transfers between devices  17.4 us (33%)
  Pallas kernels  14 us (27%)
  local copies, waits for them, and re-layouts  1.08 us (2%)
  between operations  0.84 us (2%)
    ppermute x16, starting transfers between devices, trade(): return lax.ppermute(values, 'dp', [(i, i ^ mask) for i in range(n)])  18.4 us
    ppermute x16, waiting for transfers between devices, trade(): return lax.ppermute(values, 'dp', [(i, i ^ mask) for i in range(n)])  17.4 us
    pallas_call x1, Pallas kernels, on_device(): call(functools.partial(feed_kernel, hops, rows), [SMALL] * 2 + [NEAR] * 7...  4.15 us
    pallas_call x1, Pallas kernels, on_device(): call(functools.partial(attend_kernel, hops, rows), [SMALL] * 2 + [NEAR] *...  2.78 us
    pallas_call x1, Pallas kernels, on_device(): call(functools.partial(attend_back_kernel, hops, rows), [SMALL] + [NEAR]...  2.43 us
    pallas_call x1, Pallas kernels, on_device(): call(outputs_kernel, [SMALL] + [NEAR] * 8, [((count, D), bf16), ((count,...  2.43 us
    pallas_call x1, Pallas kernels, on_device(): pl.pallas_call(pack_kernel, out_specs=NEAR, out_shape=jax.ShapeDtypeStruc...  1.55 us
  transfers between devices with their start and end apart: 16, of which 11 were waited for; matrix products, arithmetic and copies ran while one was open for 2% of the time, Pallas kernels for 10%

profile of v4, /device:TPU:0, one launch (start us, length us, event | category | flops | bytes accessed | tf_op | source)
XLA Modules:
  0.0 52.0 jit_solution(9079753040728001028)
XLA Ops:
  0.6 1.6 %shard_map.170 = bf16[8,2304]{1,0:T(8,128)(2,1)} custom-call(bf16[8,768]{1,0:T(8,128)(2,1)} %refs_4_.1, bf16[8,256]{1,0:T(8,128)(2,1)} %w_attn.1, bf16[8,768]{1,0:T(8,128)(2,1)} %refs_5_.1, bf16[8,384]{1,0:T(8,128)(2,1)} %bitcast.42, bf16[1,8]{1,0:T(2,128)(2,1)} %bitcast.34, bf16[1,8]{1,0:T(2,128)(2,1)} %bitcast.36), custom_call_target="tpu_custom_call" | custom-call | tf_op jit(solution)/shard_map/pallas_call | solution.py:315
  2.2 5.0 %collective-permute-start = (bf16[1,8,2304]{2,1,0:T(8,128)(2,1)}, bf16[1,8,2304]{2,1,0:T(8,128)(2,1)S(1)}, u32[]{:S(2)}, u32[]{:S(2)}) collective-permute-start(bf16[1,8,2304]{2,1,0:T(8,128)(2,1)} %bitcast.38), channel_id=1, source_target_pairs={{0,24},{1,25},{2,26},{3,27},{4,28},{5,29},{6,30},{7,31},{8,16},{9,... | collective-permute-start | bytes 110600 | tf_op jit(solution)/shard_map/ppermute | solution.py:313
  7.8 0.8 %dynamic_update_slice.28 = bf16[4,8,2304]{2,1,0:T(8,128)(2,1)S(1)} pad(bf16[1,8,2304]{2,1,0:T(8,128)(2,1)} %bitcast.41, bf16[]{:T(256)} %constant.12.clone.1), padding=0_3x0_0x0_0 | pad | bytes 184322 | tf_op jit(solution)/shard_map/dynamic_update_slice | solution.py:292
  8.6 0.8 %collective-permute-done = bf16[1,8,2304]{2,1,0:T(8,128)(2,1)S(1)} collective-permute-done((bf16[1,8,2304]{2,1,0:T(8,128)(2,1)}, bf16[1,8,2304]{2,1,0:T(8,128)(2,1)S(1)}, u32[]{:S(2)}, u32[]{:S(2)}) %collective-permute-start) | collective-permute-done | bytes 36896 | tf_op jit(solution)/shard_map/ppermute | solution.py:313
  9.4 2.9 %collective-permute-done.1 = bf16[1,8,2304]{2,1,0:T(8,128)(2,1)S(1)} collective-permute-done((bf16[1,8,2304]{2,1,0:T(8,128)(2,1)}, bf16[1,8,2304]{2,1,0:T(8,128)(2,1)S(1)}, u32[]{:S(2)}, u32[]{:S(2)}) %collective-permute-start.1) | collective-permute-done | bytes 36896 | tf_op jit(solution)/shard_map/ppermute | solution.py:313
  12.3 2.5 %collective-permute-start.3 = (bf16[4,8,2304]{2,1,0:T(8,128)(2,1)S(1)}, bf16[4,8,2304]{2,1,0:T(8,128)(2,1)S(1)}, u32[]{:S(2)}, u32[]{:S(2)}) collective-permute-start(bf16[4,8,2304]{2,1,0:T(8,128)(2,1)S(1)} %constant_dynamic-update-slice_fusion.3), channel_id=1, source_target_pairs={{0,6},{1,7},{2,4},{3,5},{4,2},{5,3},{6,0},{7,1},{8,14},{9,15},{10,... | collective-permute-start | bytes 442376 | tf_op jit(solution)/shard_map/ppermute | solution.py:313
  14.9 0.6 %collective-permute-start.4 = (bf16[4,8,2304]{2,1,0:T(8,128)(2,1)S(1)}, bf16[4,8,2304]{2,1,0:T(8,128)(2,1)S(1)}, u32[]{:S(2)}, u32[]{:S(2)}) collective-permute-start(bf16[4,8,2304]{2,1,0:T(8,128)(2,1)S(1)} %constant_dynamic-update-slice_fusion.3), channel_id=1, source_target_pairs={{0,4},{1,5},{2,6},{3,7},{4,0},{5,1},{6,2},{7,3},{8,12},{9,13},{10,... | collective-permute-start | bytes 442376 | tf_op jit(solution)/shard_map/ppermute | solution.py:313
  16.0 4.0 %collective-permute-done.3 = bf16[4,8,2304]{2,1,0:T(8,128)(2,1)S(1)} collective-permute-done((bf16[4,8,2304]{2,1,0:T(8,128)(2,1)S(1)}, bf16[4,8,2304]{2,1,0:T(8,128)(2,1)S(1)}, u32[]{:S(2)}, u32[]{:S(2)}) %collective-permute-start.3) | collective-permute-done | bytes 147488 | tf_op jit(solution)/shard_map/ppermute | solution.py:313
  20.1 0.8 %collective-permute-done.4 = bf16[4,8,2304]{2,1,0:T(8,128)(2,1)S(1)} collective-permute-done((bf16[4,8,2304]{2,1,0:T(8,128)(2,1)S(1)}, bf16[4,8,2304]{2,1,0:T(8,128)(2,1)S(1)}, u32[]{:S(2)}, u32[]{:S(2)}) %collective-permute-start.4) | collective-permute-done | bytes 147488 | tf_op jit(solution)/shard_map/ppermute | solution.py:313
  21.6 1.1 %collective-permute-done.6 = bf16[16,8,1152]{2,1,0:T(8,128)(2,1)S(1)} collective-permute-done((bf16[16,8,1152]{2,1,0:T(8,128)(2,1)S(1)}, bf16[16,8,1152]{2,1,0:T(8,128)(2,1)S(1)}, u32[]{:S(2)}, u32[]{:S(2)}) %collective-permute-start.6) | collective-permute-done | bytes 294944 | tf_op jit(solution)/shard_map/ppermute | solution.py:313
  22.7 2.8 %shard_map.171 = (bf16[256,768]{1,0:T(8,128)(2,1)S(1)}, bf16[256,256]{1,0:T(8,128)(2,1)S(1)}, f32[2,256]{1,0:T(2,128)S(1)}, bf16[768,256]{1,0:T(8,128)(2,1)S(1)}...) custom-call(s32[1]{0:T(128)} %bitcast.me, s32[6]{0:T(128)S(1)} %copy-done.6, ...), custom_call_target="tpu_custom_call" | custom-call | tf_op jit(solution)/shard_map/pallas_call | solution.py:333
  25.4 4.2 %shard_map.172 = (bf16[256,384]{1,0:T(8,128)(2,1)S(1)}, f32[768,256]{1,0:T(8,128)S(1)}, bf16[768,384]{1,0:T(8,128)(2,1)S(1)}, f32[768,256]{1,0:T(8,128)S(1)}, bf...) custom-call(s32[1]{0:T(128)} %bitcast.me, s32[6]{0:T(128)S(1)} %copy-done.6, ...), custom_call_target="tpu_custom_call" | custom-call | tf_op jit(solution)/shard_map/pallas_call | solution.py:338
  29.6 2.4 %shard_map.173 = (bf16[256,1024]{1,0:T(8,128)(2,1)S(1)}, bf16[768,768]{1,0:T(8,128)(2,1)S(1)}) custom-call(s32[1]{0:T(128)} %bitcast.me, bf16[768,768]{1,0:T(8,128)(2,1)S(1)} %get-tuple-element.35.heads, f32[768,512]{1,0:T(8,128)S(1)} %get-tuple-element.36.shares, bf16[768,256]{1,0:T(8,128)(2,1)S(1)} %get-tuple-element.40.d_mixture, ...), custom_call_target="tpu_custom_call" | custom-call | tf_op jit(solution)/shard_map/pallas_call | solution.py:344
  32.7 0.9 %collective-permute-done.8 = bf16[16,8,1024]{2,1,0:T(8,128)(2,1)S(1)} collective-permute-done((bf16[16,8,1024]{2,1,0:T(8,128)(2,1)S(1)}, bf16[16,8,1024]{2,1,0:T(8,128)(2,1)S(1)}, u32[]{:S(2)}, u32[]{:S(2)}) %collective-permute-start.8) | collective-permute-done | bytes 262176 | tf_op jit(solution)/shard_map/ppermute | solution.py:313
  34.2 1.4 %collective-permute-start.12 = (bf16[4,8,2176]{2,1,0:T(8,128)(2,1)S(1)}, bf16[4,8,2176]{2,1,0:T(8,128)(2,1)S(1)}, u32[]{:S(2)}, u32[]{:S(2)}) collective-permute-start(bf16[4,8,2176]{2,1,0:T(8,128)(2,1)S(1)} %get-tuple-element.67), channel_id=1, source_target_pairs={{0,2},{1,3},{2,0},{3,1},{4,6},{5,7},{6,4},{7,5},{8,10},{9,11},{10,... | collective-permute-start | bytes 417800 | tf_op jit(solution)/shard_map/ppermute | solution.py:313
  35.7 0.8 %collective-permute-start.11 = (bf16[4,8,2176]{2,1,0:T(8,128)(2,1)S(1)}, bf16[4,8,2176]{2,1,0:T(8,128)(2,1)S(1)}, u32[]{:S(2)}, u32[]{:S(2)}) collective-permute-start(bf16[4,8,2176]{2,1,0:T(8,128)(2,1)S(1)} %get-tuple-element.68), channel_id=1, source_target_pairs={{0,4},{1,5},{2,6},{3,7},{4,0},{5,1},{6,2},{7,3},{8,12},{9,13},{10,... | collective-permute-start | bytes 417800 | tf_op jit(solution)/shard_map/ppermute | solution.py:313
  36.5 1.3 %collective-permute-start.10 = (bf16[4,8,2176]{2,1,0:T(8,128)(2,1)S(1)}, bf16[4,8,2176]{2,1,0:T(8,128)(2,1)S(1)}, u32[]{:S(2)}, u32[]{:S(2)}) collective-permute-start(bf16[4,8,2176]{2,1,0:T(8,128)(2,1)S(1)} %get-tuple-element.66), channel_id=1, source_target_pairs={{0,6},{1,7},{2,4},{3,5},{4,2},{5,3},{6,0},{7,1},{8,14},{9,15},{10,... | collective-permute-start | bytes 417800 | tf_op jit(solution)/shard_map/ppermute | solution.py:313
  37.8 2.4 %shard_map.174 = (bf16[768,256]{1,0:T(8,128)(2,1)}, f32[768,256]{1,0:T(8,128)}) custom-call(s32[6]{0:T(128)S(1)} %copy-done.6, bf16[768,256]{1,0:T(8,128)(2,1)S(1)} %copy-done, bf16[256,768]{1,0:T(8,128)(2,1)S(1)} %get-tuple-element.45.weights, f32[2,256]{1,0:T(2,128)S(1)} %get-tuple-element.38.gains, bf16[768,768]{1,0:T(8,128)(2,1)S(1)} %get-tuple-element.46.d_qkv, ...), custom_call_target="tpu_custom_call" | custom-call | tf_op jit(solution)/shard_map/pallas_call | solution.py:349
  40.7 3.5 %collective-permute-done.11 = bf16[4,8,2176]{2,1,0:T(8,128)(2,1)S(1)} collective-permute-done((bf16[4,8,2176]{2,1,0:T(8,128)(2,1)S(1)}, bf16[4,8,2176]{2,1,0:T(8,128)(2,1)S(1)}, u32[]{:S(2)}, u32[]{:S(2)}) %collective-permute-start.11) | collective-permute-done | bytes 139296 | tf_op jit(solution)/shard_map/ppermute | solution.py:313
  44.3 1.8 %collective-permute-start.13 = (bf16[1,8,2176]{2,1,0:T(8,128)(2,1)S(1)}, bf16[1,8,2176]{2,1,0:T(8,128)(2,1)S(1)}, u32[]{:S(2)}, u32[]{:S(2)}) collective-permute-start(bf16[1,8,2176]{2,1,0:T(8,128)(2,1)S(1)} %get-tuple-element.71), channel_id=1, source_target_pairs={{0,24},{1,25},{2,26},{3,27},{4,28},{5,29},{6,30},{7,31},{8,16},{9,... | collective-permute-start | bytes 104456 | tf_op jit(solution)/shard_map/ppermute | solution.py:313
  46.4 2.3 %collective-permute-start.15 = (bf16[1,8,2176]{2,1,0:T(8,128)(2,1)S(1)}, bf16[1,8,2176]{2,1,0:T(8,128)(2,1)S(1)}, u32[]{:S(2)}, u32[]{:S(2)}) collective-permute-start(bf16[1,8,2176]{2,1,0:T(8,128)(2,1)S(1)} %get-tuple-element.69), channel_id=1, source_target_pairs={{0,8},{1,9},{2,10},{3,11},{4,12},{5,13},{6,14},{7,15},{8,0},{9,1},... | collective-permute-start | bytes 104456 | tf_op jit(solution)/shard_map/ppermute | solution.py:313
  48.7 1.7 %collective-permute-done.13 = bf16[1,8,2176]{2,1,0:T(8,128)(2,1)S(1)} collective-permute-done((bf16[1,8,2176]{2,1,0:T(8,128)(2,1)S(1)}, bf16[1,8,2176]{2,1,0:T(8,128)(2,1)S(1)}, u32[]{:S(2)}, u32[]{:S(2)}) %collective-permute-start.13) | collective-permute-done | bytes 34848 | tf_op jit(solution)/shard_map/ppermute | solution.py:313
  50.4 0.9 %collective-permute-done.14 = bf16[1,8,2176]{2,1,0:T(8,128)(2,1)S(1)} collective-permute-done((bf16[1,8,2176]{2,1,0:T(8,128)(2,1)S(1)}, bf16[1,8,2176]{2,1,0:T(8,128)(2,1)S(1)}, u32[]{:S(2)}, u32[]{:S(2)}) %collective-permute-start.14) | collective-permute-done | bytes 34848 | tf_op jit(solution)/shard_map/ppermute | solution.py:313
  51.4 0.6 %shard_map.175 = (f32[8,768]{1,0:T(8,128)}, f32[8,256]{1,0:T(8,128)}, f32[8,768]{1,0:T(8,128)}, f32[8,384]{1,0:T(8,128)}, f32[1,8]{1,0:T(1,128)}, /*index=5*/f32[1,8]{1,0:T(1,128)}) custom-call(bf16[8,2176]{1,0:T(8,128)(2,1)S(1)} %get-tuple-element.72.refs_0_, bf16[8,2176]{1,0:T(8,128)(2,1)S(1)} %bitcast.31, bf16[8,2176]{1,0:T(8,128)(2,1)S(1)} %bitcast.32, ...), custom_call_target="tpu_custom_call" | custom-call | tf_op jit(solution)/shard_map/pallas_call | solution.py:372
  (48 shorter events, 4.0 us)
Async XLA Ops:
  2.2 7.2 %collective-permute-start = (bf16[1,8,2304]{2,1,0:T(8,128)(2,1)}, bf16[1,8,2304]{2,1,0:T(8,128)(2,1)S(1)}, u32[]{:S(2)}, u32[]{:S(2)}) collective-permute-start(bf16[1,8,2304]{2,1,0:T(8,128)(2,1)} %bitcast.38), channel_id=1, source_target_pairs={{0,24},{1,25},{2,26},{3,27},{4,28},{5,29},{6,30},{7,31},{8,16},{9,... | collective-permute-start | bytes 110600 | tf_op jit(solution)/shard_map/ppermute | solution.py:313
  7.2 5.1 %collective-permute-start.1 = (bf16[1,8,2304]{2,1,0:T(8,128)(2,1)}, bf16[1,8,2304]{2,1,0:T(8,128)(2,1)S(1)}, u32[]{:S(2)}, u32[]{:S(2)}) collective-permute-start(bf16[1,8,2304]{2,1,0:T(8,128)(2,1)} %bitcast.39), channel_id=1, source_target_pairs={{0,16},{1,17},{2,18},{3,19},{4,20},{5,21},{6,22},{7,23},{8,24},{9,... | collective-permute-start | bytes 110600 | tf_op jit(solution)/shard_map/ppermute | solution.py:313
  7.2 5.1 %collective-permute-start.2 = (bf16[1,8,2304]{2,1,0:T(8,128)(2,1)}, bf16[1,8,2304]{2,1,0:T(8,128)(2,1)S(1)}, u32[]{:S(2)}, u32[]{:S(2)}) collective-permute-start(bf16[1,8,2304]{2,1,0:T(8,128)(2,1)} %bitcast.40), channel_id=1, source_target_pairs={{0,8},{1,9},{2,10},{3,11},{4,12},{5,13},{6,14},{7,15},{8,0},{9,1},... | collective-permute-start | bytes 110600 | tf_op jit(solution)/shard_map/ppermute | solution.py:313
  12.3 7.7 %collective-permute-start.3 = (bf16[4,8,2304]{2,1,0:T(8,128)(2,1)S(1)}, bf16[4,8,2304]{2,1,0:T(8,128)(2,1)S(1)}, u32[]{:S(2)}, u32[]{:S(2)}) collective-permute-start(bf16[4,8,2304]{2,1,0:T(8,128)(2,1)S(1)} %constant_dynamic-update-slice_fusion.3), channel_id=1, source_target_pairs={{0,6},{1,7},{2,4},{3,5},{4,2},{5,3},{6,0},{7,1},{8,14},{9,15},{10,... | collective-permute-start | bytes 442376 | tf_op jit(solution)/shard_map/ppermute | solution.py:313
  14.9 6.0 %collective-permute-start.4 = (bf16[4,8,2304]{2,1,0:T(8,128)(2,1)S(1)}, bf16[4,8,2304]{2,1,0:T(8,128)(2,1)S(1)}, u32[]{:S(2)}, u32[]{:S(2)}) collective-permute-start(bf16[4,8,2304]{2,1,0:T(8,128)(2,1)S(1)} %constant_dynamic-update-slice_fusion.3), channel_id=1, source_target_pairs={{0,4},{1,5},{2,6},{3,7},{4,0},{5,1},{6,2},{7,3},{8,12},{9,13},{10,... | collective-permute-start | bytes 442376 | tf_op jit(solution)/shard_map/ppermute | solution.py:313
  15.4 5.4 %collective-permute-start.5 = (bf16[4,8,2304]{2,1,0:T(8,128)(2,1)S(1)}, bf16[4,8,2304]{2,1,0:T(8,128)(2,1)S(1)}, u32[]{:S(2)}, u32[]{:S(2)}) collective-permute-start(bf16[4,8,2304]{2,1,0:T(8,128)(2,1)S(1)} %constant_dynamic-update-slice_fusion.3), channel_id=1, source_target_pairs={{0,2},{1,3},{2,0},{3,1},{4,6},{5,7},{6,4},{7,5},{8,10},{9,11},{10,... | collective-permute-start | bytes 442376 | tf_op jit(solution)/shard_map/ppermute | solution.py:313
  20.0 2.6 %copy-start = (bf16[768,256]{1,0:T(8,128)(2,1)S(1)}, bf16[768,256]{1,0:T(8,128)(2,1)}, u32[]{:S(2)}) copy-start(bf16[768,256]{1,0:T(8,128)(2,1)} %tokens.5) | copy-start | bytes 1179652
  20.0 2.6 %copy-start.2 = (f32[128,128]{1,0:T(8,128)S(1)}, f32[128,128]{1,0:T(8,128)}, u32[]{:S(2)}) copy-start(f32[128,128]{1,0:T(8,128)} %constant.8.clone.cos) | copy-start | bytes 196612
  20.0 2.6 %copy-start.3 = (f32[128,128]{1,0:T(8,128)S(1)}, f32[128,128]{1,0:T(8,128)}, u32[]{:S(2)}) copy-start(f32[128,128]{1,0:T(8,128)} %constant.9.clone.sin) | copy-start | bytes 196612
  20.9 4.6 %copy-start.1 = (bf16[768,256]{1,0:T(8,128)(2,1)S(1)}, bf16[768,256]{1,0:T(8,128)(2,1)}, u32[]{:S(2)}) copy-start(bf16[768,256]{1,0:T(8,128)(2,1)} %cot.1) | copy-start | bytes 1179652
  21.0 1.6 %collective-permute-start.6 = (bf16[16,8,1152]{2,1,0:T(8,128)(2,1)S(1)}, bf16[16,8,1152]{2,1,0:T(8,128)(2,1)S(1)}, u32[]{:S(2)}, u32[]{:S(2)}) collective-permute-start(bf16[16,8,1152]{2,1,0:T(8,128)(2,1)S(1)} %get-tuple-element.62), channel_id=1, source_target_pairs={{0,1},{1,0},{2,3},{3,2},{4,5},{5,4},{6,7},{7,6},{8,9},{9,8},{10,11... | collective-permute-start | bytes 884744 | tf_op jit(solution)/shard_map/ppermute | solution.py:313
  21.1 4.4 %collective-permute-start.7 = (bf16[16,8,1152]{2,1,0:T(8,128)(2,1)S(1)}, bf16[16,8,1152]{2,1,0:T(8,128)(2,1)S(1)}, u32[]{:S(2)}, u32[]{:S(2)}) collective-permute-start(bf16[16,8,1152]{2,1,0:T(8,128)(2,1)S(1)} %get-tuple-element.65), channel_id=1, source_target_pairs={{0,1},{1,0},{2,3},{3,2},{4,5},{5,4},{6,7},{7,6},{8,9},{9,8},{10,11... | collective-permute-start | bytes 884744 | tf_op jit(solution)/shard_map/ppermute | solution.py:313
  32.1 1.6 %collective-permute-start.8 = (bf16[16,8,1024]{2,1,0:T(8,128)(2,1)S(1)}, bf16[16,8,1024]{2,1,0:T(8,128)(2,1)S(1)}, u32[]{:S(2)}, u32[]{:S(2)}) collective-permute-start(bf16[16,8,1024]{2,1,0:T(8,128)(2,1)S(1)} %slice_bitcast_fusion.1), channel_id=1, source_target_pairs={{0,1},{1,0},{2,3},{3,2},{4,5},{5,4},{6,7},{7,6},{8,9},{9,8},{10,11... | collective-permute-start | bytes 786440 | tf_op jit(solution)/shard_map/ppermute | solution.py:313
  32.3 1.8 %collective-permute-start.9 = (bf16[16,8,1152]{2,1,0:T(8,128)(2,1)S(1)}, bf16[16,8,1152]{2,1,0:T(8,128)(2,1)S(1)}, u32[]{:S(2)}, u32[]{:S(2)}) collective-permute-start(bf16[16,8,1152]{2,1,0:T(8,128)(2,1)S(1)} %slice_bitcast_fusion), channel_id=1, source_target_pairs={{0,1},{1,0},{2,3},{3,2},{4,5},{5,4},{6,7},{7,6},{8,9},{9,8},{10,11... | collective-permute-start | bytes 884744 | tf_op jit(solution)/shard_map/ppermute | solution.py:313
  34.2 6.5 %collective-permute-start.12 = (bf16[4,8,2176]{2,1,0:T(8,128)(2,1)S(1)}, bf16[4,8,2176]{2,1,0:T(8,128)(2,1)S(1)}, u32[]{:S(2)}, u32[]{:S(2)}) collective-permute-start(bf16[4,8,2176]{2,1,0:T(8,128)(2,1)S(1)} %get-tuple-element.67), channel_id=1, source_target_pairs={{0,2},{1,3},{2,0},{3,1},{4,6},{5,7},{6,4},{7,5},{8,10},{9,11},{10,... | collective-permute-start | bytes 417800 | tf_op jit(solution)/shard_map/ppermute | solution.py:313
  35.7 8.5 %collective-permute-start.11 = (bf16[4,8,2176]{2,1,0:T(8,128)(2,1)S(1)}, bf16[4,8,2176]{2,1,0:T(8,128)(2,1)S(1)}, u32[]{:S(2)}, u32[]{:S(2)}) collective-permute-start(bf16[4,8,2176]{2,1,0:T(8,128)(2,1)S(1)} %get-tuple-element.68), channel_id=1, source_target_pairs={{0,4},{1,5},{2,6},{3,7},{4,0},{5,1},{6,2},{7,3},{8,12},{9,13},{10,... | collective-permute-start | bytes 417800 | tf_op jit(solution)/shard_map/ppermute | solution.py:313
  36.5 7.7 %collective-permute-start.10 = (bf16[4,8,2176]{2,1,0:T(8,128)(2,1)S(1)}, bf16[4,8,2176]{2,1,0:T(8,128)(2,1)S(1)}, u32[]{:S(2)}, u32[]{:S(2)}) collective-permute-start(bf16[4,8,2176]{2,1,0:T(8,128)(2,1)S(1)} %get-tuple-element.66), channel_id=1, source_target_pairs={{0,6},{1,7},{2,4},{3,5},{4,2},{5,3},{6,0},{7,1},{8,14},{9,15},{10,... | collective-permute-start | bytes 417800 | tf_op jit(solution)/shard_map/ppermute | solution.py:313
  40.2 11.1 %copy-start.4 = (bf16[8,768]{1,0:T(8,128)(2,1)S(1)}, bf16[8,768]{1,0:T(8,128)(2,1)}, u32[]{:S(2)}) copy-start(bf16[8,768]{1,0:T(8,128)(2,1)} %refs_4_.1) | copy-start | bytes 36868
  40.2 11.1 %copy-start.5 = (bf16[8,768]{1,0:T(8,128)(2,1)S(1)}, bf16[8,768]{1,0:T(8,128)(2,1)}, u32[]{:S(2)}) copy-start(bf16[8,768]{1,0:T(8,128)(2,1)} %refs_5_.1) | copy-start | bytes 36868
  40.2 11.1 %copy-start.7 = (bf16[8]{0:T(256)(128)(2,1)S(1)}, bf16[8]{0:T(256)(128)(2,1)}, u32[]{:S(2)}) copy-start(bf16[8]{0:T(256)(128)(2,1)} %param.17) | copy-start | bytes 52
  40.2 11.1 %copy-start.8 = (bf16[8]{0:T(256)(128)(2,1)S(1)}, bf16[8]{0:T(256)(128)(2,1)}, u32[]{:S(2)}) copy-start(bf16[8]{0:T(256)(128)(2,1)} %param.18) | copy-start | bytes 52
  44.3 6.1 %collective-permute-start.13 = (bf16[1,8,2176]{2,1,0:T(8,128)(2,1)S(1)}, bf16[1,8,2176]{2,1,0:T(8,128)(2,1)S(1)}, u32[]{:S(2)}, u32[]{:S(2)}) collective-permute-start(bf16[1,8,2176]{2,1,0:T(8,128)(2,1)S(1)} %get-tuple-element.71), channel_id=1, source_target_pairs={{0,24},{1,25},{2,26},{3,27},{4,28},{5,29},{6,30},{7,31},{8,16},{9,... | collective-permute-start | bytes 104456 | tf_op jit(solution)/shard_map/ppermute | solution.py:313
  46.1 5.2 %collective-permute-start.14 = (bf16[1,8,2176]{2,1,0:T(8,128)(2,1)S(1)}, bf16[1,8,2176]{2,1,0:T(8,128)(2,1)S(1)}, u32[]{:S(2)}, u32[]{:S(2)}) collective-permute-start(bf16[1,8,2176]{2,1,0:T(8,128)(2,1)S(1)} %get-tuple-element.70), channel_id=1, source_target_pairs={{0,16},{1,17},{2,18},{3,19},{4,20},{5,21},{6,22},{7,23},{8,24},{9,... | collective-permute-start | bytes 104456 | tf_op jit(solution)/shard_map/ppermute | solution.py:313
  46.4 5.0 %collective-permute-start.15 = (bf16[1,8,2176]{2,1,0:T(8,128)(2,1)S(1)}, bf16[1,8,2176]{2,1,0:T(8,128)(2,1)S(1)}, u32[]{:S(2)}, u32[]{:S(2)}) collective-permute-start(bf16[1,8,2176]{2,1,0:T(8,128)(2,1)S(1)} %get-tuple-element.69), channel_id=1, source_target_pairs={{0,8},{1,9},{2,10},{3,11},{4,12},{5,13},{6,14},{7,15},{8,0},{9,1},... | collective-permute-start | bytes 104456 | tf_op jit(solution)/shard_map/ppermute | solution.py:313
  (1 other events, 2.6 us)

commit v5 on v4

--- a/solution.py
+++ b/solution.py
@@ -119,16 +119,6 @@
     )
 
 
-def slot_order(hops, rows, me, slot_axis):
-    slots = lax.broadcasted_iota(jnp.int32, (D, D), slot_axis)
-    place = slots // rows
-    owner = jnp.full((D, D), me, jnp.int32)
-    for bit, mask in enumerate(hops):
-        owner = owner ^ (((place >> bit) & 1) * mask)
-    found = owner * rows + slots % rows == lax.broadcasted_iota(jnp.int32, (D, D), 1 - slot_axis)
-    return jnp.where(found, 1.0, 0.0).astype(bf16)
-
-
 def head_masks():
     lane = lax.broadcasted_iota(jnp.int32, (1, D), 1)
     spread = [jnp.where((lane % HALF) // 32 == h, 1.0, 0.0).astype(bf16) for h in range(HEADS)]
@@ -142,25 +132,27 @@
     return jnp.concatenate(live, axis=0) > 0.5
 
 
+def early_kernel(lengths, tokens, cot, hat, out_low):
+    hat[...] = standardize(tokens[...].astype(f32))[0]
+    live = live_rows(lengths, tokens.shape[0])
+    out_low[...] = jnp.where(live, cot[...].astype(f32), 0.0).astype(bf16)
+
+
 def attend_kernel(
-    hops, rows, me, lengths, tokens, packed, other, cos, sin, weights, w_attn, gains, normed, heads, shares, mixture
+    lengths, hat, packed, cos, sin, gains, normed, heads, shares, mixture
 ):
-    order = slot_order(hops, rows, me[0], 1)
-    ordered = mm(order[:, : D // 2], packed[...]) + mm(order[:, D // 2 :], other[...])
-    weights[...] = ordered[:, :QKV].astype(bf16)
-    w_attn[...] = ordered[:, QKV : QKV + D].astype(bf16)
+    w_qkv = packed[:, :QKV]
     here = lax.broadcasted_iota(jnp.int32, (D, D), 0) == lax.broadcasted_iota(jnp.int32, (D, D), 1)
     for k in range(2):
-        column = ordered[:, QKV + D + k : QKV + D + k + 1]
+        column = packed[:, QKV + D + k : QKV + D + k + 1].astype(f32)
         gains[k : k + 1, :] = jnp.sum(jnp.where(here, column, 0.0), axis=0, keepdims=True)
     gain = gains[0:1, :]
-    w_qkv = weights[...]
     c, s = cos[...], sin[...]
     spread_masks, plain_masks = head_masks()
     key_lane = lax.broadcasted_iota(jnp.int32, (1, BLOCK), 1)
-    count = tokens.shape[0] // BLOCK
+    count = hat.shape[0] // BLOCK
     for part in [slice(b * BLOCK, (b + 1) * BLOCK) for b in range(count)]:
-        normed[part] = (standardize(tokens[part].astype(f32))[0] * gain).astype(bf16)
+        normed[part] = (hat[part] * gain).astype(bf16)
 
     def rope(base):
         both = mm(normed[...], w_qkv[:, base : base + D])
@@ -187,15 +179,12 @@
 
 
 def feed_kernel(
-    hops, rows, me, lengths, tokens, cot, packed, other, attn, gains, mixture,
-    w_mlp, middle, hidden, d_middle, d_mixture, g_attn, sums, hat_two_low, out_low, d_att, d_merged,
+    tokens, out_low, first, second, gains, mixture,
+    middle, hidden, d_middle, d_mixture, g_attn, sums, hat_two_low, d_att, d_merged,
 ):
-    order = slot_order(hops, rows, me[0], 1)
-    ordered = mm(order[:, : D // 2], packed[...]) + mm(order[:, D // 2 :], other[...])
-    ordered = ordered.astype(bf16)
-    w_attn = attn[...]
-    w_in = ordered[:, : 2 * FF]
-    w_mlp[...] = ordered[:, 2 * FF :]
+    w_attn = first[:, QKV : QKV + D]
+    w_in = second[:, : 2 * FF]
+    w_mlp = second[:, 2 * FF :]
     gain = gains[1:2, :]
     mid = tokens[...].astype(f32) + mm(mixture[...], w_attn)
     middle[...] = mid
@@ -208,9 +197,8 @@
     curved = inner * cdf
     slope = cdf + inner * jnp.exp(-0.5 * inner * inner) * 0.3989422804014327
     hidden[...] = (curved * gate).astype(bf16)
-    out_grad = jnp.where(live_rows(lengths, tokens.shape[0]), cot[...].astype(f32), 0.0)
-    out_low[...] = out_grad.astype(bf16)
-    d_hidden = mm(out_low[...], w_mlp[...])
+    out_grad = out_low[...].astype(f32)
+    d_hidden = mm(out_low[...], w_mlp)
     d_merged[:, :FF] = (d_hidden * gate * slope).astype(bf16)
     d_merged[:, FF:] = (d_hidden * curved).astype(bf16)
     d_normed = mm_nt(d_merged[...], w_in)
@@ -218,16 +206,13 @@
     d_middle[...] = d_mid
     d_att[...] = d_mid.astype(bf16)
     d_mixture[...] = mm_nt(d_att[...], w_attn).astype(bf16)
-    order = slot_order(hops, rows, me[0], 0)
-    total = mm_tn(hat_two_low[...], d_merged[...]).astype(bf16)
-    sums[:, : 2 * FF] = mm(order, total).astype(bf16)
-    total = mm_tn(out_low[...], hidden[...]).astype(bf16)
-    sums[:, 2 * FF :] = mm(order, total).astype(bf16)
+    sums[:, : 2 * FF] = mm_tn(hat_two_low[...], d_merged[...]).astype(bf16)
+    sums[:, 2 * FF :] = mm_tn(out_low[...], hidden[...]).astype(bf16)
     g_attn[...] = mm_tn(mixture[...], d_att[...]).astype(bf16)
 
 
 def attend_back_kernel(
-    hops, rows, me, heads, shares, d_mixture, normed, g_attn, cos, sin, sums, d_qkv
+    heads, shares, d_mixture, normed, g_attn, cos, sin, sums, d_qkv
 ):
     c, s = cos[...], sin[...]
     spread_masks, plain_masks = head_masks()
@@ -254,22 +239,20 @@
         d_qkv[block, :D] = rope_back(mm(d_score, stack_heads(heads[block, D : 2 * D], spread_masks)) * HEAD_DIM ** (-0.5))
     for block, d_score in zip(parts, d_scores):
         d_qkv[block, D : 2 * D] = rope_back(mm(turn_heads(d_score), stack_heads(heads[block, :D], spread_masks)))
-    order = slot_order(hops, rows, me[0], 0)
     total = mm_tn(normed[...], d_qkv[...]).astype(bf16)
-    placed = mm(order, total).astype(bf16)
     spread = spread_columns(False)
-    sums[:, :D] = mm(placed[:, :D], spread).astype(bf16)
-    sums[:, D : 2 * D] = mm(placed[:, D : 2 * D], spread).astype(bf16)
-    sums[:, 2 * D : QKV] = placed[:, 2 * D :]
-    sums[:, QKV:] = mm(order, g_attn[...]).astype(bf16)
-
-
-def outputs_kernel(lengths, tokens, weights, gains, d_qkv, d_middle, middle, hidden, w_mlp, out, grad):
+    sums[:, :D] = mm(total[:, :D], spread).astype(bf16)
+    sums[:, D : 2 * D] = mm(total[:, D : 2 * D], spread).astype(bf16)
+    sums[:, 2 * D : QKV] = total[:, 2 * D :]
+    sums[:, QKV:] = g_attn[...]
+
+
+def outputs_kernel(lengths, tokens, first, second, gains, d_qkv, d_middle, middle, hidden, out, grad):
     gain = gains[0:1, :]
-    result = middle[...] + mm_nt(hidden[...], w_mlp[...])
+    result = middle[...] + mm_nt(hidden[...], second[:, 2 * FF :])
     out[...] = jnp.where(live_rows(lengths, tokens.shape[0]), result, 0.0).astype(bf16)
     hat_one, inv_one = standardize(tokens[...].astype(f32))
-    d_normed = mm_nt(d_qkv[...], weights[...])
+    d_normed = mm_nt(d_qkv[...], first[:, :QKV])
     grad[...] = d_middle[...] + norm_back(d_normed * gain, hat_one, inv_one)
 
 
@@ -288,8 +271,13 @@
     )
 
 
-def put(room, piece, slot, column=0):
-    return lax.dynamic_update_slice(room, piece, (slot, 0, column))
+def put(room, piece, place, column=0):
+    return lax.dynamic_update_slice(room, piece[:, None], (0, place, 0, column))
+
+
+def cut(room, place, ways):
+    room = room.reshape(-1, ways, *room.shape[1:])
+    return lax.dynamic_index_in_dim(room, place, 1, keepdims=False)
 
 
 def on_device(n, tokens, lengths, w_qkv, w_attn, w_in, w_mlp, gain_attn, gain_mlp, cotangent):
@@ -300,12 +288,14 @@
         hops.append(n >> (len(hops) + 1))
     hops = tuple(hops)
     lead = hops[:-1]
+    me = lax.axis_index("dp")
+    core = me & 1
     rounds = []
     if len(lead) % 2:
-        rounds.append(((lead[0], 1),))
+        rounds.append((me // lead[0], ((lead[0], 1),)))
     for k in range(len(lead) % 2, len(lead), 2):
         one, two = lead[k], lead[k + 1]
-        rounds.append(((one ^ two, 3), (one, 1), (two, 2)))
+        rounds.append(((me // two) & 3, ((one ^ two, 3), (one, 2), (two, 1))))
     gain_attn = gain_attn.reshape(1, rows)
     gain_mlp = gain_mlp.reshape(1, rows)
 
@@ -316,54 +306,59 @@
         pack_kernel, out_specs=NEAR, out_shape=jax.ShapeDtypeStruct((rows, FIRST + SECOND), bf16)
     )(w_qkv, w_attn, w_in, w_mlp.T, gain_attn, gain_mlp)
     room = held[None]
-    for partners in rounds:
-        size = room.shape[0]
-        got = [(trade(room, mask), place) for mask, place in partners]
-        room = put(jnp.zeros((size * (len(got) + 1), rows, FIRST + SECOND), bf16), room, 0)
-        for piece, place in got:
-            room = put(room, piece, size * place)
-    first, second = room[:, :, :FIRST], room[:, :, FIRST:]
-    first_got, second_got = trade(first, 1), trade(second, 1)
-    first = first.reshape(D // 2, FIRST), first_got.reshape(D // 2, FIRST)
-    second = second.reshape(D // 2, SECOND), second_got.reshape(D // 2, SECOND)
+    for place, partners in rounds:
+        got = [(trade(room, mask), other) for mask, other in partners]
+        wide = put(jnp.zeros((room.shape[0], len(got) + 1, rows, FIRST + SECOND), bf16), room, place)
+        for piece, other in got:
+            wide = put(wide, piece, place ^ other)
+        room = wide.reshape(-1, rows, FIRST + SECOND)
+        if place is rounds[0][0]:
+            early = lax.optimization_barrier((room, tokens, cotangent))
+            room = early[0]
+            hat, out_low = call(
+                early_kernel, [SMALL] + [NEAR] * 2, [((count, D), f32), ((count, D), bf16)]
+            )(lengths, *early[1:])
+    room, hat, out_low = lax.optimization_barrier((room, hat, out_low))
+
+    def both(half):
+        wide = put(jnp.zeros((n // 2, 2) + half.shape[1:], bf16), half, core)
+        return put(wide, trade(half, 1), core ^ 1).reshape(D, half.shape[2])
+
+    first, second = both(room[:, :, :FIRST]), both(room[:, :, FIRST:])
 
     cos, sin = tables()
     cos, sin = jnp.asarray(cos), jnp.asarray(sin)
-    me = lax.axis_index("dp").astype(jnp.int32).reshape(1)
-    weights, attn, gains, normed, heads, shares, mixture = call(
-        functools.partial(attend_kernel, hops, rows),
-        [SMALL] * 2 + [NEAR] * 5,
-        [((D, QKV), bf16), ((D, D), bf16), ((2, D), f32), ((count, D), bf16), ((count, QKV), bf16), ((count, WIDE), f32), ((count, D), bf16)],
-    )(me, lengths, tokens, *first, cos, sin)
-    w_mlp_all, middle, hidden, d_middle, d_mixture, g_attn, second_sums = call(
-        functools.partial(feed_kernel, hops, rows),
-        [SMALL] * 2 + [NEAR] * 7,
-        [((D, FF), bf16), ((count, D), f32), ((count, FF), bf16), ((count, D), f32), ((count, D), bf16), ((D, D), bf16), ((D, 3 * FF), bf16)],
-        [((count, D), bf16), ((count, D), bf16), ((count, D), bf16), ((count, 2 * FF), bf16)],
-    )(me, lengths, tokens, cotangent, *second, attn, gains, mixture)
+    gains, normed, heads, shares, mixture = call(
+        attend_kernel,
+        [SMALL] + [NEAR] * 4,
+        [((2, D), f32), ((count, D), bf16), ((count, QKV), bf16), ((count, WIDE), f32), ((count, D), bf16)],
+    )(lengths, hat, first, cos, sin)
+    middle, hidden, d_middle, d_mixture, g_attn, second_sums = call(
+        feed_kernel,
+        [NEAR] * 6,
+        [((count, D), f32), ((count, FF), bf16), ((count, D), f32), ((count, D), bf16), ((D, D), bf16), ((D, 3 * FF), bf16)],
+        [((count, D), bf16), ((count, D), bf16), ((count, 2 * FF), bf16)],
+    )(tokens, out_low, first, second, gains, mixture)
     first_sums, d_qkv = call(
-        functools.partial(attend_back_kernel, hops, rows),
-        [SMALL] + [NEAR] * 7,
-        [((D, SUMS), bf16), ((count, QKV), bf16)],
-    )(me, heads, shares, d_mixture, normed, g_attn, cos, sin)
+        attend_back_kernel, [NEAR] * 7, [((D, SUMS), bf16), ((count, QKV), bf16)]
+    )(heads, shares, d_mixture, normed, g_attn, cos, sin)
     out, grad = call(
         outputs_kernel, [SMALL] + [NEAR] * 8, [((count, D), bf16), ((count, D), f32)]
-    )(lengths, tokens, weights, gains, d_qkv, d_middle, middle, hidden, w_mlp_all)
-
-    def halve(kept, mask):
-        half = kept.shape[0] // 2
-        got = trade(kept[half:], mask)
-        return (kept[:half].astype(f32) + got.astype(f32)).astype(bf16)
-
-    first, second = first_sums.reshape(n, rows, SUMS), second_sums.reshape(n, rows, 3 * FF)
-    first, second = halve(first, 1), halve(second, 1)
-    kept = put(put(jnp.zeros((n // 2, rows, SUMS + 3 * FF), bf16), first, 0), second, 0, SUMS)
-    for k, partners in enumerate(rounds[::-1]):
-        size = kept.shape[0] // (len(partners) + 1)
-        got = [trade(kept[size * place : size * (place + 1)], mask) for mask, place in partners]
+    )(lengths, tokens, first, second, gains, d_qkv, d_middle, middle, hidden)
+
+    def halve(sums):
+        sums = sums.reshape(n, rows, sums.shape[1])
+        got = trade(cut(sums, core ^ 1, 2), 1)
+        return (cut(sums, core, 2).astype(f32) + got.astype(f32)).astype(bf16)
+
+    kept = jnp.concatenate([halve(first_sums), halve(second_sums)], axis=2)
+    for k, (place, partners) in enumerate(rounds[::-1]):
+        ways = len(partners) + 1
+        got = [trade(cut(kept, place ^ other, ways), mask) for mask, other in partners]
+        kept = cut(kept, place, ways)
         if k == len(rounds) - 1:
             break
-        total = kept[:size].astype(f32)
+        total = kept.astype(f32)
         for piece in got:
             total = total + piece.astype(f32)
         kept = total.astype(bf16)

time: 52.2 us -> 50.6 us (0.969)
  waiting for transfers between devices: 17.4 us -> 16.2 us
  Pallas kernels: 14 us -> 13.3 us
    ppermute x16, waiting for transfers between devices: 17.4 us -> 16.2 us  [trade(): return lax.ppermute(values, 'dp', [(i, i ^ mask) for i in range(n)])]
    pallas_call x3 -> x4, Pallas kernels: 9.36 us -> 8.59 us  [the longest x1 3.07 us: on_device(): call(feed_kernel, [NEAR] * 6, [((count, D), f32), ((count, FF), bf16), ((...]
  transfers between devices with their start and end apart: 16 -> 16, of which waited for: 11 -> 11; matrix products, arithmetic and copies ran while one was open for 2% -> 2% of each run, Pallas kernels for 10% -> 11%
where the time goes in v5:
time: 50.6 us; the launch traced here: 50.4 us
  starting transfers between devices  18.4 us (36%)
  waiting for transfers between devices  16.2 us (32%)
  Pallas kernels  13.3 us (26%)
  local copies, waits for them, and re-layouts  1.37 us (3%)
  between operations  0.93 us (2%)
    ppermute x16, starting transfers between devices, trade(): return lax.ppermute(values, 'dp', [(i, i ^ mask) for i in range(n)])  18.4 us
    ppermute x16, waiting for transfers between devices, trade(): return lax.ppermute(values, 'dp', [(i, i ^ mask) for i in range(n)])  16.2 us
    pallas_call x1, Pallas kernels, on_device(): call(feed_kernel, [NEAR] * 6, [((count, D), f32), ((count, FF), bf16), ((...  3.07 us
    pallas_call x1, Pallas kernels, on_device(): call(outputs_kernel, [SMALL] + [NEAR] * 8, [((count, D), bf16), ((count,...  2.44 us
    pallas_call x1, Pallas kernels, on_device(): call(attend_back_kernel, [NEAR] * 7, [((D, SUMS), bf16), ((count, QKV), b...  2.27 us
    pallas_call x1, Pallas kernels, on_device(): call(attend_kernel, [SMALL] + [NEAR] * 4, [((2, D), f32), ((count, D), bf...  2.26 us
    pallas_call x1, Pallas kernels, on_device(): pl.pallas_call(pack_kernel, out_specs=NEAR, out_shape=jax.ShapeDtypeStruc...  1.62 us
    dynamic_update_slice x12, local copies, waits for them, and re-layouts, put(): return lax.dynamic_update_slice(room, piece[:, None], (0, place, 0, column))  1.01 us
  transfers between devices with their start and end apart: 16, of which 11 were waited for; matrix products, arithmetic and copies ran while one was open for 2% of the time, Pallas kernels for 11%

profile of v5, /device:TPU:0, one launch (start us, length us, event | category | flops | bytes accessed | tf_op | source)
XLA Modules:
  0.0 50.4 jit_solution(5373783917570040479)
XLA Ops:
  0.7 1.6 %shard_map.170 = bf16[8,2304]{1,0:T(8,128)(2,1)} custom-call(bf16[8,768]{1,0:T(8,128)(2,1)} %refs_4_.1, bf16[8,256]{1,0:T(8,128)(2,1)} %w_attn.1, bf16[8,768]{1,0:T(8,128)(2,1)} %refs_5_.1, bf16[8,384]{1,0:T(8,128)(2,1)} %bitcast.90, bf16[1,8]{1,0:T(2,128)(2,1)} %bitcast.78, bf16[1,8]{1,0:T(2,128)(2,1)} %bitcast.80), custom_call_target="tpu_custom_call" | custom-call | tf_op jit(solution)/shard_map/pallas_call | solution.py:305
  2.3 5.0 %collective-permute-start = (bf16[1,8,2304]{2,1,0:T(8,128)(2,1)}, bf16[1,8,2304]{2,1,0:T(8,128)(2,1)S(1)}, u32[]{:S(2)}, u32[]{:S(2)}) collective-permute-start(bf16[1,8,2304]{2,1,0:T(8,128)(2,1)} %bitcast.87), channel_id=1, source_target_pairs={{0,24},{1,25},{2,26},{3,27},{4,28},{5,29},{6,30},{7,31},{8,16},{9,... | collective-permute-start | bytes 110600 | tf_op jit(solution)/shard_map/ppermute | solution.py:303
  7.9 0.8 %constant_dynamic-update-slice_fusion.3 = bf16[4,8,2304]{2,1,0:T(8,128)(2,1)S(1)} fusion(bf16[4,8,2304]{2,1,0:T(8,128)(2,1)S(1)} %reshape.79, s32[]{:T(128)S(6)} %select_n.57, bf16[8,2304]{1,0:T(8,128)(2,1)} %shard_map.170), kind=kLoop, calls=%fused_computation.29 | loop fusion | bytes 73732 | tf_op jit(solution)/shard_map/dynamic_update_slice | solution.py:275
  8.7 0.8 %collective-permute-done = bf16[1,8,2304]{2,1,0:T(8,128)(2,1)S(1)} collective-permute-done((bf16[1,8,2304]{2,1,0:T(8,128)(2,1)}, bf16[1,8,2304]{2,1,0:T(8,128)(2,1)S(1)}, u32[]{:S(2)}, u32[]{:S(2)}) %collective-permute-start) | collective-permute-done | bytes 36896 | tf_op jit(solution)/shard_map/ppermute | solution.py:303
  9.5 2.9 %collective-permute-done.1 = bf16[1,8,2304]{2,1,0:T(8,128)(2,1)S(1)} collective-permute-done((bf16[1,8,2304]{2,1,0:T(8,128)(2,1)}, bf16[1,8,2304]{2,1,0:T(8,128)(2,1)S(1)}, u32[]{:S(2)}, u32[]{:S(2)}) %collective-permute-start.1) | collective-permute-done | bytes 36896 | tf_op jit(solution)/shard_map/ppermute | solution.py:303
  12.4 2.5 %collective-permute-start.3 = (bf16[4,8,2304]{2,1,0:T(8,128)(2,1)S(1)}, bf16[4,8,2304]{2,1,0:T(8,128)(2,1)S(1)}, u32[]{:S(2)}, u32[]{:S(2)}) collective-permute-start(bf16[4,8,2304]{2,1,0:T(8,128)(2,1)S(1)} %constant_dynamic-update-slice_fusion), channel_id=1, source_target_pairs={{0,6},{1,7},{2,4},{3,5},{4,2},{5,3},{6,0},{7,1},{8,14},{9,15},{10,... | collective-permute-start | bytes 442376 | tf_op jit(solution)/shard_map/ppermute | solution.py:303
  16.1 1.0 %shard_map.171 = (f32[768,256]{1,0:T(8,128)S(1)}, bf16[768,256]{1,0:T(8,128)(2,1)S(1)}) custom-call(s32[6]{0:T(128)S(1)} %copy-done.6, bf16[768,256]{1,0:T(8,128)(2,1)S(1)} %copy-done, bf16[768,256]{1,0:T(8,128)(2,1)S(1)} %copy-done.1), custom_call_target="tpu_custom_call" | custom-call | tf_op jit(solution)/shard_map/pallas_call | solution.py:318
  17.1 3.0 %collective-permute-done.3 = bf16[4,8,2304]{2,1,0:T(8,128)(2,1)S(1)} collective-permute-done((bf16[4,8,2304]{2,1,0:T(8,128)(2,1)S(1)}, bf16[4,8,2304]{2,1,0:T(8,128)(2,1)S(1)}, u32[]{:S(2)}, u32[]{:S(2)}) %collective-permute-start.3) | collective-permute-done | bytes 147488 | tf_op jit(solution)/shard_map/ppermute | solution.py:303
  20.1 0.8 %collective-permute-done.4 = bf16[4,8,2304]{2,1,0:T(8,128)(2,1)S(1)} collective-permute-done((bf16[4,8,2304]{2,1,0:T(8,128)(2,1)S(1)}, bf16[4,8,2304]{2,1,0:T(8,128)(2,1)S(1)}, u32[]{:S(2)}, u32[]{:S(2)}) %collective-permute-start.4) | collective-permute-done | bytes 147488 | tf_op jit(solution)/shard_map/ppermute | solution.py:303
  21.8 0.9 %collective-permute-done.6 = bf16[16,8,1152]{2,1,0:T(8,128)(2,1)S(1)} collective-permute-done((bf16[16,8,1152]{2,1,0:T(8,128)(2,1)S(1)}, bf16[16,8,1152]{2,1,0:T(8,128)(2,1)S(1)}, u32[]{:S(2)}, u32[]{:S(2)}) %collective-permute-start.6) | collective-permute-done | bytes 294944 | tf_op jit(solution)/shard_map/ppermute | solution.py:303
  22.7 2.3 %shard_map.172 = (f32[2,256]{1,0:T(2,128)S(1)}, bf16[768,256]{1,0:T(8,128)(2,1)S(1)}, bf16[768,768]{1,0:T(8,128)(2,1)S(1)}, f32[768,512]{1,0:T(8,128)S(1)}, bf16[768,256]{1,0:T(8,128)(2,1)S(1)}) custom-call(s32[6]{0:T(128)S(1)} %copy-done.6, f32[768,256]{1,0:T(8,128)S(1)} %get-tuple-element.45.hat, bf16[256,1152]{1,0:T(8,128)(2,1)S(1)} %bitcast.66, ...), custom_call_target="tpu_custom_call" | custom-call | tf_op jit(solution)/shard_map/pallas_call | solution.py:331
  25.0 3.1 %shard_map.173 = (f32[768,256]{1,0:T(8,128)S(1)}, bf16[768,384]{1,0:T(8,128)(2,1)S(1)}, f32[768,256]{1,0:T(8,128)S(1)}, bf16[768,256]{1,0:T(8,128)(2,1)S(1)}, bf...) custom-call(bf16[768,256]{1,0:T(8,128)(2,1)S(1)} %copy-done, bf16[768,256]{1,0:T(8,128)(2,1)S(1)} %get-tuple-element.49.out_low, ...), custom_call_target="tpu_custom_call" | custom-call | tf_op jit(solution)/shard_map/pallas_call | solution.py:336
  28.1 2.3 %shard_map.174 = (bf16[256,1024]{1,0:T(8,128)(2,1)S(1)}, bf16[768,768]{1,0:T(8,128)(2,1)S(1)}) custom-call(bf16[768,768]{1,0:T(8,128)(2,1)S(1)} %get-tuple-element.47.heads, f32[768,512]{1,0:T(8,128)S(1)} %get-tuple-element.48.shares, bf16[768,256]{1,0:T(8,128)(2,1)S(1)} %get-tuple-element.52.d_mixture, bf16[768,256]{1,0:T(8,128)(2,1)S(1)} %get-tuple-element.53.normed, ...), custom_call_target="tpu_custom_call" | custom-call | tf_op jit(solution)/shard_map/pallas_call | solution.py:342
  31.1 0.9 %collective-permute-done.8 = bf16[16,8,1024]{2,1,0:T(8,128)(2,1)S(1)} collective-permute-done((bf16[16,8,1024]{2,1,0:T(8,128)(2,1)S(1)}, bf16[16,8,1024]{2,1,0:T(8,128)(2,1)S(1)}, u32[]{:S(2)}, u32[]{:S(2)}) %collective-permute-start.8) | collective-permute-done | bytes 262176 | tf_op jit(solution)/shard_map/ppermute | solution.py:303
  32.6 1.5 %collective-permute-start.12 = (bf16[4,8,2176]{2,1,0:T(8,128)(2,1)S(1)}, bf16[4,8,2176]{2,1,0:T(8,128)(2,1)S(1)}, u32[]{:S(2)}, u32[]{:S(2)}) collective-permute-start(bf16[4,8,2176]{2,1,0:T(8,128)(2,1)S(1)} %get-tuple-element.75), channel_id=1, source_target_pairs={{0,2},{1,3},{2,0},{3,1},{4,6},{5,7},{6,4},{7,5},{8,10},{9,11},{10,... | collective-permute-start | bytes 417800 | tf_op jit(solution)/shard_map/ppermute | solution.py:303
  34.1 0.7 %collective-permute-start.11 = (bf16[4,8,2176]{2,1,0:T(8,128)(2,1)S(1)}, bf16[4,8,2176]{2,1,0:T(8,128)(2,1)S(1)}, u32[]{:S(2)}, u32[]{:S(2)}) collective-permute-start(bf16[4,8,2176]{2,1,0:T(8,128)(2,1)S(1)} %get-tuple-element.76), channel_id=1, source_target_pairs={{0,4},{1,5},{2,6},{3,7},{4,0},{5,1},{6,2},{7,3},{8,12},{9,13},{10,... | collective-permute-start | bytes 417800 | tf_op jit(solution)/shard_map/ppermute | solution.py:303
  34.8 1.4 %collective-permute-start.10 = (bf16[4,8,2176]{2,1,0:T(8,128)(2,1)S(1)}, bf16[4,8,2176]{2,1,0:T(8,128)(2,1)S(1)}, u32[]{:S(2)}, u32[]{:S(2)}) collective-permute-start(bf16[4,8,2176]{2,1,0:T(8,128)(2,1)S(1)} %get-tuple-element.74), channel_id=1, source_target_pairs={{0,6},{1,7},{2,4},{3,5},{4,2},{5,3},{6,0},{7,1},{8,14},{9,15},{10,... | collective-permute-start | bytes 417800 | tf_op jit(solution)/shard_map/ppermute | solution.py:303
  36.2 2.4 %shard_map.175 = (bf16[768,256]{1,0:T(8,128)(2,1)}, f32[768,256]{1,0:T(8,128)}) custom-call(s32[6]{0:T(128)S(1)} %copy-done.6, bf16[768,256]{1,0:T(8,128)(2,1)S(1)} %copy-done, bf16[256,1152]{1,0:T(8,128)(2,1)S(1)} %bitcast.68, bf16[256,1152]{1,0:T(8,128)(2,1)S(1)} %bitcast.70, f32[2,256]{1,0:T(2,128)S(1)} %get-tuple-element.50.gains, ...), custom_call_target="tpu_custom_call" | custom-call | tf_op jit(solution)/shard_map/pallas_call | solution.py:345
  39.1 3.5 %collective-permute-done.11 = bf16[4,8,2176]{2,1,0:T(8,128)(2,1)S(1)} collective-permute-done((bf16[4,8,2176]{2,1,0:T(8,128)(2,1)S(1)}, bf16[4,8,2176]{2,1,0:T(8,128)(2,1)S(1)}, u32[]{:S(2)}, u32[]{:S(2)}) %collective-permute-start.11) | collective-permute-done | bytes 139296 | tf_op jit(solution)/shard_map/ppermute | solution.py:303
  42.7 1.8 %collective-permute-start.13 = (bf16[1,8,2176]{2,1,0:T(8,128)(2,1)S(1)}, bf16[1,8,2176]{2,1,0:T(8,128)(2,1)S(1)}, u32[]{:S(2)}, u32[]{:S(2)}) collective-permute-start(bf16[1,8,2176]{2,1,0:T(8,128)(2,1)S(1)} %get-tuple-element.79), channel_id=1, source_target_pairs={{0,24},{1,25},{2,26},{3,27},{4,28},{5,29},{6,30},{7,31},{8,16},{9,... | collective-permute-start | bytes 104456 | tf_op jit(solution)/shard_map/ppermute | solution.py:303
  44.8 2.4 %collective-permute-start.15 = (bf16[1,8,2176]{2,1,0:T(8,128)(2,1)S(1)}, bf16[1,8,2176]{2,1,0:T(8,128)(2,1)S(1)}, u32[]{:S(2)}, u32[]{:S(2)}) collective-permute-start(bf16[1,8,2176]{2,1,0:T(8,128)(2,1)S(1)} %get-tuple-element.77), channel_id=1, source_target_pairs={{0,8},{1,9},{2,10},{3,11},{4,12},{5,13},{6,14},{7,15},{8,0},{9,1},... | collective-permute-start | bytes 104456 | tf_op jit(solution)/shard_map/ppermute | solution.py:303
  47.2 1.7 %collective-permute-done.13 = bf16[1,8,2176]{2,1,0:T(8,128)(2,1)S(1)} collective-permute-done((bf16[1,8,2176]{2,1,0:T(8,128)(2,1)S(1)}, bf16[1,8,2176]{2,1,0:T(8,128)(2,1)S(1)}, u32[]{:S(2)}, u32[]{:S(2)}) %collective-permute-start.13) | collective-permute-done | bytes 34848 | tf_op jit(solution)/shard_map/ppermute | solution.py:303
  48.8 0.9 %collective-permute-done.14 = bf16[1,8,2176]{2,1,0:T(8,128)(2,1)S(1)} collective-permute-done((bf16[1,8,2176]{2,1,0:T(8,128)(2,1)S(1)}, bf16[1,8,2176]{2,1,0:T(8,128)(2,1)S(1)}, u32[]{:S(2)}, u32[]{:S(2)}) %collective-permute-start.14) | collective-permute-done | bytes 34848 | tf_op jit(solution)/shard_map/ppermute | solution.py:303
  49.8 0.6 %shard_map.176 = (f32[8,768]{1,0:T(8,128)}, f32[8,256]{1,0:T(8,128)}, f32[8,768]{1,0:T(8,128)}, f32[8,384]{1,0:T(8,128)}, f32[1,8]{1,0:T(1,128)}, /*index=5*/f32[1,8]{1,0:T(1,128)}) custom-call(bf16[8,2176]{1,0:T(8,128)(2,1)S(1)} %get-tuple-element.80.refs_0_, bf16[8,2176]{1,0:T(8,128)(2,1)S(1)} %bitcast.75, bf16[8,2176]{1,0:T(8,128)(2,1)S(1)} %bitcast.76, ...), custom_call_target="tpu_custom_call" | custom-call | tf_op jit(solution)/shard_map/pallas_call | solution.py:367
  (58 shorter events, 4.7 us)
Async XLA Ops:
  0.6 15.4 %copy-start = (bf16[768,256]{1,0:T(8,128)(2,1)S(1)}, bf16[768,256]{1,0:T(8,128)(2,1)}, u32[]{:S(2)}) copy-start(bf16[768,256]{1,0:T(8,128)(2,1)} %tokens.4) | copy-start | bytes 1179652
  0.6 15.4 %copy-start.1 = (bf16[768,256]{1,0:T(8,128)(2,1)S(1)}, bf16[768,256]{1,0:T(8,128)(2,1)}, u32[]{:S(2)}) copy-start(bf16[768,256]{1,0:T(8,128)(2,1)} %cot) | copy-start | bytes 1179652
  0.7 15.4 %copy-start.6 = (s32[6]{0:T(128)S(1)}, s32[6]{0:T(128)}, u32[]{:S(2)}) copy-start(s32[6]{0:T(128)} %lengths.5) | copy-start | bytes 76
  2.3 7.2 %collective-permute-start = (bf16[1,8,2304]{2,1,0:T(8,128)(2,1)}, bf16[1,8,2304]{2,1,0:T(8,128)(2,1)S(1)}, u32[]{:S(2)}, u32[]{:S(2)}) collective-permute-start(bf16[1,8,2304]{2,1,0:T(8,128)(2,1)} %bitcast.87), channel_id=1, source_target_pairs={{0,24},{1,25},{2,26},{3,27},{4,28},{5,29},{6,30},{7,31},{8,16},{9,... | collective-permute-start | bytes 110600 | tf_op jit(solution)/shard_map/ppermute | solution.py:303
  7.3 5.1 %collective-permute-start.1 = (bf16[1,8,2304]{2,1,0:T(8,128)(2,1)}, bf16[1,8,2304]{2,1,0:T(8,128)(2,1)S(1)}, u32[]{:S(2)}, u32[]{:S(2)}) collective-permute-start(bf16[1,8,2304]{2,1,0:T(8,128)(2,1)} %bitcast.88), channel_id=1, source_target_pairs={{0,16},{1,17},{2,18},{3,19},{4,20},{5,21},{6,22},{7,23},{8,24},{9,... | collective-permute-start | bytes 110600 | tf_op jit(solution)/shard_map/ppermute | solution.py:303
  7.3 5.1 %collective-permute-start.2 = (bf16[1,8,2304]{2,1,0:T(8,128)(2,1)}, bf16[1,8,2304]{2,1,0:T(8,128)(2,1)S(1)}, u32[]{:S(2)}, u32[]{:S(2)}) collective-permute-start(bf16[1,8,2304]{2,1,0:T(8,128)(2,1)} %bitcast.89), channel_id=1, source_target_pairs={{0,8},{1,9},{2,10},{3,11},{4,12},{5,13},{6,14},{7,15},{8,0},{9,1},... | collective-permute-start | bytes 110600 | tf_op jit(solution)/shard_map/ppermute | solution.py:303
  12.4 7.7 %collective-permute-start.3 = (bf16[4,8,2304]{2,1,0:T(8,128)(2,1)S(1)}, bf16[4,8,2304]{2,1,0:T(8,128)(2,1)S(1)}, u32[]{:S(2)}, u32[]{:S(2)}) collective-permute-start(bf16[4,8,2304]{2,1,0:T(8,128)(2,1)S(1)} %constant_dynamic-update-slice_fusion), channel_id=1, source_target_pairs={{0,6},{1,7},{2,4},{3,5},{4,2},{5,3},{6,0},{7,1},{8,14},{9,15},{10,... | collective-permute-start | bytes 442376 | tf_op jit(solution)/shard_map/ppermute | solution.py:303
  14.9 6.0 %collective-permute-start.4 = (bf16[4,8,2304]{2,1,0:T(8,128)(2,1)S(1)}, bf16[4,8,2304]{2,1,0:T(8,128)(2,1)S(1)}, u32[]{:S(2)}, u32[]{:S(2)}) collective-permute-start(bf16[4,8,2304]{2,1,0:T(8,128)(2,1)S(1)} %constant_dynamic-update-slice_fusion), channel_id=1, source_target_pairs={{0,4},{1,5},{2,6},{3,7},{4,0},{5,1},{6,2},{7,3},{8,12},{9,13},{10,... | collective-permute-start | bytes 442376 | tf_op jit(solution)/shard_map/ppermute | solution.py:303
  15.4 5.5 %collective-permute-start.5 = (bf16[4,8,2304]{2,1,0:T(8,128)(2,1)S(1)}, bf16[4,8,2304]{2,1,0:T(8,128)(2,1)S(1)}, u32[]{:S(2)}, u32[]{:S(2)}) collective-permute-start(bf16[4,8,2304]{2,1,0:T(8,128)(2,1)S(1)} %constant_dynamic-update-slice_fusion), channel_id=1, source_target_pairs={{0,2},{1,3},{2,0},{3,1},{4,6},{5,7},{6,4},{7,5},{8,10},{9,11},{10,... | collective-permute-start | bytes 442376 | tf_op jit(solution)/shard_map/ppermute | solution.py:303
  21.0 1.6 %collective-permute-start.6 = (bf16[16,8,1152]{2,1,0:T(8,128)(2,1)S(1)}, bf16[16,8,1152]{2,1,0:T(8,128)(2,1)S(1)}, u32[]{:S(2)}, u32[]{:S(2)}) collective-permute-start(bf16[16,8,1152]{2,1,0:T(8,128)(2,1)S(1)} %get-tuple-element.73), channel_id=1, source_target_pairs={{0,1},{1,0},{2,3},{3,2},{4,5},{5,4},{6,7},{7,6},{8,9},{9,8},{10,11... | collective-permute-start | bytes 884744 | tf_op jit(solution)/shard_map/ppermute | solution.py:303
  21.1 3.9 %collective-permute-start.7 = (bf16[16,8,1152]{2,1,0:T(8,128)(2,1)S(1)}, bf16[16,8,1152]{2,1,0:T(8,128)(2,1)S(1)}, u32[]{:S(2)}, u32[]{:S(2)}) collective-permute-start(bf16[16,8,1152]{2,1,0:T(8,128)(2,1)S(1)} %get-tuple-element.72), channel_id=1, source_target_pairs={{0,1},{1,0},{2,3},{3,2},{4,5},{5,4},{6,7},{7,6},{8,9},{9,8},{10,11... | collective-permute-start | bytes 884744 | tf_op jit(solution)/shard_map/ppermute | solution.py:303
  21.6 1.1 %copy-start.2 = (f32[128,128]{1,0:T(8,128)S(1)}, f32[128,128]{1,0:T(8,128)}, u32[]{:S(2)}) copy-start(f32[128,128]{1,0:T(8,128)} %constant.79.clone.cos) | copy-start | bytes 196612
  30.4 1.6 %collective-permute-start.8 = (bf16[16,8,1024]{2,1,0:T(8,128)(2,1)S(1)}, bf16[16,8,1024]{2,1,0:T(8,128)(2,1)S(1)}, u32[]{:S(2)}, u32[]{:S(2)}) collective-permute-start(bf16[16,8,1024]{2,1,0:T(8,128)(2,1)S(1)} %dynamic-slice_bitcast_fusion.1), channel_id=1, source_target_pairs={{0,1},{1,0},{2,3},{3,2},{4,5},{5,4},{6,7},{7,6},{8,9},{9,8},{10,11... | collective-permute-start | bytes 786440 | tf_op jit(solution)/shard_map/ppermute | solution.py:303
  30.6 1.8 %collective-permute-start.9 = (bf16[16,8,1152]{2,1,0:T(8,128)(2,1)S(1)}, bf16[16,8,1152]{2,1,0:T(8,128)(2,1)S(1)}, u32[]{:S(2)}, u32[]{:S(2)}) collective-permute-start(bf16[16,8,1152]{2,1,0:T(8,128)(2,1)S(1)} %dynamic-slice_bitcast_fusion), channel_id=1, source_target_pairs={{0,1},{1,0},{2,3},{3,2},{4,5},{5,4},{6,7},{7,6},{8,9},{9,8},{10,11... | collective-permute-start | bytes 884744 | tf_op jit(solution)/shard_map/ppermute | solution.py:303
  32.6 6.5 %collective-permute-start.12 = (bf16[4,8,2176]{2,1,0:T(8,128)(2,1)S(1)}, bf16[4,8,2176]{2,1,0:T(8,128)(2,1)S(1)}, u32[]{:S(2)}, u32[]{:S(2)}) collective-permute-start(bf16[4,8,2176]{2,1,0:T(8,128)(2,1)S(1)} %get-tuple-element.75), channel_id=1, source_target_pairs={{0,2},{1,3},{2,0},{3,1},{4,6},{5,7},{6,4},{7,5},{8,10},{9,11},{10,... | collective-permute-start | bytes 417800 | tf_op jit(solution)/shard_map/ppermute | solution.py:303
  34.1 8.5 %collective-permute-start.11 = (bf16[4,8,2176]{2,1,0:T(8,128)(2,1)S(1)}, bf16[4,8,2176]{2,1,0:T(8,128)(2,1)S(1)}, u32[]{:S(2)}, u32[]{:S(2)}) collective-permute-start(bf16[4,8,2176]{2,1,0:T(8,128)(2,1)S(1)} %get-tuple-element.76), channel_id=1, source_target_pairs={{0,4},{1,5},{2,6},{3,7},{4,0},{5,1},{6,2},{7,3},{8,12},{9,13},{10,... | collective-permute-start | bytes 417800 | tf_op jit(solution)/shard_map/ppermute | solution.py:303
  34.8 7.8 %collective-permute-start.10 = (bf16[4,8,2176]{2,1,0:T(8,128)(2,1)S(1)}, bf16[4,8,2176]{2,1,0:T(8,128)(2,1)S(1)}, u32[]{:S(2)}, u32[]{:S(2)}) collective-permute-start(bf16[4,8,2176]{2,1,0:T(8,128)(2,1)S(1)} %get-tuple-element.74), channel_id=1, source_target_pairs={{0,6},{1,7},{2,4},{3,5},{4,2},{5,3},{6,0},{7,1},{8,14},{9,15},{10,... | collective-permute-start | bytes 417800 | tf_op jit(solution)/shard_map/ppermute | solution.py:303
  36.2 13.6 %copy-start.4 = (bf16[8,768]{1,0:T(8,128)(2,1)S(1)}, bf16[8,768]{1,0:T(8,128)(2,1)}, u32[]{:S(2)}) copy-start(bf16[8,768]{1,0:T(8,128)(2,1)} %refs_4_.1) | copy-start | bytes 36868
  36.2 13.6 %copy-start.5 = (bf16[8,768]{1,0:T(8,128)(2,1)S(1)}, bf16[8,768]{1,0:T(8,128)(2,1)}, u32[]{:S(2)}) copy-start(bf16[8,768]{1,0:T(8,128)(2,1)} %refs_5_.1) | copy-start | bytes 36868
  36.2 13.6 %copy-start.7 = (bf16[8]{0:T(256)(128)(2,1)S(1)}, bf16[8]{0:T(256)(128)(2,1)}, u32[]{:S(2)}) copy-start(bf16[8]{0:T(256)(128)(2,1)} %param.17) | copy-start | bytes 52
  36.2 13.6 %copy-start.8 = (bf16[8]{0:T(256)(128)(2,1)S(1)}, bf16[8]{0:T(256)(128)(2,1)}, u32[]{:S(2)}) copy-start(bf16[8]{0:T(256)(128)(2,1)} %param.18) | copy-start | bytes 52
  42.7 6.1 %collective-permute-start.13 = (bf16[1,8,2176]{2,1,0:T(8,128)(2,1)S(1)}, bf16[1,8,2176]{2,1,0:T(8,128)(2,1)S(1)}, u32[]{:S(2)}, u32[]{:S(2)}) collective-permute-start(bf16[1,8,2176]{2,1,0:T(8,128)(2,1)S(1)} %get-tuple-element.79), channel_id=1, source_target_pairs={{0,24},{1,25},{2,26},{3,27},{4,28},{5,29},{6,30},{7,31},{8,16},{9,... | collective-permute-start | bytes 104456 | tf_op jit(solution)/shard_map/ppermute | solution.py:303
  44.6 5.2 %collective-permute-start.14 = (bf16[1,8,2176]{2,1,0:T(8,128)(2,1)S(1)}, bf16[1,8,2176]{2,1,0:T(8,128)(2,1)S(1)}, u32[]{:S(2)}, u32[]{:S(2)}) collective-permute-start(bf16[1,8,2176]{2,1,0:T(8,128)(2,1)S(1)} %get-tuple-element.78), channel_id=1, source_target_pairs={{0,16},{1,17},{2,18},{3,19},{4,20},{5,21},{6,22},{7,23},{8,24},{9,... | collective-permute-start | bytes 104456 | tf_op jit(solution)/shard_map/ppermute | solution.py:303
  44.8 5.0 %collective-permute-start.15 = (bf16[1,8,2176]{2,1,0:T(8,128)(2,1)S(1)}, bf16[1,8,2176]{2,1,0:T(8,128)(2,1)S(1)}, u32[]{:S(2)}, u32[]{:S(2)}) collective-permute-start(bf16[1,8,2176]{2,1,0:T(8,128)(2,1)S(1)} %get-tuple-element.77), channel_id=1, source_target_pairs={{0,8},{1,9},{2,10},{3,11},{4,12},{5,13},{6,14},{7,15},{8,0},{9,1},... | collective-permute-start | bytes 104456 | tf_op jit(solution)/shard_map/ppermute | solution.py:303
  (1 other events, 1.1 us)

commit v6 on v5

--- a/solution.py
+++ b/solution.py
@@ -178,9 +178,22 @@
         mixture[block] = mixed.astype(bf16)
 
 
-def feed_kernel(
+def middle_kernel(
+    tokens, out_low, first, second, gains, mixture, heads, shares, normed, cos, sin,
+    middle, hidden, d_middle, second_sums, first_sums, d_qkv, d_mixture, hat_two_low, d_att, d_merged,
+):
+    feed(
+        tokens, out_low, first, second, gains, mixture,
+        middle, hidden, d_middle, d_mixture, hat_two_low, d_att, d_merged,
+    )
+    second_sums[:, : 2 * FF] = mm_tn(hat_two_low[...], d_merged[...]).astype(bf16)
+    second_sums[:, 2 * FF :] = mm_tn(out_low[...], hidden[...]).astype(bf16)
+    attend_back(heads, shares, d_mixture, normed, mixture, d_att, cos, sin, first_sums, d_qkv)
+
+
+def feed(
     tokens, out_low, first, second, gains, mixture,
-    middle, hidden, d_middle, d_mixture, g_attn, sums, hat_two_low, d_att, d_merged,
+    middle, hidden, d_middle, d_mixture, hat_two_low, d_att, d_merged,
 ):
     w_attn = first[:, QKV : QKV + D]
     w_in = second[:, : 2 * FF]
@@ -206,14 +219,9 @@
     d_middle[...] = d_mid
     d_att[...] = d_mid.astype(bf16)
     d_mixture[...] = mm_nt(d_att[...], w_attn).astype(bf16)
-    sums[:, : 2 * FF] = mm_tn(hat_two_low[...], d_merged[...]).astype(bf16)
-    sums[:, 2 * FF :] = mm_tn(out_low[...], hidden[...]).astype(bf16)
-    g_attn[...] = mm_tn(mixture[...], d_att[...]).astype(bf16)
-
-
-def attend_back_kernel(
-    heads, shares, d_mixture, normed, g_attn, cos, sin, sums, d_qkv
-):
+
+
+def attend_back(heads, shares, d_mixture, normed, mixture, d_att, cos, sin, sums, d_qkv):
     c, s = cos[...], sin[...]
     spread_masks, plain_masks = head_masks()
 
@@ -244,7 +252,7 @@
     sums[:, :D] = mm(total[:, :D], spread).astype(bf16)
     sums[:, D : 2 * D] = mm(total[:, D : 2 * D], spread).astype(bf16)
     sums[:, 2 * D : QKV] = total[:, 2 * D :]
-    sums[:, QKV:] = g_attn[...]
+    sums[:, QKV:] = mm_tn(mixture[...], d_att[...]).astype(bf16)
 
 
 def outputs_kernel(lengths, tokens, first, second, gains, d_qkv, d_middle, middle, hidden, out, grad):
@@ -256,6 +264,8 @@
     grad[...] = d_middle[...] + norm_back(d_normed * gain, hat_one, inv_one)
 
 
+GATHER_LEAD, GATHER_LAST = (2, 3, 1), (1, 2, 3)
+REDUCE_LEAD, REDUCE_LAST = (1, 2, 3), (3, 1, 2)
 SMALL = pl.BlockSpec(memory_space=pltpu.SMEM)
 NEAR = pl.BlockSpec(memory_space=pltpu.VMEM)
 
@@ -292,10 +302,12 @@
     core = me & 1
     rounds = []
     if len(lead) % 2:
-        rounds.append((me // lead[0], ((lead[0], 1),)))
+        rounds.append((me // lead[0], ((lead[0], 1),), ((lead[0], 1),)))
     for k in range(len(lead) % 2, len(lead), 2):
         one, two = lead[k], lead[k + 1]
-        rounds.append(((me // two) & 3, ((one ^ two, 3), (one, 2), (two, 1))))
+        masks = {1: two, 2: one, 3: one ^ two}
+        orders = (GATHER_LAST, REDUCE_LAST) if k + 2 == len(lead) else (GATHER_LEAD, REDUCE_LEAD)
+        rounds.append(((me // two) & 3, *[tuple((masks[p], p) for p in order) for order in orders]))
     gain_attn = gain_attn.reshape(1, rows)
     gain_mlp = gain_mlp.reshape(1, rows)
 
@@ -306,7 +318,7 @@
         pack_kernel, out_specs=NEAR, out_shape=jax.ShapeDtypeStruct((rows, FIRST + SECOND), bf16)
     )(w_qkv, w_attn, w_in, w_mlp.T, gain_attn, gain_mlp)
     room = held[None]
-    for place, partners in rounds:
+    for place, partners, _ in rounds:
         got = [(trade(room, mask), other) for mask, other in partners]
         wide = put(jnp.zeros((room.shape[0], len(got) + 1, rows, FIRST + SECOND), bf16), room, place)
         for piece, other in got:
@@ -320,11 +332,14 @@
             )(lengths, *early[1:])
     room, hat, out_low = lax.optimization_barrier((room, hat, out_low))
 
-    def both(half):
+    def both(half, got):
         wide = put(jnp.zeros((n // 2, 2) + half.shape[1:], bf16), half, core)
-        return put(wide, trade(half, 1), core ^ 1).reshape(D, half.shape[2])
-
-    first, second = both(room[:, :, :FIRST]), both(room[:, :, FIRST:])
+        return put(wide, got, core ^ 1).reshape(D, half.shape[2])
+
+    first, second = room[:, :, :FIRST], room[:, :, FIRST:]
+    got = trade(first, 1)
+    got, second = lax.optimization_barrier((got, second))
+    first, second = both(first, got), both(second, trade(second, 1))
 
     cos, sin = tables()
     cos, sin = jnp.asarray(cos), jnp.asarray(sin)
@@ -333,15 +348,12 @@
         [SMALL] + [NEAR] * 4,
         [((2, D), f32), ((count, D), bf16), ((count, QKV), bf16), ((count, WIDE), f32), ((count, D), bf16)],
     )(lengths, hat, first, cos, sin)
-    middle, hidden, d_middle, d_mixture, g_attn, second_sums = call(
-        feed_kernel,
-        [NEAR] * 6,
-        [((count, D), f32), ((count, FF), bf16), ((count, D), f32), ((count, D), bf16), ((D, D), bf16), ((D, 3 * FF), bf16)],
-        [((count, D), bf16), ((count, D), bf16), ((count, 2 * FF), bf16)],
-    )(tokens, out_low, first, second, gains, mixture)
-    first_sums, d_qkv = call(
-        attend_back_kernel, [NEAR] * 7, [((D, SUMS), bf16), ((count, QKV), bf16)]
-    )(heads, shares, d_mixture, normed, g_attn, cos, sin)
+    middle, hidden, d_middle, second_sums, first_sums, d_qkv = call(
+        middle_kernel,
+        [NEAR] * 11,
+        [((count, D), f32), ((count, FF), bf16), ((count, D), f32), ((D, 3 * FF), bf16), ((D, SUMS), bf16), ((count, QKV), bf16)],
+        [((count, D), bf16), ((count, D), bf16), ((count, D), bf16), ((count, 2 * FF), bf16)],
+    )(tokens, out_low, first, second, gains, mixture, heads, shares, normed, cos, sin)
     out, grad = call(
         outputs_kernel, [SMALL] + [NEAR] * 8, [((count, D), bf16), ((count, D), f32)]
     )(lengths, tokens, first, second, gains, d_qkv, d_middle, middle, hidden)
@@ -352,7 +364,7 @@
         return (cut(sums, core, 2).astype(f32) + got.astype(f32)).astype(bf16)
 
     kept = jnp.concatenate([halve(first_sums), halve(second_sums)], axis=2)
-    for k, (place, partners) in enumerate(rounds[::-1]):
+    for k, (place, _, partners) in enumerate(rounds[::-1]):
         ways = len(partners) + 1
         got = [trade(cut(kept, place ^ other, ways), mask) for mask, other in partners]
         kept = cut(kept, place, ways)

time: 50.6 us -> 50.3 us (level)
    pallas_call x2 -> x1, Pallas kernels: 5.34 us -> 4.85 us  [on_device(): call(middle_kernel, [NEAR] * 11, [((count, D), f32), ((count, FF), bf16),...]
    dynamic_update_slice x12 -> x11, local copies, waits for them, and re-layouts: 1.01 us -> 1.04 us  [put(): return lax.dynamic_update_slice(room, piece[:, None], (0, place, 0, column))]
  transfers between devices with their start and end apart: 16 -> 16, of which waited for: 11 -> 10; matrix products, arithmetic and copies ran while one was open for 2% -> 2% of each run, Pallas kernels for 11% -> 11%
where the time goes in v6:
time: 50.3 us; the launch traced here: 50.1 us
  starting transfers between devices  18 us (36%)
  waiting for transfers between devices  16.6 us (33%)
  Pallas kernels  12.9 us (26%)
  local copies, waits for them, and re-layouts  1.39 us (3%)
  between operations  0.93 us (2%)
    ppermute x16, starting transfers between devices, trade(): return lax.ppermute(values, 'dp', [(i, i ^ mask) for i in range(n)])  18 us
    ppermute x16, waiting for transfers between devices, trade(): return lax.ppermute(values, 'dp', [(i, i ^ mask) for i in range(n)])  16.6 us
    pallas_call x1, Pallas kernels, on_device(): call(middle_kernel, [NEAR] * 11, [((count, D), f32), ((count, FF), bf16),...  4.85 us
    pallas_call x1, Pallas kernels, on_device(): call(outputs_kernel, [SMALL] + [NEAR] * 8, [((count, D), bf16), ((count,...  2.45 us
    pallas_call x1, Pallas kernels, on_device(): call(attend_kernel, [SMALL] + [NEAR] * 4, [((2, D), f32), ((count, D), bf...  2.29 us
    pallas_call x1, Pallas kernels, on_device(): pl.pallas_call(pack_kernel, out_specs=NEAR, out_shape=jax.ShapeDtypeStruc...  1.62 us
    dynamic_update_slice x11, local copies, waits for them, and re-layouts, put(): return lax.dynamic_update_slice(room, piece[:, None], (0, place, 0, column))  1.04 us
  transfers between devices with their start and end apart: 16, of which 10 were waited for; matrix products, arithmetic and copies ran while one was open for 2% of the time, Pallas kernels for 11%

profile of v6, /device:TPU:0, one launch (start us, length us, event | category | flops | bytes accessed | tf_op | source)
XLA Modules:
  0.0 50.1 jit_solution(3969702650226201760)
XLA Ops:
  0.7 1.6 %shard_map.170 = bf16[8,2304]{1,0:T(8,128)(2,1)} custom-call(bf16[8,768]{1,0:T(8,128)(2,1)} %refs_4_.1, bf16[8,256]{1,0:T(8,128)(2,1)} %w_attn.1, bf16[8,768]{1,0:T(8,128)(2,1)} %refs_5_.1, bf16[8,384]{1,0:T(8,128)(2,1)} %bitcast.89, bf16[1,8]{1,0:T(2,128)(2,1)} %bitcast.78, bf16[1,8]{1,0:T(2,128)(2,1)} %bitcast.80), custom_call_target="tpu_custom_call" | custom-call | tf_op jit(solution)/shard_map/pallas_call | solution.py:317
  2.3 5.0 %collective-permute-start.1 = (bf16[1,8,2304]{2,1,0:T(8,128)(2,1)}, bf16[1,8,2304]{2,1,0:T(8,128)(2,1)S(1)}, u32[]{:S(2)}, u32[]{:S(2)}) collective-permute-start(bf16[1,8,2304]{2,1,0:T(8,128)(2,1)} %bitcast.86), channel_id=1, source_target_pairs={{0,24},{1,25},{2,26},{3,27},{4,28},{5,29},{6,30},{7,31},{8,16},{9,... | collective-permute-start | bytes 110600 | tf_op jit(solution)/shard_map/ppermute | solution.py:315
  7.3 0.6 %collective-permute-start.2 = (bf16[1,8,2304]{2,1,0:T(8,128)(2,1)}, bf16[1,8,2304]{2,1,0:T(8,128)(2,1)S(1)}, u32[]{:S(2)}, u32[]{:S(2)}) collective-permute-start(bf16[1,8,2304]{2,1,0:T(8,128)(2,1)} %bitcast.88), channel_id=1, source_target_pairs={{0,8},{1,9},{2,10},{3,11},{4,12},{5,13},{6,14},{7,15},{8,0},{9,1},... | collective-permute-start | bytes 110600 | tf_op jit(solution)/shard_map/ppermute | solution.py:315
  7.9 0.8 %constant_dynamic-update-slice_fusion.3 = bf16[4,8,2304]{2,1,0:T(8,128)(2,1)S(1)} fusion(bf16[4,8,2304]{2,1,0:T(8,128)(2,1)S(1)} %reshape.79, s32[]{:T(128)S(6)} %select_n.57, bf16[8,2304]{1,0:T(8,128)(2,1)} %shard_map.170), kind=kLoop, calls=%fused_computation.29 | loop fusion | bytes 73732 | tf_op jit(solution)/shard_map/dynamic_update_slice | solution.py:285
  8.7 3.7 %collective-permute-done = bf16[1,8,2304]{2,1,0:T(8,128)(2,1)S(1)} collective-permute-done((bf16[1,8,2304]{2,1,0:T(8,128)(2,1)}, bf16[1,8,2304]{2,1,0:T(8,128)(2,1)S(1)}, u32[]{:S(2)}, u32[]{:S(2)}) %collective-permute-start) | collective-permute-done | bytes 36896 | tf_op jit(solution)/shard_map/ppermute | solution.py:315
  12.5 2.5 %collective-permute-start.5 = (bf16[4,8,2304]{2,1,0:T(8,128)(2,1)S(1)}, bf16[4,8,2304]{2,1,0:T(8,128)(2,1)S(1)}, u32[]{:S(2)}, u32[]{:S(2)}) collective-permute-start(bf16[4,8,2304]{2,1,0:T(8,128)(2,1)S(1)} %constant_dynamic-update-slice_fusion), channel_id=1, source_target_pairs={{0,6},{1,7},{2,4},{3,5},{4,2},{5,3},{6,0},{7,1},{8,14},{9,15},{10,... | collective-permute-start | bytes 442376 | tf_op jit(solution)/shard_map/ppermute | solution.py:315
  15.5 0.5 %collective-permute-start.3 = (bf16[4,8,2304]{2,1,0:T(8,128)(2,1)S(1)}, bf16[4,8,2304]{2,1,0:T(8,128)(2,1)S(1)}, u32[]{:S(2)}, u32[]{:S(2)}) collective-permute-start(bf16[4,8,2304]{2,1,0:T(8,128)(2,1)S(1)} %constant_dynamic-update-slice_fusion), channel_id=1, source_target_pairs={{0,2},{1,3},{2,0},{3,1},{4,6},{5,7},{6,4},{7,5},{8,10},{9,11},{10,... | collective-permute-start | bytes 442376 | tf_op jit(solution)/shard_map/ppermute | solution.py:315
  16.1 1.0 %shard_map.171 = (f32[768,256]{1,0:T(8,128)S(1)}, bf16[768,256]{1,0:T(8,128)(2,1)S(1)}) custom-call(s32[6]{0:T(128)S(1)} %copy-done.6, bf16[768,256]{1,0:T(8,128)(2,1)S(1)} %copy-done, bf16[768,256]{1,0:T(8,128)(2,1)S(1)} %copy-done.1), custom_call_target="tpu_custom_call" | custom-call | tf_op jit(solution)/shard_map/pallas_call | solution.py:330
  17.1 3.7 %collective-permute-done.3 = bf16[4,8,2304]{2,1,0:T(8,128)(2,1)S(1)} collective-permute-done((bf16[4,8,2304]{2,1,0:T(8,128)(2,1)S(1)}, bf16[4,8,2304]{2,1,0:T(8,128)(2,1)S(1)}, u32[]{:S(2)}, u32[]{:S(2)}) %collective-permute-start.3) | collective-permute-done | bytes 147488 | tf_op jit(solution)/shard_map/ppermute | solution.py:315
  21.2 1.4 %collective-permute-done.6 = bf16[16,8,1152]{2,1,0:T(8,128)(2,1)S(1)} collective-permute-done((bf16[16,8,1152]{2,1,0:T(8,128)(2,1)S(1)}, bf16[16,8,1152]{2,1,0:T(8,128)(2,1)S(1)}, u32[]{:S(2)}, u32[]{:S(2)}) %collective-permute-start.6) | collective-permute-done | bytes 294944 | tf_op jit(solution)/shard_map/ppermute | solution.py:315
  23.0 2.3 %shard_map.172 = (f32[2,256]{1,0:T(2,128)S(1)}, bf16[768,256]{1,0:T(8,128)(2,1)S(1)}, bf16[768,768]{1,0:T(8,128)(2,1)S(1)}, f32[768,512]{1,0:T(8,128)S(1)}, bf16[768,256]{1,0:T(8,128)(2,1)S(1)}) custom-call(s32[6]{0:T(128)S(1)} %copy-done.6, f32[768,256]{1,0:T(8,128)S(1)} %get-tuple-element.49.hat, bf16[256,1152]{1,0:T(8,128)(2,1)S(1)} %bitcast.66, ...), custom_call_target="tpu_custom_call" | custom-call | tf_op jit(solution)/shard_map/pallas_call | solution.py:346
  25.3 4.9 %shard_map.173 = (f32[768,256]{1,0:T(8,128)S(1)}, bf16[768,384]{1,0:T(8,128)(2,1)S(1)}, f32[768,256]{1,0:T(8,128)S(1)}, bf16[256,1152]{1,0:T(8,128)(2,1)S(1)}, b...) custom-call(bf16[768,256]{1,0:T(8,128)(2,1)S(1)} %copy-done, bf16[768,256]{1,0:T(8,128)(2,1)S(1)} %get-tuple-element.45.out_low, ...), custom_call_target="tpu_custom_call" | custom-call | tf_op jit(solution)/shard_map/pallas_call | solution.py:351
  30.9 0.9 %collective-permute-done.8 = bf16[16,8,1024]{2,1,0:T(8,128)(2,1)S(1)} collective-permute-done((bf16[16,8,1024]{2,1,0:T(8,128)(2,1)S(1)}, bf16[16,8,1024]{2,1,0:T(8,128)(2,1)S(1)}, u32[]{:S(2)}, u32[]{:S(2)}) %collective-permute-start.8) | collective-permute-done | bytes 262176 | tf_op jit(solution)/shard_map/ppermute | solution.py:315
  32.5 1.6 %collective-permute-start.10 = (bf16[4,8,2176]{2,1,0:T(8,128)(2,1)S(1)}, bf16[4,8,2176]{2,1,0:T(8,128)(2,1)S(1)}, u32[]{:S(2)}, u32[]{:S(2)}) collective-permute-start(bf16[4,8,2176]{2,1,0:T(8,128)(2,1)S(1)} %get-tuple-element.74), channel_id=1, source_target_pairs={{0,6},{1,7},{2,4},{3,5},{4,2},{5,3},{6,0},{7,1},{8,14},{9,15},{10,... | collective-permute-start | bytes 417800 | tf_op jit(solution)/shard_map/ppermute | solution.py:315
  34.1 1.4 %collective-permute-start.12 = (bf16[4,8,2176]{2,1,0:T(8,128)(2,1)S(1)}, bf16[4,8,2176]{2,1,0:T(8,128)(2,1)S(1)}, u32[]{:S(2)}, u32[]{:S(2)}) collective-permute-start(bf16[4,8,2176]{2,1,0:T(8,128)(2,1)S(1)} %get-tuple-element.75), channel_id=1, source_target_pairs={{0,4},{1,5},{2,6},{3,7},{4,0},{5,1},{6,2},{7,3},{8,12},{9,13},{10,... | collective-permute-start | bytes 417800 | tf_op jit(solution)/shard_map/ppermute | solution.py:315
  35.5 0.5 %collective-permute-start.11 = (bf16[4,8,2176]{2,1,0:T(8,128)(2,1)S(1)}, bf16[4,8,2176]{2,1,0:T(8,128)(2,1)S(1)}, u32[]{:S(2)}, u32[]{:S(2)}) collective-permute-start(bf16[4,8,2176]{2,1,0:T(8,128)(2,1)S(1)} %get-tuple-element.76), channel_id=1, source_target_pairs={{0,2},{1,3},{2,0},{3,1},{4,6},{5,7},{6,4},{7,5},{8,10},{9,11},{10,... | collective-permute-start | bytes 417800 | tf_op jit(solution)/shard_map/ppermute | solution.py:315
  36.1 2.5 %shard_map.174 = (bf16[768,256]{1,0:T(8,128)(2,1)}, f32[768,256]{1,0:T(8,128)}) custom-call(s32[6]{0:T(128)S(1)} %copy-done.6, bf16[768,256]{1,0:T(8,128)(2,1)S(1)} %copy-done, bf16[256,1152]{1,0:T(8,128)(2,1)S(1)} %bitcast.68, bf16[256,1152]{1,0:T(8,128)(2,1)S(1)} %bitcast.70, f32[2,256]{1,0:T(2,128)S(1)} %get-tuple-element.50.gains, ...), custom_call_target="tpu_custom_call" | custom-call | tf_op jit(solution)/shard_map/pallas_call | solution.py:357
  38.5 1.5 %collective-permute-done.10 = bf16[4,8,2176]{2,1,0:T(8,128)(2,1)S(1)} collective-permute-done((bf16[4,8,2176]{2,1,0:T(8,128)(2,1)S(1)}, bf16[4,8,2176]{2,1,0:T(8,128)(2,1)S(1)}, u32[]{:S(2)}, u32[]{:S(2)}) %collective-permute-start.10) | collective-permute-done | bytes 139296 | tf_op jit(solution)/shard_map/ppermute | solution.py:315
  40.0 2.3 %collective-permute-done.12 = bf16[4,8,2176]{2,1,0:T(8,128)(2,1)S(1)} collective-permute-done((bf16[4,8,2176]{2,1,0:T(8,128)(2,1)S(1)}, bf16[4,8,2176]{2,1,0:T(8,128)(2,1)S(1)}, u32[]{:S(2)}, u32[]{:S(2)}) %collective-permute-start.12) | collective-permute-done | bytes 139296 | tf_op jit(solution)/shard_map/ppermute | solution.py:315
  42.4 1.8 %collective-permute-start.15 = (bf16[1,8,2176]{2,1,0:T(8,128)(2,1)S(1)}, bf16[1,8,2176]{2,1,0:T(8,128)(2,1)S(1)}, u32[]{:S(2)}, u32[]{:S(2)}) collective-permute-start(bf16[1,8,2176]{2,1,0:T(8,128)(2,1)S(1)} %get-tuple-element.77), channel_id=1, source_target_pairs={{0,24},{1,25},{2,26},{3,27},{4,28},{5,29},{6,30},{7,31},{8,16},{9,... | collective-permute-start | bytes 104456 | tf_op jit(solution)/shard_map/ppermute | solution.py:315
  44.5 2.4 %collective-permute-start.13 = (bf16[1,8,2176]{2,1,0:T(8,128)(2,1)S(1)}, bf16[1,8,2176]{2,1,0:T(8,128)(2,1)S(1)}, u32[]{:S(2)}, u32[]{:S(2)}) collective-permute-start(bf16[1,8,2176]{2,1,0:T(8,128)(2,1)S(1)} %get-tuple-element.79), channel_id=1, source_target_pairs={{0,8},{1,9},{2,10},{3,11},{4,12},{5,13},{6,14},{7,15},{8,0},{9,1},... | collective-permute-start | bytes 104456 | tf_op jit(solution)/shard_map/ppermute | solution.py:315
  46.9 1.6 %collective-permute-done.15 = bf16[1,8,2176]{2,1,0:T(8,128)(2,1)S(1)} collective-permute-done((bf16[1,8,2176]{2,1,0:T(8,128)(2,1)S(1)}, bf16[1,8,2176]{2,1,0:T(8,128)(2,1)S(1)}, u32[]{:S(2)}, u32[]{:S(2)}) %collective-permute-start.15) | collective-permute-done | bytes 34848 | tf_op jit(solution)/shard_map/ppermute | solution.py:315
  48.5 0.9 %collective-permute-done.14 = bf16[1,8,2176]{2,1,0:T(8,128)(2,1)S(1)} collective-permute-done((bf16[1,8,2176]{2,1,0:T(8,128)(2,1)S(1)}, bf16[1,8,2176]{2,1,0:T(8,128)(2,1)S(1)}, u32[]{:S(2)}, u32[]{:S(2)}) %collective-permute-start.14) | collective-permute-done | bytes 34848 | tf_op jit(solution)/shard_map/ppermute | solution.py:315
  49.4 0.6 %shard_map.175 = (f32[8,768]{1,0:T(8,128)}, f32[8,256]{1,0:T(8,128)}, f32[8,768]{1,0:T(8,128)}, f32[8,384]{1,0:T(8,128)}, f32[1,8]{1,0:T(1,128)}, /*index=5*/f32[1,8]{1,0:T(1,128)}) custom-call(bf16[8,2176]{1,0:T(8,128)(2,1)S(1)} %get-tuple-element.80.refs_0_, bf16[8,2176]{1,0:T(8,128)(2,1)S(1)} %bitcast.77, bf16[8,2176]{1,0:T(8,128)(2,1)S(1)} %bitcast.76, ...), custom_call_target="tpu_custom_call" | custom-call | tf_op jit(solution)/shard_map/pallas_call | solution.py:379
  (56 shorter events, 3.0 us)
Async XLA Ops:
  0.6 15.5 %copy-start = (bf16[768,256]{1,0:T(8,128)(2,1)S(1)}, bf16[768,256]{1,0:T(8,128)(2,1)}, u32[]{:S(2)}) copy-start(bf16[768,256]{1,0:T(8,128)(2,1)} %tokens.4) | copy-start | bytes 1179652
  0.6 15.5 %copy-start.1 = (bf16[768,256]{1,0:T(8,128)(2,1)S(1)}, bf16[768,256]{1,0:T(8,128)(2,1)}, u32[]{:S(2)}) copy-start(bf16[768,256]{1,0:T(8,128)(2,1)} %cot) | copy-start | bytes 1179652
  0.7 15.5 %copy-start.6 = (s32[6]{0:T(128)S(1)}, s32[6]{0:T(128)}, u32[]{:S(2)}) copy-start(s32[6]{0:T(128)} %lengths.5) | copy-start | bytes 76
  2.3 10.1 %collective-permute-start.1 = (bf16[1,8,2304]{2,1,0:T(8,128)(2,1)}, bf16[1,8,2304]{2,1,0:T(8,128)(2,1)S(1)}, u32[]{:S(2)}, u32[]{:S(2)}) collective-permute-start(bf16[1,8,2304]{2,1,0:T(8,128)(2,1)} %bitcast.86), channel_id=1, source_target_pairs={{0,24},{1,25},{2,26},{3,27},{4,28},{5,29},{6,30},{7,31},{8,16},{9,... | collective-permute-start | bytes 110600 | tf_op jit(solution)/shard_map/ppermute | solution.py:315
  7.3 5.1 %collective-permute-start = (bf16[1,8,2304]{2,1,0:T(8,128)(2,1)}, bf16[1,8,2304]{2,1,0:T(8,128)(2,1)S(1)}, u32[]{:S(2)}, u32[]{:S(2)}) collective-permute-start(bf16[1,8,2304]{2,1,0:T(8,128)(2,1)} %bitcast.87), channel_id=1, source_target_pairs={{0,16},{1,17},{2,18},{3,19},{4,20},{5,21},{6,22},{7,23},{8,24},{9,... | collective-permute-start | bytes 110600 | tf_op jit(solution)/shard_map/ppermute | solution.py:315
  7.3 5.1 %collective-permute-start.2 = (bf16[1,8,2304]{2,1,0:T(8,128)(2,1)}, bf16[1,8,2304]{2,1,0:T(8,128)(2,1)S(1)}, u32[]{:S(2)}, u32[]{:S(2)}) collective-permute-start(bf16[1,8,2304]{2,1,0:T(8,128)(2,1)} %bitcast.88), channel_id=1, source_target_pairs={{0,8},{1,9},{2,10},{3,11},{4,12},{5,13},{6,14},{7,15},{8,0},{9,1},... | collective-permute-start | bytes 110600 | tf_op jit(solution)/shard_map/ppermute | solution.py:315
  12.5 8.5 %collective-permute-start.5 = (bf16[4,8,2304]{2,1,0:T(8,128)(2,1)S(1)}, bf16[4,8,2304]{2,1,0:T(8,128)(2,1)S(1)}, u32[]{:S(2)}, u32[]{:S(2)}) collective-permute-start(bf16[4,8,2304]{2,1,0:T(8,128)(2,1)S(1)} %constant_dynamic-update-slice_fusion), channel_id=1, source_target_pairs={{0,6},{1,7},{2,4},{3,5},{4,2},{5,3},{6,0},{7,1},{8,14},{9,15},{10,... | collective-permute-start | bytes 442376 | tf_op jit(solution)/shard_map/ppermute | solution.py:315
  15.0 6.0 %collective-permute-start.4 = (bf16[4,8,2304]{2,1,0:T(8,128)(2,1)S(1)}, bf16[4,8,2304]{2,1,0:T(8,128)(2,1)S(1)}, u32[]{:S(2)}, u32[]{:S(2)}) collective-permute-start(bf16[4,8,2304]{2,1,0:T(8,128)(2,1)S(1)} %constant_dynamic-update-slice_fusion), channel_id=1, source_target_pairs={{0,4},{1,5},{2,6},{3,7},{4,0},{5,1},{6,2},{7,3},{8,12},{9,13},{10,... | collective-permute-start | bytes 442376 | tf_op jit(solution)/shard_map/ppermute | solution.py:315
  15.5 5.4 %collective-permute-start.3 = (bf16[4,8,2304]{2,1,0:T(8,128)(2,1)S(1)}, bf16[4,8,2304]{2,1,0:T(8,128)(2,1)S(1)}, u32[]{:S(2)}, u32[]{:S(2)}) collective-permute-start(bf16[4,8,2304]{2,1,0:T(8,128)(2,1)S(1)} %constant_dynamic-update-slice_fusion), channel_id=1, source_target_pairs={{0,2},{1,3},{2,0},{3,1},{4,6},{5,7},{6,4},{7,5},{8,10},{9,11},{10,... | collective-permute-start | bytes 442376 | tf_op jit(solution)/shard_map/ppermute | solution.py:315
  21.0 1.6 %collective-permute-start.6 = (bf16[16,8,1152]{2,1,0:T(8,128)(2,1)S(1)}, bf16[16,8,1152]{2,1,0:T(8,128)(2,1)S(1)}, u32[]{:S(2)}, u32[]{:S(2)}) collective-permute-start(bf16[16,8,1152]{2,1,0:T(8,128)(2,1)S(1)} %get-tuple-element.73), channel_id=1, source_target_pairs={{0,1},{1,0},{2,3},{3,2},{4,5},{5,4},{6,7},{7,6},{8,9},{9,8},{10,11... | collective-permute-start | bytes 884744 | tf_op jit(solution)/shard_map/ppermute | solution.py:315
  21.2 1.8 %copy-start.2 = (f32[128,128]{1,0:T(8,128)S(1)}, f32[128,128]{1,0:T(8,128)}, u32[]{:S(2)}) copy-start(f32[128,128]{1,0:T(8,128)} %constant.80.clone.sin) | copy-start | bytes 196612
  22.7 2.6 %collective-permute-start.7 = (bf16[16,8,1152]{2,1,0:T(8,128)(2,1)S(1)}, bf16[16,8,1152]{2,1,0:T(8,128)(2,1)S(1)}, u32[]{:S(2)}, u32[]{:S(2)}) collective-permute-start(bf16[16,8,1152]{2,1,0:T(8,128)(2,1)S(1)} %get-tuple-element.48), channel_id=1, source_target_pairs={{0,1},{1,0},{2,3},{3,2},{4,5},{5,4},{6,7},{7,6},{8,9},{9,8},{10,11... | collective-permute-start | bytes 884744 | tf_op jit(solution)/shard_map/ppermute | solution.py:315
  30.2 1.6 %collective-permute-start.8 = (bf16[16,8,1024]{2,1,0:T(8,128)(2,1)S(1)}, bf16[16,8,1024]{2,1,0:T(8,128)(2,1)S(1)}, u32[]{:S(2)}, u32[]{:S(2)}) collective-permute-start(bf16[16,8,1024]{2,1,0:T(8,128)(2,1)S(1)} %dynamic-slice_bitcast_fusion.1), channel_id=1, source_target_pairs={{0,1},{1,0},{2,3},{3,2},{4,5},{5,4},{6,7},{7,6},{8,9},{9,8},{10,11... | collective-permute-start | bytes 786440 | tf_op jit(solution)/shard_map/ppermute | solution.py:315
  30.7 1.6 %collective-permute-start.9 = (bf16[16,8,1152]{2,1,0:T(8,128)(2,1)S(1)}, bf16[16,8,1152]{2,1,0:T(8,128)(2,1)S(1)}, u32[]{:S(2)}, u32[]{:S(2)}) collective-permute-start(bf16[16,8,1152]{2,1,0:T(8,128)(2,1)S(1)} %dynamic-slice_bitcast_fusion), channel_id=1, source_target_pairs={{0,1},{1,0},{2,3},{3,2},{4,5},{5,4},{6,7},{7,6},{8,9},{9,8},{10,11... | collective-permute-start | bytes 884744 | tf_op jit(solution)/shard_map/ppermute | solution.py:315
  32.5 7.5 %collective-permute-start.10 = (bf16[4,8,2176]{2,1,0:T(8,128)(2,1)S(1)}, bf16[4,8,2176]{2,1,0:T(8,128)(2,1)S(1)}, u32[]{:S(2)}, u32[]{:S(2)}) collective-permute-start(bf16[4,8,2176]{2,1,0:T(8,128)(2,1)S(1)} %get-tuple-element.74), channel_id=1, source_target_pairs={{0,6},{1,7},{2,4},{3,5},{4,2},{5,3},{6,0},{7,1},{8,14},{9,15},{10,... | collective-permute-start | bytes 417800 | tf_op jit(solution)/shard_map/ppermute | solution.py:315
  34.1 8.2 %collective-permute-start.12 = (bf16[4,8,2176]{2,1,0:T(8,128)(2,1)S(1)}, bf16[4,8,2176]{2,1,0:T(8,128)(2,1)S(1)}, u32[]{:S(2)}, u32[]{:S(2)}) collective-permute-start(bf16[4,8,2176]{2,1,0:T(8,128)(2,1)S(1)} %get-tuple-element.75), channel_id=1, source_target_pairs={{0,4},{1,5},{2,6},{3,7},{4,0},{5,1},{6,2},{7,3},{8,12},{9,13},{10,... | collective-permute-start | bytes 417800 | tf_op jit(solution)/shard_map/ppermute | solution.py:315
  35.5 6.8 %collective-permute-start.11 = (bf16[4,8,2176]{2,1,0:T(8,128)(2,1)S(1)}, bf16[4,8,2176]{2,1,0:T(8,128)(2,1)S(1)}, u32[]{:S(2)}, u32[]{:S(2)}) collective-permute-start(bf16[4,8,2176]{2,1,0:T(8,128)(2,1)S(1)} %get-tuple-element.76), channel_id=1, source_target_pairs={{0,2},{1,3},{2,0},{3,1},{4,6},{5,7},{6,4},{7,5},{8,10},{9,11},{10,... | collective-permute-start | bytes 417800 | tf_op jit(solution)/shard_map/ppermute | solution.py:315
  36.1 13.3 %copy-start.4 = (bf16[8,768]{1,0:T(8,128)(2,1)S(1)}, bf16[8,768]{1,0:T(8,128)(2,1)}, u32[]{:S(2)}) copy-start(bf16[8,768]{1,0:T(8,128)(2,1)} %refs_4_.1) | copy-start | bytes 36868
  36.1 13.3 %copy-start.5 = (bf16[8,768]{1,0:T(8,128)(2,1)S(1)}, bf16[8,768]{1,0:T(8,128)(2,1)}, u32[]{:S(2)}) copy-start(bf16[8,768]{1,0:T(8,128)(2,1)} %refs_5_.1) | copy-start | bytes 36868
  36.1 13.4 %copy-start.7 = (bf16[8]{0:T(256)(128)(2,1)S(1)}, bf16[8]{0:T(256)(128)(2,1)}, u32[]{:S(2)}) copy-start(bf16[8]{0:T(256)(128)(2,1)} %param.17) | copy-start | bytes 52
  36.1 13.4 %copy-start.8 = (bf16[8]{0:T(256)(128)(2,1)S(1)}, bf16[8]{0:T(256)(128)(2,1)}, u32[]{:S(2)}) copy-start(bf16[8]{0:T(256)(128)(2,1)} %param.18) | copy-start | bytes 52
  42.4 6.1 %collective-permute-start.15 = (bf16[1,8,2176]{2,1,0:T(8,128)(2,1)S(1)}, bf16[1,8,2176]{2,1,0:T(8,128)(2,1)S(1)}, u32[]{:S(2)}, u32[]{:S(2)}) collective-permute-start(bf16[1,8,2176]{2,1,0:T(8,128)(2,1)S(1)} %get-tuple-element.77), channel_id=1, source_target_pairs={{0,24},{1,25},{2,26},{3,27},{4,28},{5,29},{6,30},{7,31},{8,16},{9,... | collective-permute-start | bytes 104456 | tf_op jit(solution)/shard_map/ppermute | solution.py:315
  44.2 5.2 %collective-permute-start.14 = (bf16[1,8,2176]{2,1,0:T(8,128)(2,1)S(1)}, bf16[1,8,2176]{2,1,0:T(8,128)(2,1)S(1)}, u32[]{:S(2)}, u32[]{:S(2)}) collective-permute-start(bf16[1,8,2176]{2,1,0:T(8,128)(2,1)S(1)} %get-tuple-element.78), channel_id=1, source_target_pairs={{0,16},{1,17},{2,18},{3,19},{4,20},{5,21},{6,22},{7,23},{8,24},{9,... | collective-permute-start | bytes 104456 | tf_op jit(solution)/shard_map/ppermute | solution.py:315
  44.5 4.9 %collective-permute-start.13 = (bf16[1,8,2176]{2,1,0:T(8,128)(2,1)S(1)}, bf16[1,8,2176]{2,1,0:T(8,128)(2,1)S(1)}, u32[]{:S(2)}, u32[]{:S(2)}) collective-permute-start(bf16[1,8,2176]{2,1,0:T(8,128)(2,1)S(1)} %get-tuple-element.79), channel_id=1, source_target_pairs={{0,8},{1,9},{2,10},{3,11},{4,12},{5,13},{6,14},{7,15},{8,0},{9,1},... | collective-permute-start | bytes 104456 | tf_op jit(solution)/shard_map/ppermute | solution.py:315
  (1 other events, 1.8 us)

commit v7 on v6

--- a/solution.py
+++ b/solution.py
@@ -180,15 +180,15 @@
 
 def middle_kernel(
     tokens, out_low, first, second, gains, mixture, heads, shares, normed, cos, sin,
-    middle, hidden, d_middle, second_sums, first_sums, d_qkv, d_mixture, hat_two_low, d_att, d_merged,
+    middle, hidden, d_middle, sums, d_qkv, d_mixture, hat_two_low, d_att, d_merged,
 ):
     feed(
         tokens, out_low, first, second, gains, mixture,
         middle, hidden, d_middle, d_mixture, hat_two_low, d_att, d_merged,
     )
-    second_sums[:, : 2 * FF] = mm_tn(hat_two_low[...], d_merged[...]).astype(bf16)
-    second_sums[:, 2 * FF :] = mm_tn(out_low[...], hidden[...]).astype(bf16)
-    attend_back(heads, shares, d_mixture, normed, mixture, d_att, cos, sin, first_sums, d_qkv)
+    sums[:, SUMS : SUMS + 2 * FF] = mm_tn(hat_two_low[...], d_merged[...]).astype(bf16)
+    sums[:, SUMS + 2 * FF :] = mm_tn(out_low[...], hidden[...]).astype(bf16)
+    attend_back(heads, shares, d_mixture, normed, mixture, d_att, cos, sin, sums, d_qkv)
 
 
 def feed(
@@ -252,7 +252,19 @@
     sums[:, :D] = mm(total[:, :D], spread).astype(bf16)
     sums[:, D : 2 * D] = mm(total[:, D : 2 * D], spread).astype(bf16)
     sums[:, 2 * D : QKV] = total[:, 2 * D :]
-    sums[:, QKV:] = mm_tn(mixture[...], d_att[...]).astype(bf16)
+    sums[:, QKV:SUMS] = mm_tn(mixture[...], d_att[...]).astype(bf16)
+
+
+def layer_kernel(
+    lengths, hat, tokens, out_low, first, second, cos, sin,
+    gains, middle, hidden, d_middle, sums, d_qkv,
+    normed, heads, shares, mixture, d_mixture, hat_two_low, d_att, d_merged,
+):
+    attend_kernel(lengths, hat, first, cos, sin, gains, normed, heads, shares, mixture)
+    middle_kernel(
+        tokens, out_low, first, second, gains, mixture, heads, shares, normed, cos, sin,
+        middle, hidden, d_middle, sums, d_qkv, d_mixture, hat_two_low, d_att, d_merged,
+    )
 
 
 def outputs_kernel(lengths, tokens, first, second, gains, d_qkv, d_middle, middle, hidden, out, grad):
@@ -338,22 +350,16 @@
 
     first, second = room[:, :, :FIRST], room[:, :, FIRST:]
     got = trade(first, 1)
-    got, second = lax.optimization_barrier((got, second))
     first, second = both(first, got), both(second, trade(second, 1))
 
     cos, sin = tables()
     cos, sin = jnp.asarray(cos), jnp.asarray(sin)
-    gains, normed, heads, shares, mixture = call(
-        attend_kernel,
-        [SMALL] + [NEAR] * 4,
-        [((2, D), f32), ((count, D), bf16), ((count, QKV), bf16), ((count, WIDE), f32), ((count, D), bf16)],
-    )(lengths, hat, first, cos, sin)
-    middle, hidden, d_middle, second_sums, first_sums, d_qkv = call(
-        middle_kernel,
-        [NEAR] * 11,
-        [((count, D), f32), ((count, FF), bf16), ((count, D), f32), ((D, 3 * FF), bf16), ((D, SUMS), bf16), ((count, QKV), bf16)],
-        [((count, D), bf16), ((count, D), bf16), ((count, D), bf16), ((count, 2 * FF), bf16)],
-    )(tokens, out_low, first, second, gains, mixture, heads, shares, normed, cos, sin)
+    gains, middle, hidden, d_middle, sums, d_qkv = call(
+        layer_kernel,
+        [SMALL] + [NEAR] * 7,
+        [((2, D), f32), ((count, D), f32), ((count, FF), bf16), ((count, D), f32), ((D, SUMS + 3 * FF), bf16), ((count, QKV), bf16)],
+        [((count, D), bf16), ((count, QKV), bf16), ((count, WIDE), f32), ((count, D), bf16), ((count, D), bf16), ((count, D), bf16), ((count, D), bf16), ((count, 2 * FF), bf16)],
+    )(lengths, hat, tokens, out_low, first, second, cos, sin)
     out, grad = call(
         outputs_kernel, [SMALL] + [NEAR] * 8, [((count, D), bf16), ((count, D), f32)]
     )(lengths, tokens, first, second, gains, d_qkv, d_middle, middle, hidden)
@@ -363,7 +369,7 @@
         got = trade(cut(sums, core ^ 1, 2), 1)
         return (cut(sums, core, 2).astype(f32) + got.astype(f32)).astype(bf16)
 
-    kept = jnp.concatenate([halve(first_sums), halve(second_sums)], axis=2)
+    kept = halve(sums)
     for k, (place, _, partners) in enumerate(rounds[::-1]):
         ways = len(partners) + 1
         got = [trade(cut(kept, place ^ other, ways), mask) for mask, other in partners]

time: 50.3 us -> 49.9 us (level)
    pallas_call x2 -> x1, Pallas kernels: 7.14 us -> 6.86 us  [on_device(): call(layer_kernel, [SMALL] + [NEAR] * 7, [((2, D), f32), ((count, D), f32...]
    ppermute x16 -> x15, waiting for transfers between devices: 16.6 us -> 16.7 us  [trade(): return lax.ppermute(values, 'dp', [(i, i ^ mask) for i in range(n)])]
    ppermute x16 -> x15, starting transfers between devices: 18 us -> 17.9 us  [trade(): return lax.ppermute(values, 'dp', [(i, i ^ mask) for i in range(n)])]
    dynamic_update_slice x11 -> x12, local copies, waits for them, and re-layouts: 1.04 us -> 1.01 us  [put(): return lax.dynamic_update_slice(room, piece[:, None], (0, place, 0, column))]
  transfers between devices with their start and end apart: 16 -> 15, of which waited for: 10 -> 10; matrix products, arithmetic and copies ran while one was open for 2% -> 2% of each run, Pallas kernels for 11% -> 7%
where the time goes in v7:
time: 49.9 us; the launch traced here: 49.7 us
  starting transfers between devices  17.9 us (36%)
  waiting for transfers between devices  16.7 us (33%)
  Pallas kernels  12.6 us (25%)
  local copies, waits for them, and re-layouts  1.36 us (3%)
  between operations  0.9 us (2%)
    ppermute x15, starting transfers between devices, trade(): return lax.ppermute(values, 'dp', [(i, i ^ mask) for i in range(n)])  17.9 us
    ppermute x15, waiting for transfers between devices, trade(): return lax.ppermute(values, 'dp', [(i, i ^ mask) for i in range(n)])  16.7 us
    pallas_call x1, Pallas kernels, on_device(): call(layer_kernel, [SMALL] + [NEAR] * 7, [((2, D), f32), ((count, D), f32...  6.86 us
    pallas_call x1, Pallas kernels, on_device(): call(outputs_kernel, [SMALL] + [NEAR] * 8, [((count, D), bf16), ((count,...  2.46 us
    pallas_call x1, Pallas kernels, on_device(): pl.pallas_call(pack_kernel, out_specs=NEAR, out_shape=jax.ShapeDtypeStruc...  1.62 us
    dynamic_update_slice x12, local copies, waits for them, and re-layouts, put(): return lax.dynamic_update_slice(room, piece[:, None], (0, place, 0, column))  1.01 us
    pallas_call x1, Pallas kernels, on_device(): call(early_kernel, [SMALL] + [NEAR] * 2, [((count, D), f32), ((count, D),...  1 us
  transfers between devices with their start and end apart: 15, of which 10 were waited for; matrix products, arithmetic and copies ran while one was open for 2% of the time, Pallas kernels for 7%

profile of v7, /device:TPU:0, one launch (start us, length us, event | category | flops | bytes accessed | tf_op | source)
XLA Modules:
  0.0 49.7 jit_solution(14279405775363351290)
XLA Ops:
  0.7 1.6 %shard_map.170 = bf16[8,2304]{1,0:T(8,128)(2,1)} custom-call(bf16[8,768]{1,0:T(8,128)(2,1)} %refs_4_.1, bf16[8,256]{1,0:T(8,128)(2,1)} %w_attn.1, bf16[8,768]{1,0:T(8,128)(2,1)} %refs_5_.1, bf16[8,384]{1,0:T(8,128)(2,1)} %bitcast.79, bf16[1,8]{1,0:T(2,128)(2,1)} %bitcast.67, bf16[1,8]{1,0:T(2,128)(2,1)} %bitcast.69), custom_call_target="tpu_custom_call" | custom-call | tf_op jit(solution)/shard_map/pallas_call | solution.py:329
  2.3 5.0 %collective-permute-start.1 = (bf16[1,8,2304]{2,1,0:T(8,128)(2,1)}, bf16[1,8,2304]{2,1,0:T(8,128)(2,1)S(1)}, u32[]{:S(2)}, u32[]{:S(2)}) collective-permute-start(bf16[1,8,2304]{2,1,0:T(8,128)(2,1)} %bitcast.76), channel_id=1, source_target_pairs={{0,24},{1,25},{2,26},{3,27},{4,28},{5,29},{6,30},{7,31},{8,16},{9,... | collective-permute-start | bytes 110600 | tf_op jit(solution)/shard_map/ppermute | solution.py:327
  7.3 0.6 %collective-permute-start.2 = (bf16[1,8,2304]{2,1,0:T(8,128)(2,1)}, bf16[1,8,2304]{2,1,0:T(8,128)(2,1)S(1)}, u32[]{:S(2)}, u32[]{:S(2)}) collective-permute-start(bf16[1,8,2304]{2,1,0:T(8,128)(2,1)} %bitcast.78), channel_id=1, source_target_pairs={{0,8},{1,9},{2,10},{3,11},{4,12},{5,13},{6,14},{7,15},{8,0},{9,1},... | collective-permute-start | bytes 110600 | tf_op jit(solution)/shard_map/ppermute | solution.py:327
  7.9 0.8 %constant_dynamic-update-slice_fusion.3 = bf16[4,8,2304]{2,1,0:T(8,128)(2,1)S(1)} fusion(bf16[4,8,2304]{2,1,0:T(8,128)(2,1)S(1)} %reshape.77, s32[]{:T(128)S(6)} %select_n.54, bf16[8,2304]{1,0:T(8,128)(2,1)} %shard_map.170), kind=kLoop, calls=%fused_computation.25 | loop fusion | bytes 73732 | tf_op jit(solution)/shard_map/dynamic_update_slice | solution.py:297
  8.7 3.7 %collective-permute-done = bf16[1,8,2304]{2,1,0:T(8,128)(2,1)S(1)} collective-permute-done((bf16[1,8,2304]{2,1,0:T(8,128)(2,1)}, bf16[1,8,2304]{2,1,0:T(8,128)(2,1)S(1)}, u32[]{:S(2)}, u32[]{:S(2)}) %collective-permute-start) | collective-permute-done | bytes 36896 | tf_op jit(solution)/shard_map/ppermute | solution.py:327
  12.5 2.5 %collective-permute-start.5 = (bf16[4,8,2304]{2,1,0:T(8,128)(2,1)S(1)}, bf16[4,8,2304]{2,1,0:T(8,128)(2,1)S(1)}, u32[]{:S(2)}, u32[]{:S(2)}) collective-permute-start(bf16[4,8,2304]{2,1,0:T(8,128)(2,1)S(1)} %constant_dynamic-update-slice_fusion), channel_id=1, source_target_pairs={{0,6},{1,7},{2,4},{3,5},{4,2},{5,3},{6,0},{7,1},{8,14},{9,15},{10,... | collective-permute-start | bytes 442376 | tf_op jit(solution)/shard_map/ppermute | solution.py:327
  15.0 0.5 %collective-permute-start.4 = (bf16[4,8,2304]{2,1,0:T(8,128)(2,1)S(1)}, bf16[4,8,2304]{2,1,0:T(8,128)(2,1)S(1)}, u32[]{:S(2)}, u32[]{:S(2)}) collective-permute-start(bf16[4,8,2304]{2,1,0:T(8,128)(2,1)S(1)} %constant_dynamic-update-slice_fusion), channel_id=1, source_target_pairs={{0,4},{1,5},{2,6},{3,7},{4,0},{5,1},{6,2},{7,3},{8,12},{9,13},{10,... | collective-permute-start | bytes 442376 | tf_op jit(solution)/shard_map/ppermute | solution.py:327
  15.5 0.5 %collective-permute-start.3 = (bf16[4,8,2304]{2,1,0:T(8,128)(2,1)S(1)}, bf16[4,8,2304]{2,1,0:T(8,128)(2,1)S(1)}, u32[]{:S(2)}, u32[]{:S(2)}) collective-permute-start(bf16[4,8,2304]{2,1,0:T(8,128)(2,1)S(1)} %constant_dynamic-update-slice_fusion), channel_id=1, source_target_pairs={{0,2},{1,3},{2,0},{3,1},{4,6},{5,7},{6,4},{7,5},{8,10},{9,11},{10,... | collective-permute-start | bytes 442376 | tf_op jit(solution)/shard_map/ppermute | solution.py:327
  16.1 1.0 %shard_map.171 = (f32[768,256]{1,0:T(8,128)S(1)}, bf16[768,256]{1,0:T(8,128)(2,1)S(1)}) custom-call(s32[6]{0:T(128)S(1)} %copy-done.6, bf16[768,256]{1,0:T(8,128)(2,1)S(1)} %copy-done, bf16[768,256]{1,0:T(8,128)(2,1)S(1)} %copy-done.1), custom_call_target="tpu_custom_call" | custom-call | tf_op jit(solution)/shard_map/pallas_call | solution.py:342
  17.1 3.7 %collective-permute-done.3 = bf16[4,8,2304]{2,1,0:T(8,128)(2,1)S(1)} collective-permute-done((bf16[4,8,2304]{2,1,0:T(8,128)(2,1)S(1)}, bf16[4,8,2304]{2,1,0:T(8,128)(2,1)S(1)}, u32[]{:S(2)}, u32[]{:S(2)}) %collective-permute-start.3) | collective-permute-done | bytes 147488 | tf_op jit(solution)/shard_map/ppermute | solution.py:327
  21.8 0.9 %collective-permute-done.7 = bf16[16,8,1152]{2,1,0:T(8,128)(2,1)S(1)} collective-permute-done((bf16[16,8,1152]{2,1,0:T(8,128)(2,1)S(1)}, bf16[16,8,1152]{2,1,0:T(8,128)(2,1)S(1)}, u32[]{:S(2)}, u32[]{:S(2)}) %collective-permute-start.7) | collective-permute-done | bytes 294944 | tf_op jit(solution)/shard_map/ppermute | solution.py:327
  23.2 6.9 %shard_map.172 = (f32[2,256]{1,0:T(2,128)S(1)}, f32[768,256]{1,0:T(8,128)S(1)}, bf16[768,384]{1,0:T(8,128)(2,1)S(1)}, f32[768,256]{1,0:T(8,128)S(1)}, bf16[256,2...) custom-call(s32[6]{0:T(128)S(1)} %copy-done.6, f32[768,256]{1,0:T(8,128)S(1)} %get-tuple-element.38.hat, ...), custom_call_target="tpu_custom_call" | custom-call | tf_op jit(solution)/shard_map/pallas_call | solution.py:357
  30.3 1.8 %collective-permute-done.8 = bf16[16,8,2176]{2,1,0:T(8,128)(2,1)S(1)} collective-permute-done((bf16[16,8,2176]{2,1,0:T(8,128)(2,1)S(1)}, bf16[16,8,2176]{2,1,0:T(8,128)(2,1)S(1)}, u32[]{:S(2)}, u32[]{:S(2)}) %collective-permute-start.8) | collective-permute-done | bytes 557088 | tf_op jit(solution)/shard_map/ppermute | solution.py:327
  32.3 1.6 %collective-permute-start.9 = (bf16[4,8,2176]{2,1,0:T(8,128)(2,1)S(1)}, bf16[4,8,2176]{2,1,0:T(8,128)(2,1)S(1)}, u32[]{:S(2)}, u32[]{:S(2)}) collective-permute-start(bf16[4,8,2176]{2,1,0:T(8,128)(2,1)S(1)} %get-tuple-element.60), channel_id=1, source_target_pairs={{0,6},{1,7},{2,4},{3,5},{4,2},{5,3},{6,0},{7,1},{8,14},{9,15},{10,... | collective-permute-start | bytes 417800 | tf_op jit(solution)/shard_map/ppermute | solution.py:327
  33.9 1.4 %collective-permute-start.11 = (bf16[4,8,2176]{2,1,0:T(8,128)(2,1)S(1)}, bf16[4,8,2176]{2,1,0:T(8,128)(2,1)S(1)}, u32[]{:S(2)}, u32[]{:S(2)}) collective-permute-start(bf16[4,8,2176]{2,1,0:T(8,128)(2,1)S(1)} %get-tuple-element.61), channel_id=1, source_target_pairs={{0,4},{1,5},{2,6},{3,7},{4,0},{5,1},{6,2},{7,3},{8,12},{9,13},{10,... | collective-permute-start | bytes 417800 | tf_op jit(solution)/shard_map/ppermute | solution.py:327
  35.3 0.5 %collective-permute-start.10 = (bf16[4,8,2176]{2,1,0:T(8,128)(2,1)S(1)}, bf16[4,8,2176]{2,1,0:T(8,128)(2,1)S(1)}, u32[]{:S(2)}, u32[]{:S(2)}) collective-permute-start(bf16[4,8,2176]{2,1,0:T(8,128)(2,1)S(1)} %get-tuple-element.62), channel_id=1, source_target_pairs={{0,2},{1,3},{2,0},{3,1},{4,6},{5,7},{6,4},{7,5},{8,10},{9,11},{10,... | collective-permute-start | bytes 417800 | tf_op jit(solution)/shard_map/ppermute | solution.py:327
  35.9 2.5 %shard_map.173 = (bf16[768,256]{1,0:T(8,128)(2,1)}, f32[768,256]{1,0:T(8,128)}) custom-call(s32[6]{0:T(128)S(1)} %copy-done.6, bf16[768,256]{1,0:T(8,128)(2,1)S(1)} %copy-done, bf16[256,1152]{1,0:T(8,128)(2,1)S(1)} %bitcast.59, bf16[256,1152]{1,0:T(8,128)(2,1)S(1)} %bitcast.61, f32[2,256]{1,0:T(2,128)S(1)} %get-tuple-element.42.gains, ...), custom_call_target="tpu_custom_call" | custom-call | tf_op jit(solution)/shard_map/pallas_call | solution.py:363
  38.3 1.5 %collective-permute-done.9 = bf16[4,8,2176]{2,1,0:T(8,128)(2,1)S(1)} collective-permute-done((bf16[4,8,2176]{2,1,0:T(8,128)(2,1)S(1)}, bf16[4,8,2176]{2,1,0:T(8,128)(2,1)S(1)}, u32[]{:S(2)}, u32[]{:S(2)}) %collective-permute-start.9) | collective-permute-done | bytes 139296 | tf_op jit(solution)/shard_map/ppermute | solution.py:327
  39.8 2.2 %collective-permute-done.11 = bf16[4,8,2176]{2,1,0:T(8,128)(2,1)S(1)} collective-permute-done((bf16[4,8,2176]{2,1,0:T(8,128)(2,1)S(1)}, bf16[4,8,2176]{2,1,0:T(8,128)(2,1)S(1)}, u32[]{:S(2)}, u32[]{:S(2)}) %collective-permute-start.11) | collective-permute-done | bytes 139296 | tf_op jit(solution)/shard_map/ppermute | solution.py:327
  42.1 1.8 %collective-permute-start.14 = (bf16[1,8,2176]{2,1,0:T(8,128)(2,1)S(1)}, bf16[1,8,2176]{2,1,0:T(8,128)(2,1)S(1)}, u32[]{:S(2)}, u32[]{:S(2)}) collective-permute-start(bf16[1,8,2176]{2,1,0:T(8,128)(2,1)S(1)} %get-tuple-element.63), channel_id=1, source_target_pairs={{0,24},{1,25},{2,26},{3,27},{4,28},{5,29},{6,30},{7,31},{8,16},{9,... | collective-permute-start | bytes 104456 | tf_op jit(solution)/shard_map/ppermute | solution.py:327
  44.1 2.4 %collective-permute-start.12 = (bf16[1,8,2176]{2,1,0:T(8,128)(2,1)S(1)}, bf16[1,8,2176]{2,1,0:T(8,128)(2,1)S(1)}, u32[]{:S(2)}, u32[]{:S(2)}) collective-permute-start(bf16[1,8,2176]{2,1,0:T(8,128)(2,1)S(1)} %get-tuple-element.65), channel_id=1, source_target_pairs={{0,8},{1,9},{2,10},{3,11},{4,12},{5,13},{6,14},{7,15},{8,0},{9,1},... | collective-permute-start | bytes 104456 | tf_op jit(solution)/shard_map/ppermute | solution.py:327
  46.5 1.6 %collective-permute-done.14 = bf16[1,8,2176]{2,1,0:T(8,128)(2,1)S(1)} collective-permute-done((bf16[1,8,2176]{2,1,0:T(8,128)(2,1)S(1)}, bf16[1,8,2176]{2,1,0:T(8,128)(2,1)S(1)}, u32[]{:S(2)}, u32[]{:S(2)}) %collective-permute-start.14) | collective-permute-done | bytes 34848 | tf_op jit(solution)/shard_map/ppermute | solution.py:327
  48.1 0.9 %collective-permute-done.13 = bf16[1,8,2176]{2,1,0:T(8,128)(2,1)S(1)} collective-permute-done((bf16[1,8,2176]{2,1,0:T(8,128)(2,1)S(1)}, bf16[1,8,2176]{2,1,0:T(8,128)(2,1)S(1)}, u32[]{:S(2)}, u32[]{:S(2)}) %collective-permute-start.13) | collective-permute-done | bytes 34848 | tf_op jit(solution)/shard_map/ppermute | solution.py:327
  49.1 0.6 %shard_map.174 = (f32[8,768]{1,0:T(8,128)}, f32[8,256]{1,0:T(8,128)}, f32[8,768]{1,0:T(8,128)}, f32[8,384]{1,0:T(8,128)}, f32[1,8]{1,0:T(1,128)}, /*index=5*/f32[1,8]{1,0:T(1,128)}) custom-call(bf16[8,2176]{1,0:T(8,128)(2,1)S(1)} %get-tuple-element.66.refs_0_, bf16[8,2176]{1,0:T(8,128)(2,1)S(1)} %bitcast.66, bf16[8,2176]{1,0:T(8,128)(2,1)S(1)} %bitcast.65, ...), custom_call_target="tpu_custom_call" | custom-call | tf_op jit(solution)/shard_map/pallas_call | solution.py:385
  (51 shorter events, 2.3 us)
Async XLA Ops:
  0.6 15.5 %copy-start = (bf16[768,256]{1,0:T(8,128)(2,1)S(1)}, bf16[768,256]{1,0:T(8,128)(2,1)}, u32[]{:S(2)}) copy-start(bf16[768,256]{1,0:T(8,128)(2,1)} %tokens.4) | copy-start | bytes 1179652
  0.6 15.5 %copy-start.1 = (bf16[768,256]{1,0:T(8,128)(2,1)S(1)}, bf16[768,256]{1,0:T(8,128)(2,1)}, u32[]{:S(2)}) copy-start(bf16[768,256]{1,0:T(8,128)(2,1)} %cot) | copy-start | bytes 1179652
  0.7 15.5 %copy-start.6 = (s32[6]{0:T(128)S(1)}, s32[6]{0:T(128)}, u32[]{:S(2)}) copy-start(s32[6]{0:T(128)} %lengths.5) | copy-start | bytes 76
  2.3 10.1 %collective-permute-start.1 = (bf16[1,8,2304]{2,1,0:T(8,128)(2,1)}, bf16[1,8,2304]{2,1,0:T(8,128)(2,1)S(1)}, u32[]{:S(2)}, u32[]{:S(2)}) collective-permute-start(bf16[1,8,2304]{2,1,0:T(8,128)(2,1)} %bitcast.76), channel_id=1, source_target_pairs={{0,24},{1,25},{2,26},{3,27},{4,28},{5,29},{6,30},{7,31},{8,16},{9,... | collective-permute-start | bytes 110600 | tf_op jit(solution)/shard_map/ppermute | solution.py:327
  7.3 5.1 %collective-permute-start = (bf16[1,8,2304]{2,1,0:T(8,128)(2,1)}, bf16[1,8,2304]{2,1,0:T(8,128)(2,1)S(1)}, u32[]{:S(2)}, u32[]{:S(2)}) collective-permute-start(bf16[1,8,2304]{2,1,0:T(8,128)(2,1)} %bitcast.77), channel_id=1, source_target_pairs={{0,16},{1,17},{2,18},{3,19},{4,20},{5,21},{6,22},{7,23},{8,24},{9,... | collective-permute-start | bytes 110600 | tf_op jit(solution)/shard_map/ppermute | solution.py:327
  7.3 5.1 %collective-permute-start.2 = (bf16[1,8,2304]{2,1,0:T(8,128)(2,1)}, bf16[1,8,2304]{2,1,0:T(8,128)(2,1)S(1)}, u32[]{:S(2)}, u32[]{:S(2)}) collective-permute-start(bf16[1,8,2304]{2,1,0:T(8,128)(2,1)} %bitcast.78), channel_id=1, source_target_pairs={{0,8},{1,9},{2,10},{3,11},{4,12},{5,13},{6,14},{7,15},{8,0},{9,1},... | collective-permute-start | bytes 110600 | tf_op jit(solution)/shard_map/ppermute | solution.py:327
  12.5 8.5 %collective-permute-start.5 = (bf16[4,8,2304]{2,1,0:T(8,128)(2,1)S(1)}, bf16[4,8,2304]{2,1,0:T(8,128)(2,1)S(1)}, u32[]{:S(2)}, u32[]{:S(2)}) collective-permute-start(bf16[4,8,2304]{2,1,0:T(8,128)(2,1)S(1)} %constant_dynamic-update-slice_fusion), channel_id=1, source_target_pairs={{0,6},{1,7},{2,4},{3,5},{4,2},{5,3},{6,0},{7,1},{8,14},{9,15},{10,... | collective-permute-start | bytes 442376 | tf_op jit(solution)/shard_map/ppermute | solution.py:327
  15.0 6.0 %collective-permute-start.4 = (bf16[4,8,2304]{2,1,0:T(8,128)(2,1)S(1)}, bf16[4,8,2304]{2,1,0:T(8,128)(2,1)S(1)}, u32[]{:S(2)}, u32[]{:S(2)}) collective-permute-start(bf16[4,8,2304]{2,1,0:T(8,128)(2,1)S(1)} %constant_dynamic-update-slice_fusion), channel_id=1, source_target_pairs={{0,4},{1,5},{2,6},{3,7},{4,0},{5,1},{6,2},{7,3},{8,12},{9,13},{10,... | collective-permute-start | bytes 442376 | tf_op jit(solution)/shard_map/ppermute | solution.py:327
  15.5 5.4 %collective-permute-start.3 = (bf16[4,8,2304]{2,1,0:T(8,128)(2,1)S(1)}, bf16[4,8,2304]{2,1,0:T(8,128)(2,1)S(1)}, u32[]{:S(2)}, u32[]{:S(2)}) collective-permute-start(bf16[4,8,2304]{2,1,0:T(8,128)(2,1)S(1)} %constant_dynamic-update-slice_fusion), channel_id=1, source_target_pairs={{0,2},{1,3},{2,0},{3,1},{4,6},{5,7},{6,4},{7,5},{8,10},{9,11},{10,... | collective-permute-start | bytes 442376 | tf_op jit(solution)/shard_map/ppermute | solution.py:327
  21.0 1.6 %collective-permute-start.7 = (bf16[16,8,1152]{2,1,0:T(8,128)(2,1)S(1)}, bf16[16,8,1152]{2,1,0:T(8,128)(2,1)S(1)}, u32[]{:S(2)}, u32[]{:S(2)}) collective-permute-start(bf16[16,8,1152]{2,1,0:T(8,128)(2,1)S(1)} %get-tuple-element.58), channel_id=1, source_target_pairs={{0,1},{1,0},{2,3},{3,2},{4,5},{5,4},{6,7},{7,6},{8,9},{9,8},{10,11... | collective-permute-start | bytes 884744 | tf_op jit(solution)/shard_map/ppermute | solution.py:327
  21.1 2.0 %collective-permute-start.6 = (bf16[16,8,1152]{2,1,0:T(8,128)(2,1)S(1)}, bf16[16,8,1152]{2,1,0:T(8,128)(2,1)S(1)}, u32[]{:S(2)}, u32[]{:S(2)}) collective-permute-start(bf16[16,8,1152]{2,1,0:T(8,128)(2,1)S(1)} %get-tuple-element.59), channel_id=1, source_target_pairs={{0,1},{1,0},{2,3},{3,2},{4,5},{5,4},{6,7},{7,6},{8,9},{9,8},{10,11... | collective-permute-start | bytes 884744 | tf_op jit(solution)/shard_map/ppermute | solution.py:327
  21.7 1.4 %copy-start.2 = (f32[128,128]{1,0:T(8,128)S(1)}, f32[128,128]{1,0:T(8,128)}, u32[]{:S(2)}) copy-start(f32[128,128]{1,0:T(8,128)} %constant.74.clone.sin) | copy-start | bytes 196612
  21.7 1.4 %copy-start.3 = (f32[128,128]{1,0:T(8,128)S(1)}, f32[128,128]{1,0:T(8,128)}, u32[]{:S(2)}) copy-start(f32[128,128]{1,0:T(8,128)} %constant.73.clone.cos) | copy-start | bytes 196612
  30.1 2.0 %collective-permute-start.8 = (bf16[16,8,2176]{2,1,0:T(8,128)(2,1)S(1)}, bf16[16,8,2176]{2,1,0:T(8,128)(2,1)S(1)}, u32[]{:S(2)}, u32[]{:S(2)}) collective-permute-start(bf16[16,8,2176]{2,1,0:T(8,128)(2,1)S(1)} %dynamic-slice_bitcast_fusion), channel_id=1, source_target_pairs={{0,1},{1,0},{2,3},{3,2},{4,5},{5,4},{6,7},{7,6},{8,9},{9,8},{10,11... | collective-permute-start | bytes 1671176 | tf_op jit(solution)/shard_map/ppermute | solution.py:327
  32.3 7.5 %collective-permute-start.9 = (bf16[4,8,2176]{2,1,0:T(8,128)(2,1)S(1)}, bf16[4,8,2176]{2,1,0:T(8,128)(2,1)S(1)}, u32[]{:S(2)}, u32[]{:S(2)}) collective-permute-start(bf16[4,8,2176]{2,1,0:T(8,128)(2,1)S(1)} %get-tuple-element.60), channel_id=1, source_target_pairs={{0,6},{1,7},{2,4},{3,5},{4,2},{5,3},{6,0},{7,1},{8,14},{9,15},{10,... | collective-permute-start | bytes 417800 | tf_op jit(solution)/shard_map/ppermute | solution.py:327
  33.9 8.0 %collective-permute-start.11 = (bf16[4,8,2176]{2,1,0:T(8,128)(2,1)S(1)}, bf16[4,8,2176]{2,1,0:T(8,128)(2,1)S(1)}, u32[]{:S(2)}, u32[]{:S(2)}) collective-permute-start(bf16[4,8,2176]{2,1,0:T(8,128)(2,1)S(1)} %get-tuple-element.61), channel_id=1, source_target_pairs={{0,4},{1,5},{2,6},{3,7},{4,0},{5,1},{6,2},{7,3},{8,12},{9,13},{10,... | collective-permute-start | bytes 417800 | tf_op jit(solution)/shard_map/ppermute | solution.py:327
  35.3 6.7 %collective-permute-start.10 = (bf16[4,8,2176]{2,1,0:T(8,128)(2,1)S(1)}, bf16[4,8,2176]{2,1,0:T(8,128)(2,1)S(1)}, u32[]{:S(2)}, u32[]{:S(2)}) collective-permute-start(bf16[4,8,2176]{2,1,0:T(8,128)(2,1)S(1)} %get-tuple-element.62), channel_id=1, source_target_pairs={{0,2},{1,3},{2,0},{3,1},{4,6},{5,7},{6,4},{7,5},{8,10},{9,11},{10,... | collective-permute-start | bytes 417800 | tf_op jit(solution)/shard_map/ppermute | solution.py:327
  35.8 13.2 %copy-start.4 = (bf16[8,768]{1,0:T(8,128)(2,1)S(1)}, bf16[8,768]{1,0:T(8,128)(2,1)}, u32[]{:S(2)}) copy-start(bf16[8,768]{1,0:T(8,128)(2,1)} %refs_4_.1) | copy-start | bytes 36868
  35.8 13.2 %copy-start.5 = (bf16[8,768]{1,0:T(8,128)(2,1)S(1)}, bf16[8,768]{1,0:T(8,128)(2,1)}, u32[]{:S(2)}) copy-start(bf16[8,768]{1,0:T(8,128)(2,1)} %refs_5_.1) | copy-start | bytes 36868
  35.8 13.2 %copy-start.7 = (bf16[8]{0:T(256)(128)(2,1)S(1)}, bf16[8]{0:T(256)(128)(2,1)}, u32[]{:S(2)}) copy-start(bf16[8]{0:T(256)(128)(2,1)} %param.17) | copy-start | bytes 52
  35.9 13.2 %copy-start.8 = (bf16[8]{0:T(256)(128)(2,1)S(1)}, bf16[8]{0:T(256)(128)(2,1)}, u32[]{:S(2)}) copy-start(bf16[8]{0:T(256)(128)(2,1)} %param.18) | copy-start | bytes 52
  42.1 6.1 %collective-permute-start.14 = (bf16[1,8,2176]{2,1,0:T(8,128)(2,1)S(1)}, bf16[1,8,2176]{2,1,0:T(8,128)(2,1)S(1)}, u32[]{:S(2)}, u32[]{:S(2)}) collective-permute-start(bf16[1,8,2176]{2,1,0:T(8,128)(2,1)S(1)} %get-tuple-element.63), channel_id=1, source_target_pairs={{0,24},{1,25},{2,26},{3,27},{4,28},{5,29},{6,30},{7,31},{8,16},{9,... | collective-permute-start | bytes 104456 | tf_op jit(solution)/shard_map/ppermute | solution.py:327
  43.8 5.2 %collective-permute-start.13 = (bf16[1,8,2176]{2,1,0:T(8,128)(2,1)S(1)}, bf16[1,8,2176]{2,1,0:T(8,128)(2,1)S(1)}, u32[]{:S(2)}, u32[]{:S(2)}) collective-permute-start(bf16[1,8,2176]{2,1,0:T(8,128)(2,1)S(1)} %get-tuple-element.64), channel_id=1, source_target_pairs={{0,16},{1,17},{2,18},{3,19},{4,20},{5,21},{6,22},{7,23},{8,24},{9,... | collective-permute-start | bytes 104456 | tf_op jit(solution)/shard_map/ppermute | solution.py:327
  44.1 4.9 %collective-permute-start.12 = (bf16[1,8,2176]{2,1,0:T(8,128)(2,1)S(1)}, bf16[1,8,2176]{2,1,0:T(8,128)(2,1)S(1)}, u32[]{:S(2)}, u32[]{:S(2)}) collective-permute-start(bf16[1,8,2176]{2,1,0:T(8,128)(2,1)S(1)} %get-tuple-element.65), channel_id=1, source_target_pairs={{0,8},{1,9},{2,10},{3,11},{4,12},{5,13},{6,14},{7,15},{8,0},{9,1},... | collective-permute-start | bytes 104456 | tf_op jit(solution)/shard_map/ppermute | solution.py:327
